TPU v7x, 1024 devices: a whole 4x8x16 slice. The times are simulated.
1024 devices in a mesh: gx: 16 (over z_lo, x), gy: 8 (over y), gz: 8 (over z_hi, core).
Axes of the slice: x: 4, y: 8, z: 16 (z_hi: 4, z_lo: 4; z = z_hi * 4 + z_lo), core: 2. Of those that a mesh axis runs over, the one named last changes fastest.
Arguments:
- conserved: float32 [32, 32, 64, 5, 512], P('gx', 'gy', 'gz'), may hold values from -1 to 6, as said below
- troubled: int32 [32, 32, 64], P('gx', 'gy', 'gz'), may hold values from 0 to 1, as said below
- blend_level: int32 [32, 32, 64], P('gx', 'gy', 'gz'), may hold values from 1 to 4
Outputs:
- residual: float32 [32, 32, 64, 5, 512], P('gx', 'gy', 'gz')
Inputs may be any that keep to these rules, and one draw needn't show every extreme that they name: `conserved`: at every node density and pressure lie within 0.5 to 2 and each velocity component within -0.5 to 0.5. `troubled`: flagged elements cluster along a shock plane. In every row of devices along gx exactly one device flags 4 times the number of devices along gx, and every other device flags exactly 4.
All inputs are finite; a program needn't handle non-finite values.
Results may differ from a plain program's by a relative error of at most 0.0001.
Values sent between devices are 32-bit elements; how exact they have to be, the bound alone decides.
No kernel may reach another device: no remote copies, remote signals or barrier semaphores. Data moves between devices by JAX's collectives and lax.ppermute only.
A program may use at most 32 MiB of HBM per device.

v0:
```python
import jax
import jax.numpy as jnp
import numpy as np
from jax import lax
from jax.sharding import PartitionSpec as P

SLOT = 4


PRECISE = lax.Precision.HIGHEST
HEAT_RATIO = 1.4
GRID_SCALE = 0.05
LOBATTO_POINTS = [
    -1.0,
    -0.8717401485096066,
    -0.5917001814331423,
    -0.2092992179024789,
    0.2092992179024789,
    0.5917001814331423,
    0.8717401485096066,
    1.0,
]
LOBATTO_WEIGHTS = [
    0.03571428571428571,
    0.21070422714350603,
    0.34112269248350435,
    0.4124587946587039,
    0.4124587946587039,
    0.34112269248350435,
    0.21070422714350603,
    0.03571428571428571,
]


def padded_2(array, sides, width):
    for axis, dim in sides:
        size, length = (lax.axis_size(axis), array.shape[dim])
        up = [(i, (i + 1) % size) for i in range(size)]
        down = [(j, i) for i, j in up]
        last = lax.slice_in_dim(array, length - width, length, axis=dim)
        leading = lax.slice_in_dim(array, 0, width, axis=dim)
        before = lax.ppermute(last, axis, up)
        after = lax.ppermute(leading, axis, down)
        array = jnp.concatenate([before, array, after], axis=dim)
    return array


def node_tables():
    points = np.array(LOBATTO_POINTS)
    weights = np.array(LOBATTO_WEIGHTS)
    barycentric = np.array(
        [
            1.0
            / np.prod(
                [
                    points[row_index] - points[other_index]
                    for other_index in range(8)
                    if other_index != row_index
                ]
            )
            for row_index in range(8)
        ]
    )
    derivative = np.zeros((8, 8))
    for row_index in range(8):
        for column in range(8):
            if row_index != column:
                derivative[row_index, column] = (
                    barycentric[column]
                    / barycentric[row_index]
                    / (points[row_index] - points[column])
                )
        derivative[row_index, row_index] = -np.sum(derivative[row_index])
    identity = np.eye(8)
    kron_list = [
        np.kron(np.kron(derivative, identity), identity),
        np.kron(np.kron(identity, derivative), identity),
        np.kron(np.kron(identity, identity), derivative),
    ]
    stacked = np.concatenate([matrix.T for matrix in kron_list], axis=0)
    numbers = np.arange(512).reshape(8, 8, 8)
    face_nodes = [
        numbers[0],
        numbers[7],
        numbers[:, 0],
        numbers[:, 7],
        numbers[:, :, 0],
        numbers[:, :, 7],
    ]
    extract = np.zeros((512, 384))
    for face_index, node_list in enumerate(face_nodes):
        extract[node_list.ravel(), face_index * 64 + np.arange(64)] = 1.0
    lifting = extract.T / weights[0]
    node_grid = np.stack(
        np.meshgrid(np.arange(8), np.arange(8), np.arange(8), indexing="ij")
    ).reshape(3, 512)
    inverse = 1.0 / weights[node_grid]
    return (
        jnp.asarray(stacked, jnp.float32),
        jnp.asarray(extract, jnp.float32),
        jnp.asarray(lifting, jnp.float32),
        jnp.asarray(inverse, jnp.float32),
        node_grid,
    )


def face_part(face_data, face_index):
    return face_data[..., face_index * 64 : (face_index + 1) * 64]


def euler_flux(values_in, axis_index):
    density = values_in[..., 0, :]
    momenta = [values_in[..., 1, :], values_in[..., 2, :], values_in[..., 3, :]]
    energy = values_in[..., 4, :]
    normal = momenta[axis_index] / density
    kinetic = (
        0.5
        * (momenta[0] * momenta[0] + momenta[1] * momenta[1] + momenta[2] * momenta[2])
        / density
    )
    pressure = (HEAT_RATIO - 1.0) * (energy - kinetic)
    sound_speed = jnp.sqrt(HEAT_RATIO * pressure / density)
    components = [
        momenta[axis_index],
        momenta[0] * normal,
        momenta[1] * normal,
        momenta[2] * normal,
        (energy + pressure) * normal,
    ]
    components[1 + axis_index] = components[1 + axis_index] + pressure
    return (jnp.stack(components, axis=-2), jnp.abs(normal) + sound_speed)


def rusanov(left_state, right_state, axis_index):
    left_flux, left_speed = euler_flux(left_state, axis_index)
    right_flux, right_speed = euler_flux(right_state, axis_index)
    largest = jnp.maximum(left_speed, right_speed)[..., None, :]
    return 0.5 * (left_flux + right_flux) - 0.5 * largest * (right_state - left_state)


def star_fluxes(face_data, below_faces, above_faces):
    columns = []
    for axis_index in range(3):
        columns.append(
            rusanov(below_faces[axis_index], face_part(face_data, 2 * axis_index), axis_index)
        )
        columns.append(
            rusanov(face_part(face_data, 2 * axis_index + 1), above_faces[axis_index], axis_index)
        )
    return jnp.concatenate(columns, axis=-1)


def dg_residual(conserved, face_data, star_flux, tables):
    stacked, extract, lifting, inverse, node_grid = tables
    fluxes = jnp.concatenate(
        [euler_flux(conserved, axis_index)[0] for axis_index in range(3)], axis=-1
    )
    volume = jnp.matmul(fluxes, stacked, precision=PRECISE)
    face_jumps = []
    for axis_index in range(3):
        face_jumps.append(
            face_part(star_flux, 2 * axis_index)
            - euler_flux(face_part(face_data, 2 * axis_index), axis_index)[0]
        )
        face_jumps.append(
            euler_flux(face_part(face_data, 2 * axis_index + 1), axis_index)[0]
            - face_part(star_flux, 2 * axis_index + 1)
        )
    surface = jnp.matmul(jnp.concatenate(face_jumps, axis=-1), lifting, precision=PRECISE)
    return GRID_SCALE * (surface - volume)


def fv_residual(conserved, star_flux, tables):
    stacked, extract, lifting, inverse, node_grid = tables
    summed = jnp.zeros_like(conserved)
    for axis_index in range(3):
        stride = 8 ** (2 - axis_index)
        neighbour = jnp.roll(conserved, -stride, axis=-1)
        interface = rusanov(conserved, neighbour, axis_index)
        lower_face = jnp.matmul(
            face_part(star_flux, 2 * axis_index),
            extract[:, 128 * axis_index : 128 * axis_index + 64].T,
            precision=PRECISE,
        )
        upper_face = jnp.matmul(
            face_part(star_flux, 2 * axis_index + 1),
            extract[:, 128 * axis_index + 64 : 128 * axis_index + 128].T,
            precision=PRECISE,
        )
        upper_flux = jnp.where(node_grid[axis_index] == 7, upper_face, interface)
        lower_flux = jnp.where(
            node_grid[axis_index] == 0, lower_face, jnp.roll(upper_flux, stride, axis=-1)
        )
        summed = summed + (lower_flux - upper_flux) * inverse[axis_index]
    return GRID_SCALE * summed


def on_device(conserved, troubled, blend_level):
    tables = node_tables()
    block_shape = conserved.shape[:3]
    face_data = jnp.matmul(conserved, tables[1], precision=PRECISE)
    mixed_rims = []
    for axis_index in range(3):
        layer_index = lax.broadcasted_iota(jnp.int32, block_shape + (1, 1), axis_index)
        choose = jnp.where(
            layer_index == block_shape[axis_index] - 1,
            face_part(face_data, 2 * axis_index + 1),
            face_part(face_data, 2 * axis_index),
        )
        mixed_rims.append(choose.reshape(block_shape + (320,)))
    padded = padded_2(jnp.stack(mixed_rims), (("gx", 1), ("gy", 2), ("gz", 3)), 1)
    below_faces = []
    above_faces = []
    for axis_index in range(3):
        slab_part = padded[axis_index]
        for other_axis in range(3):
            if other_axis != axis_index:
                slab_part = lax.slice_in_dim(
                    slab_part, 1, slab_part.shape[other_axis] - 1, axis=other_axis
                )
        slab_part = slab_part.reshape(slab_part.shape[:3] + (5, 64))
        length = block_shape[axis_index]
        from_below = lax.slice_in_dim(slab_part, 0, 1, axis=axis_index)
        from_above = lax.slice_in_dim(slab_part, length + 1, length + 2, axis=axis_index)
        below_faces.append(
            jnp.concatenate(
                [
                    from_below,
                    lax.slice_in_dim(
                        face_part(face_data, 2 * axis_index + 1), 0, length - 1, axis=axis_index
                    ),
                ],
                axis=axis_index,
            )
        )
        above_faces.append(
            jnp.concatenate(
                [
                    lax.slice_in_dim(
                        face_part(face_data, 2 * axis_index), 1, length, axis=axis_index
                    ),
                    from_above,
                ],
                axis=axis_index,
            )
        )
    star_flux = star_fluxes(face_data, below_faces, above_faces)
    smooth = dg_residual(conserved, face_data, star_flux, tables)
    elements = block_shape[0] * block_shape[1] * block_shape[2]
    groups = lax.axis_size("gx")
    total_slots = groups * SLOT
    live_int = (troubled.reshape(elements) > 0).astype(jnp.int32)
    rank_live = jnp.cumsum(live_int) - live_int
    owners = (lax.axis_index("gx") + rank_live // SLOT) % groups
    target = jnp.where(live_int > 0, owners * SLOT + rank_live % SLOT, -1)
    select = (
        lax.broadcasted_iota(jnp.int32, (total_slots, elements), 0) == target[None, :]
    ).astype(jnp.float32)
    payload = jnp.concatenate(
        [conserved.reshape(elements, 5, 512), star_flux.reshape(elements, 5, 384)], axis=-1
    )
    packed = jnp.einsum("se,evn->svn", select, payload, precision=PRECISE)
    occupied = jnp.sum(select, axis=1)
    vacant = 1.0 - occupied
    filler = jnp.zeros((5, 896), jnp.float32).at[0].set(1.0).at[4].set(2.5)
    packed = packed + vacant[:, None, None] * filler
    returned = fv_residual(packed[..., :512], packed[..., 512:], tables)
    subcell_part = jnp.einsum("se,svn->evn", select, returned, precision=PRECISE)
    weight = (
        troubled.reshape(elements).astype(jnp.float32)
        * blend_level.reshape(elements).astype(jnp.float32)
        / 5.0
    )
    flat_dg = smooth.reshape(elements, 5, 512)
    mixed_out = flat_dg + weight[:, None, None] * (subcell_part - flat_dg)
    return mixed_out.reshape(conserved.shape)


def solution(mesh):
    placed = (P("gx", "gy", "gz", None, None), P("gx", "gy", "gz"), P("gx", "gy", "gz"))
    return jax.shard_map(
        on_device,
        mesh=mesh,
        in_specs=placed,
        out_specs=P("gx", "gy", "gz", None, None),
        check_vma=False,
    )
```

profile of v0, /device:TPU:8, one launch (start us, length us, event | category | flops | bytes accessed | tf_op | source)
XLA Modules:
  0.0 92.2 jit_solution(5083410295971713449)
XLA Ops:
  0.0 2.6 %convolution_bitcast_fusion = f32[2,4,8,5,384]{4,2,3,1,0:T(8,128)S(1)} fusion(f32[512,384,1,1,1]{1,0,4,3,2:T(8,128)} %constant.205, f32[2,4,8,5,512]{4,2,3,1,0:T(8,128)} %param.17), kind=kOutput, calls=%fused_computation.46 | convolution fusion | flops 754974720 | bytes 1933312 | tf_op jit(solution)/shard_map/dot_general | solution.py:201
  3.4 10.2 %collective-permute-start.1 = (f32[3,1,4,8,320]{4,3,2,1,0:T(8,128)S(1)}, f32[3,1,4,8,320]{4,3,2,1,0:T(8,128)S(1)}, u32[]{:S(2)}, u32[]{:S(2)}) collective-permute-start(f32[3,1,4,8,320]{4,3,2,1,0:T(8,128)S(1)} %get-tuple-element.186), channel_id=1, source_target_pairs={{64,0},{128,64},{192,128},{256,192},{320,256},{384,320},{448,384},... | collective-permute-start | bytes 368648 | tf_op jit(solution)/shard_map/ppermute | solution.py:43
  13.6 1.9 %collective-permute-start = (f32[3,1,4,8,320]{4,3,2,1,0:T(8,128)S(1)}, f32[3,1,4,8,320]{4,3,2,1,0:T(8,128)S(1)}, u32[]{:S(2)}, u32[]{:S(2)}) collective-permute-start(f32[3,1,4,8,320]{4,3,2,1,0:T(8,128)S(1)} %get-tuple-element.185), channel_id=1, source_target_pairs={{0,64},{64,128},{128,192},{192,256},{256,320},{320,384},{384,448},... | collective-permute-start | bytes 368648 | tf_op jit(solution)/shard_map/ppermute | solution.py:42
  15.8 0.7 constant_dynamic-update-slice_fusion.67
  16.7 0.7 constant_dynamic-update-slice_fusion.66
  17.4 0.7 constant_dynamic-update-slice_fusion.65
  18.1 0.8 constant_dynamic-update-slice_fusion.71
  19.0 0.8 constant_dynamic-update-slice_fusion.63
  19.7 0.9 copy-done.3
  20.6 0.7 constant_dynamic-update-slice_fusion.69
  21.3 0.7 constant_dynamic-update-slice_fusion.68
  22.2 2.5 %collective-permute-done = f32[3,1,4,8,320]{4,3,2,1,0:T(8,128)S(1)} collective-permute-done((f32[3,1,4,8,320]{4,3,2,1,0:T(8,128)S(1)}, f32[3,1,4,8,320]{4,3,2,1,0:T(8,128)S(1)}, u32[]{:S(2)}, u32[]{:S(2)}) %collective-permute-start) | collective-permute-done | bytes 122912 | tf_op jit(solution)/shard_map/ppermute | solution.py:42
  24.7 6.7 %collective-permute-start.3 = (f32[3,4,1,8,320]{4,3,2,1,0:T(8,128)S(1)}, f32[3,4,1,8,320]{4,3,2,1,0:T(8,128)S(1)}, u32[]{:S(2)}, u32[]{:S(2)}) collective-permute-start(f32[3,4,1,8,320]{4,3,2,1,0:T(8,128)S(1)} %get-tuple-element.129), channel_id=1, source_target_pairs={{8,0},{16,8},{24,16},{32,24},{40,32},{48,40},{56,48},{0,56},{9,1},... | collective-permute-start | bytes 368648 | tf_op jit(solution)/shard_map/ppermute | solution.py:43
  31.4 1.9 %collective-permute-start.2 = (f32[3,4,1,8,320]{4,3,2,1,0:T(8,128)S(1)}, f32[3,4,1,8,320]{4,3,2,1,0:T(8,128)S(1)}, u32[]{:S(2)}, u32[]{:S(2)}) collective-permute-start(f32[3,4,1,8,320]{4,3,2,1,0:T(8,128)S(1)} %get-tuple-element.128), channel_id=1, source_target_pairs={{0,8},{8,16},{16,24},{24,32},{32,40},{40,48},{48,56},{56,0},{1,9},... | collective-permute-start | bytes 368648 | tf_op jit(solution)/shard_map/ppermute | solution.py:42
  33.4 0.6 collective-permute-done.3
  34.0 4.4 %collective-permute-done.2 = f32[3,4,1,8,320]{4,3,2,1,0:T(8,128)S(1)} collective-permute-done((f32[3,4,1,8,320]{4,3,2,1,0:T(8,128)S(1)}, f32[3,4,1,8,320]{4,3,2,1,0:T(8,128)S(1)}, u32[]{:S(2)}, u32[]{:S(2)}) %collective-permute-start.2) | collective-permute-done | bytes 122912 | tf_op jit(solution)/shard_map/ppermute | solution.py:42
  38.4 0.8 pad_maximum_fusion.17
  39.3 9.7 %collective-permute-start.5 = (f32[3,4,6,1,320]{4,3,2,1,0:T(1,128)}, f32[3,4,6,1,320]{4,3,2,1,0:T(1,128)}, u32[]{:S(2)}, u32[]{:S(2)}) collective-permute-start(f32[3,4,6,1,320]{4,3,2,1,0:T(1,128)} %get-tuple-element.115), channel_id=1, source_target_pairs={{1,0},{2,1},{3,2},{4,3},{5,4},{6,5},{7,6},{0,7},{9,8},{10,9},{11,1... | collective-permute-start | bytes 276488 | tf_op jit(solution)/shard_map/ppermute | solution.py:43
  49.0 2.1 %collective-permute-start.4 = (f32[3,4,6,1,320]{4,3,2,1,0:T(1,128)}, f32[3,4,6,1,320]{4,3,2,1,0:T(1,128)}, u32[]{:S(2)}, u32[]{:S(2)}) collective-permute-start(f32[3,4,6,1,320]{4,3,2,1,0:T(1,128)} %get-tuple-element.114), channel_id=1, source_target_pairs={{0,1},{1,2},{2,3},{3,4},{4,5},{5,6},{6,7},{7,0},{8,9},{9,10},{10,1... | collective-permute-start | bytes 276488 | tf_op jit(solution)/shard_map/ppermute | solution.py:42
  51.3 1.7 %collective-permute-done.5 = f32[3,4,6,1,320]{4,3,2,1,0:T(1,128)} collective-permute-done((f32[3,4,6,1,320]{4,3,2,1,0:T(1,128)}, f32[3,4,6,1,320]{4,3,2,1,0:T(1,128)}, u32[]{:S(2)}, u32[]{:S(2)}) %collective-permute-start.5) | collective-permute-done | bytes 92192 | tf_op jit(solution)/shard_map/ppermute | solution.py:43
  53.0 7.7 %collective-permute-done.4 = f32[3,4,6,1,320]{4,3,2,1,0:T(1,128)} collective-permute-done((f32[3,4,6,1,320]{4,3,2,1,0:T(1,128)}, f32[3,4,6,1,320]{4,3,2,1,0:T(1,128)}, u32[]{:S(2)}, u32[]{:S(2)}) %collective-permute-start.4) | collective-permute-done | bytes 92192 | tf_op jit(solution)/shard_map/ppermute | solution.py:42
  60.7 1.3 %pad_maximum_fusion = f32[3,4,6,10,320]{4,3,2,1,0:T(8,128)S(1)} fusion(f32[3,4,6,1,320]{4,3,2,1,0:T(1,128)} %collective-permute-done.5, f32[3,4,1,8,320]{4,3,2,1,0:T(8,128)S(1)} %collective-permute-done.3, f32[3,1,4,8,320]{4,3,2,1,0:T(8,128)S(1)} %collective-permute-done.1, f32[3,2,4,8,320]{4,3,2,1,0:T(8,128)S(1)} %constant_dynamic-update-slice_fusion, ...), kind=kLoop, calls=%fused_computation.6 | loop fusion | flops 1382400 | bytes 1843200 | tf_op jit(solution)/shard_map/concatenate | solution.py:44
  62.1 0.9 maximum_bitcast_fusion
  65.2 0.9 %fusion.129 = (f32[2,4,8,5,64]{4,2,3,1,0:T(8,128)}, f32[2,4,8,5,64]{4,2,3,1,0:T(8,128)S(1)}, f32[2,4,8,5,64]{4,2,3,1,0:T(8,128)}, f32[2,4,8,5,64]{4,2,3,1,0:T(8,...) fusion(f32[2,4,8,5,64]{4,2,3,1,0:T(8,128)S(1)} %get-tuple-element.134, ...), kind=kLoop, calls=%fused_computation.406 | loop fusion | flops 430080 | bytes 1523712 | tf_op jit(solution)/shard_map/sub | solution.py:166
  66.1 1.0 %fusion.133 = (f32[2,4,8,5,64]{4,2,3,1,0:T(8,128)}, f32[2,4,8,5,64]{4,2,3,1,0:T(8,128)S(1)}, f32[2,4,8,5,64]{4,2,3,1,0:T(8,128)}, f32[2,4,8,5,64]{4,2,3,1,0:T(8,...) fusion(f32[2,4,8,5,64]{4,2,3,1,0:T(8,128)S(1)} %get-tuple-element.162, ...), kind=kLoop, calls=%fused_computation.407 | loop fusion | flops 430080 | bytes 1523712 | tf_op jit(solution)/shard_map/sub | solution.py:162
  67.1 0.2 concatenate.78
  67.4 0.4 copy-done.11
  67.8 0.7 convolution_add_fusion
  68.6 0.7 slice.876
  69.3 0.2 slice.908
  69.5 0.2 slice.875
  70.0 2.3 %concatenate.76 = f32[2,4,8,5,384]{4,2,3,1,0:T(8,128)} concatenate(f32[2,4,8,5,64]{4,2,3,1,0:T(8,128)} %get-tuple-element.130, f32[2,4,8,5,64]{4,2,3,1,0:T(8,128)} %get-tuple-element.160, f32[2,4,8,5,64]{4,2,3,1,0:T(8,128)} %get-tuple-element.132, f32[2,4,8,5,64]{4,2,3,1,0:T(8,128)} %get-tuple-element.158, f32[2,4,8,5,64]{4,2,3,1,0:T(8,128)} %get-tuple-element.60, ...), dimensions={4} | concatenate | bytes 983040 | tf_op jit(solution)/shard_map/concatenate | solution.py:169
  72.3 2.6 %fusion.160 = f32[2,4,8,5,512]{4,2,3,1,0:T(8,128)S(1)} fusion(f32[2,4,8,5,384]{4,2,3,1,0:T(8,128)} %concatenate.76, f32[384,512,1,1,1]{1,0,4,3,2:T(8,128)} %constant.206), kind=kOutput, calls=%fused_computation.419 | convolution fusion | flops 754974720 | bytes 1933312 | tf_op jit(solution)/shard_map/dot_general | solution.py:169
  74.9 5.5 %fusion.11 = f32[2,4,8,5,512]{4,2,3,1,0:T(8,128)S(1)} fusion(f32[2,4,8,5,512]{4,2,3,1,0:T(8,128)S(1)} %fusion.160, f32[1536,512,1,1,1]{1,0,4,3,2:T(8,128)} %constant.207, f32[2,4,8,5,512]{4,2,3,1,0:T(8,128)S(1)} %copy-done.4, f32[2,4,8,5,512]{4,2,3,1,0:T(8,128)} %constant_dynamic-update-slice_fusion.68, f32[2,4,8,5,512]{4,2,3,1,0:T(8,128)S(1)} %copy-done.2), kind=kOutput, calls=%fused_computation.30 | convolution fusion | flops 3021209600 | bytes 6422528 | tf_op jit(solution)/shard_map/dot_general | solution.py:158
  80.5 0.2 multiply_bitcast_fusion
  80.8 0.6 copy-done.1
  81.4 0.2 constant_dynamic-update-slice_fusion.100
  82.1 0.8 copy-done.10
  82.8 0.8 convolution_select_fusion.4
  84.4 0.7 copy-done.9
  85.2 0.8 convolution_select_fusion.2
  86.4 0.7 copy-done.8
  87.1 0.8 convolution_select_fusion
  88.1 1.0 %fusion.22 = f32[64,5,512]{2,0,1:T(8,128)S(1)} fusion(f32[64,5,512]{2,0,1:T(8,128)S(1)} %convolution_select_fusion.4, f32[512,64,1]{1,0,2:T(8,128)S(1)} %copy-done.7, f32[64,5,448]{2,0,1:T(8,128)S(1)} %bitcast.71, f32[64,5,64]{2,0,1:T(8,128)S(1)} %slice.888, f32[512]{0:T(512)S(1)} %copy-done.16, pred[512]{0:T(512)(128)(4,1)S(1)} %copy-done.19, ...), kind=kOutput, calls=%fused_computation.45 | convolution fusion | flops 126484480 | bytes 2558464 | tf_op jit(solution)/shard_map/dot_general | solution.py:180
  89.1 0.8 fusion.20
  90.0 0.8 fusion.17
  90.8 0.5 fusion.7
  91.3 0.9 copy.33
  (161 shorter events, 5.9 us)
Async XLA Ops:
  3.3 12.5 %copy-start = (f32[2,4,8,5,512]{4,2,3,1,0:T(8,128)S(1)}, f32[2,4,8,5,512]{4,2,3,1,0:T(8,128)}, u32[]{:S(2)}) copy-start(f32[2,4,8,5,512]{4,2,3,1,0:T(8,128)} %param.17) | copy-start | bytes 1966084
  3.3 13.2 %copy-start.12 = (s32[2,4,8]{2,1,0:T(4,128)S(1)}, s32[2,4,8]{2,1,0:T(4,128)}, u32[]{:S(2)}) copy-start(s32[2,4,8]{2,1,0:T(4,128)} %param.18) | copy-start | bytes 772
  3.4 18.9 %collective-permute-start.1 = (f32[3,1,4,8,320]{4,3,2,1,0:T(8,128)S(1)}, f32[3,1,4,8,320]{4,3,2,1,0:T(8,128)S(1)}, u32[]{:S(2)}, u32[]{:S(2)}) collective-permute-start(f32[3,1,4,8,320]{4,3,2,1,0:T(8,128)S(1)} %get-tuple-element.186), channel_id=1, source_target_pairs={{64,0},{128,64},{192,128},{256,192},{320,256},{384,320},{448,384},... | collective-permute-start | bytes 368648 | tf_op jit(solution)/shard_map/ppermute | solution.py:43
  13.6 11.1 %collective-permute-start = (f32[3,1,4,8,320]{4,3,2,1,0:T(8,128)S(1)}, f32[3,1,4,8,320]{4,3,2,1,0:T(8,128)S(1)}, u32[]{:S(2)}, u32[]{:S(2)}) collective-permute-start(f32[3,1,4,8,320]{4,3,2,1,0:T(8,128)S(1)} %get-tuple-element.185), channel_id=1, source_target_pairs={{0,64},{64,128},{128,192},{192,256},{256,320},{320,384},{384,448},... | collective-permute-start | bytes 368648 | tf_op jit(solution)/shard_map/ppermute | solution.py:42
  19.0 3.2 %copy-start.13 = (s32[2,4,8]{2,1,0:T(4,128)S(1)}, s32[2,4,8]{2,1,0:T(4,128)}, u32[]{:S(2)}) copy-start(s32[2,4,8]{2,1,0:T(4,128)} %param.19) | copy-start | bytes 772
  19.7 0.9 copy-start.3
  24.7 9.3 %collective-permute-start.3 = (f32[3,4,1,8,320]{4,3,2,1,0:T(8,128)S(1)}, f32[3,4,1,8,320]{4,3,2,1,0:T(8,128)S(1)}, u32[]{:S(2)}, u32[]{:S(2)}) collective-permute-start(f32[3,4,1,8,320]{4,3,2,1,0:T(8,128)S(1)} %get-tuple-element.129), channel_id=1, source_target_pairs={{8,0},{16,8},{24,16},{32,24},{40,32},{48,40},{56,48},{0,56},{9,1},... | collective-permute-start | bytes 368648 | tf_op jit(solution)/shard_map/ppermute | solution.py:43
  31.4 7.0 %collective-permute-start.2 = (f32[3,4,1,8,320]{4,3,2,1,0:T(8,128)S(1)}, f32[3,4,1,8,320]{4,3,2,1,0:T(8,128)S(1)}, u32[]{:S(2)}, u32[]{:S(2)}) collective-permute-start(f32[3,4,1,8,320]{4,3,2,1,0:T(8,128)S(1)} %get-tuple-element.128), channel_id=1, source_target_pairs={{0,8},{8,16},{16,24},{24,32},{32,40},{40,48},{48,56},{56,0},{1,9},... | collective-permute-start | bytes 368648 | tf_op jit(solution)/shard_map/ppermute | solution.py:42
  39.3 13.7 %collective-permute-start.5 = (f32[3,4,6,1,320]{4,3,2,1,0:T(1,128)}, f32[3,4,6,1,320]{4,3,2,1,0:T(1,128)}, u32[]{:S(2)}, u32[]{:S(2)}) collective-permute-start(f32[3,4,6,1,320]{4,3,2,1,0:T(1,128)} %get-tuple-element.115), channel_id=1, source_target_pairs={{1,0},{2,1},{3,2},{4,3},{5,4},{6,5},{7,6},{0,7},{9,8},{10,9},{11,1... | collective-permute-start | bytes 276488 | tf_op jit(solution)/shard_map/ppermute | solution.py:43
  49.0 11.7 %collective-permute-start.4 = (f32[3,4,6,1,320]{4,3,2,1,0:T(1,128)}, f32[3,4,6,1,320]{4,3,2,1,0:T(1,128)}, u32[]{:S(2)}, u32[]{:S(2)}) collective-permute-start(f32[3,4,6,1,320]{4,3,2,1,0:T(1,128)} %get-tuple-element.114), channel_id=1, source_target_pairs={{0,1},{1,2},{2,3},{3,4},{4,5},{5,6},{6,7},{7,0},{8,9},{9,10},{10,1... | collective-permute-start | bytes 276488 | tf_op jit(solution)/shard_map/ppermute | solution.py:42
  67.1 0.7 copy-start.11
  72.3 2.6 %copy-start.2 = (f32[2,4,8,5,512]{4,2,3,1,0:T(8,128)S(1)}, f32[2,4,8,5,512]{4,2,3,1,0:T(8,128)}, u32[]{:S(2)}) copy-start(f32[2,4,8,5,512]{4,2,3,1,0:T(8,128)} %get-tuple-element.116) | copy-start | bytes 1966084
  72.3 2.6 %copy-start.4 = (f32[2,4,8,5,512]{4,2,3,1,0:T(8,128)S(1)}, f32[2,4,8,5,512]{4,2,3,1,0:T(8,128)}, u32[]{:S(2)}) copy-start(f32[2,4,8,5,512]{4,2,3,1,0:T(8,128)} %copy-done.3) | copy-start | bytes 1966084
  80.5 0.9 copy-start.1
  81.9 0.9 copy-start.10
  81.9 0.9 copy-start.22
  84.2 0.9 copy-start.9
  84.3 0.9 copy-start.21
  86.2 0.9 copy-start.8
  86.2 0.9 copy-start.20
  87.1 1.0 %copy-start.7 = (f32[512,64,1]{1,0,2:T(8,128)S(1)}, f32[512,64,1]{1,0,2:T(8,128)}, u32[]{:S(2)}) copy-start(f32[512,64,1]{1,0,2:T(8,128)} %constant.208) | copy-start | bytes 393220
  87.1 1.0 %copy-start.16 = (f32[512]{0:T(512)S(1)}, f32[512]{0:T(512)}, u32[]{:S(2)}) copy-start(f32[512]{0:T(512)} %constant.196) | copy-start | bytes 6148
  87.1 1.0 %copy-start.19 = (pred[512]{0:T(512)(128)(4,1)S(1)}, pred[512]{0:T(512)(128)(4,1)}, u32[]{:S(2)}) copy-start(pred[512]{0:T(512)(128)(4,1)} %constant.185.clone) | copy-start | bytes 1540
  88.0 1.0 %copy-start.6 = (f32[512,64,1]{1,0,2:T(8,128)S(1)}, f32[512,64,1]{1,0,2:T(8,128)}, u32[]{:S(2)}) copy-start(f32[512,64,1]{1,0,2:T(8,128)} %constant.210) | copy-start | bytes 393220
  88.1 1.0 %copy-start.15 = (f32[512]{0:T(512)S(1)}, f32[512]{0:T(512)}, u32[]{:S(2)}) copy-start(f32[512]{0:T(512)} %constant.200) | copy-start | bytes 6148
  88.1 1.0 %copy-start.18 = (pred[512]{0:T(512)(128)(4,1)S(1)}, pred[512]{0:T(512)(128)(4,1)}, u32[]{:S(2)}) copy-start(pred[512]{0:T(512)(128)(4,1)} %constant.187.clone) | copy-start | bytes 1540
  89.1 1.0 %copy-start.5 = (f32[512,64,1]{1,0,2:T(8,128)S(1)}, f32[512,64,1]{1,0,2:T(8,128)}, u32[]{:S(2)}) copy-start(f32[512,64,1]{1,0,2:T(8,128)} %constant.212) | copy-start | bytes 393220
  89.1 0.9 %copy-start.14 = (f32[512]{0:T(512)S(1)}, f32[512]{0:T(512)}, u32[]{:S(2)}) copy-start(f32[512]{0:T(512)} %constant.204) | copy-start | bytes 6148
  89.1 0.9 %copy-start.17 = (pred[512]{0:T(512)(128)(4,1)S(1)}, pred[512]{0:T(512)(128)(4,1)}, u32[]{:S(2)}) copy-start(pred[512]{0:T(512)(128)(4,1)} %constant.189.clone) | copy-start | bytes 1540
where the time goes:
time: 92.8 us; the launch traced here: 92.2 us
  starting transfers between devices  32.6 us (35%)
  waiting for transfers between devices  16.9 us (18%)
  matrix products  16.8 us (18%)
  other arithmetic  13.1 us (14%)
  local copies, waits for them, and re-layouts  11.9 us (13%)
  between operations  0.99 us (1%)
    ppermute x3, starting transfers between devices, padded_2(): after = lax.ppermute(leading, axis, down)  26.6 us
    ppermute x3, waiting for transfers between devices, padded_2(): before = lax.ppermute(last, axis, up)  14.5 us
    ppermute x3, starting transfers between devices, padded_2(): before = lax.ppermute(last, axis, up)  5.94 us
    dot_general x1, matrix products, dg_residual(): volume = jnp.matmul(fluxes, stacked, precision=PRECISE)  5.52 us
    unnamed x63, local copies, waits for them, and re-layouts  5.24 us
    unnamed x48, other arithmetic  4.57 us
    dot_general x1, matrix products, dg_residual(): jnp.matmul(jnp.concatenate(face_jumps, axis=-1), lifting, precision=PRECISE)  2.6 us
    dot_general x1, matrix products, on_device(): face_data = jnp.matmul(conserved, tables[1], precision=PRECISE)  2.56 us
  transfers between devices with their start and end apart: 6, of which 5 were waited for; matrix products, arithmetic and copies ran while one was open for 7% of the time, Pallas kernels for 0%

commit v1 on v0

v1 whole, which is shorter than its diff:
```python
import functools

import jax
import jax.numpy as jnp
import numpy as np
from jax import lax
from jax.experimental import pallas as pl
from jax.experimental.pallas import tpu as pltpu
from jax.sharding import PartitionSpec as P

AXES = ("gx", "gy", "gz")
HEAT_RATIO = 1.4
GRID_SCALE = 0.05
PRECISE = lax.Precision.HIGHEST
LOBATTO_POINTS = [
    -1.0,
    -0.8717401485096066,
    -0.5917001814331423,
    -0.2092992179024789,
    0.2092992179024789,
    0.5917001814331423,
    0.8717401485096066,
    1.0,
]
LOBATTO_WEIGHTS = [
    0.03571428571428571,
    0.21070422714350603,
    0.34112269248350435,
    0.4124587946587039,
    0.4124587946587039,
    0.34112269248350435,
    0.21070422714350603,
    0.03571428571428571,
]
EDGE = GRID_SCALE / LOBATTO_WEIGHTS[0]
ROWS = 40


def weak_tables():
    points = np.array(LOBATTO_POINTS)
    weights = np.array(LOBATTO_WEIGHTS)
    bary = np.array([1.0 / np.prod([points[i] - points[j] for j in range(8) if j != i]) for i in range(8)])
    derivative = np.zeros((8, 8))
    for i in range(8):
        for j in range(8):
            if i != j:
                derivative[i, j] = bary[j] / bary[i] / (points[i] - points[j])
        derivative[i, i] = -np.sum(derivative[i])
    derivative[0, 0] += 1.0 / weights[0]
    derivative[7, 7] -= 1.0 / weights[0]
    weak = -GRID_SCALE * derivative.T
    eye = np.eye(8)
    along_x = np.kron(weak, np.eye(64))
    along_y = np.kron(np.eye(4), np.kron(weak, eye))
    along_z = np.kron(np.eye(32), weak)
    return [jnp.asarray(m, jnp.float32) for m in (along_x, along_y, along_z)]


def lanes_of(shape):
    return lax.broadcasted_iota(jnp.int32, shape, len(shape) - 1)


def roll(value, shift):
    shift = shift % 128
    return value if shift == 0 else pltpu.roll(value, shift, value.ndim - 1)


def euler(u, d):
    rho, mom, energy = u[0], u[1:4], u[4]
    inv = 1.0 / rho
    normal = mom[d] * inv
    kinetic = 0.5 * (mom[0] * mom[0] + mom[1] * mom[1] + mom[2] * mom[2]) * inv
    pressure = (HEAT_RATIO - 1.0) * (energy - kinetic)
    sound = jnp.sqrt(HEAT_RATIO * pressure * inv)
    flux = [mom[d], mom[0] * normal, mom[1] * normal, mom[2] * normal, (energy + pressure) * normal]
    flux[1 + d] = flux[1 + d] + pressure
    return flux, jnp.abs(normal) + sound


def upwind(left, left_flux, left_speed, right, right_flux, right_speed):
    half = 0.5 * jnp.maximum(left_speed, right_speed)
    return [0.5 * (fl + fr) - half * (ur - ul) for ul, fl, ur, fr in zip(left, left_flux, right, right_flux)]


def rusanov(left, right, d):
    return upwind(left, *euler(left, d), right, *euler(right, d))


def squeeze(tile, lane, first):
    tile = roll(tile, -first)
    for bit in range(4):
        step = 1 << bit
        moved = functools.reduce(
            jnp.logical_or, [lane == 8 * m - 7 * (m % (2 * step)) for m in range(16) if m & step]
        )
        tile = jnp.where(moved, roll(tile, -7 * step), tile)
    return tile


def spread(tile, lane):
    for bit in reversed(range(4)):
        step = 1 << bit
        moved = functools.reduce(
            jnp.logical_or, [lane == 8 * m - 7 * (m % step) for m in range(16) if m & step]
        )
        tile = jnp.where(moved, roll(tile, 7 * step), tile)
    return tile


def faces_kernel(x_ref, out_ref):
    lane3 = lanes_of((ROWS, 128))
    for q in range(2):
        first = x_ref[pl.ds((2 * q) * ROWS, ROWS), 0:128]
        second = x_ref[pl.ds((2 * q + 1) * ROWS, ROWS), 0:128]
        out_ref[pl.ds(q * ROWS, ROWS), :] = jnp.where(lane3 < 64, first, roll(second, 64))
        first = x_ref[pl.ds((4 + 2 * q) * ROWS, ROWS), 384:512]
        second = x_ref[pl.ds((4 + 2 * q + 1) * ROWS, ROWS), 384:512]
        out_ref[pl.ds((2 + q) * ROWS, ROWS), :] = jnp.where(lane3 < 64, roll(first, 64), second)
    for face, (ey, j) in enumerate(((0, 0), (3, 7))):
        packed = None
        for ex in range(2):
            for i in range(8):
                chunk, half = i // 2, i % 2
                goal = ex * 64 + i * 8
                piece = x_ref[pl.ds((ex * 4 + ey) * ROWS, ROWS), chunk * 128 : (chunk + 1) * 128]
                piece = roll(piece, goal - half * 64 - j * 8)
                packed = piece if packed is None else jnp.where(lane3 >= goal, piece, packed)
        out_ref[pl.ds((4 + face) * ROWS, ROWS), :] = packed
    lane = lanes_of((8, 128))
    sub = lax.broadcasted_iota(jnp.int32, (8, 128), 0)
    for comp in range(5):
        packed = None
        for face, (ez, k) in enumerate(((0, 0), (7, 7))):
            for chunk in range(4):
                piece = None
                for e in range(8):
                    row = x_ref[pl.ds(e * ROWS + comp * 8 + ez, 1), chunk * 128 : (chunk + 1) * 128]
                    row = jnp.broadcast_to(row, (8, 128))
                    piece = row if piece is None else jnp.where(sub >= e, row, piece)
                piece = squeeze(piece, lane, k)
                goal = face * 64 + chunk * 16
                packed = piece if packed is None else jnp.where(lane >= goal, roll(piece, goal), packed)
        out_ref[pl.ds(6 * ROWS + comp * 8, 8), :] = packed


def inner_kernel(x_ref, blend_ref, mx_ref, my_ref, mz_ref, out_ref, flux_ref, speed_ref, gy_ref, gx_ref):
    lane = lanes_of((8, 128))
    sub = lax.broadcasted_iota(jnp.int32, (8, 128), 0)
    k, j, half = lane % 8, (lane // 8) % 8, lane // 64
    weights = [float(w) for w in LOBATTO_WEIGHTS]

    def by_index(index, table):
        value = jnp.full(index.shape, table[0], jnp.float32)
        for n in range(1, 8):
            value = jnp.where(index == n, table[n], value)
        return value

    scale = [GRID_SCALE / w for w in weights]
    scale_z, scale_y = by_index(k, scale), by_index(j, scale)
    scale_x = [jnp.where(half == 0, scale[2 * c], scale[2 * c + 1]) for c in range(4)]

    def tile(ref, row, c):
        return ref[pl.ds(pl.multiple_of(row, 8), 8), c * 128 : (c + 1) * 128]

    def put(ref, row, c, value):
        ref[pl.ds(pl.multiple_of(row, 8), 8), c * 128 : (c + 1) * 128] = value

    def fluxes(e, carry):
        for c in range(4):
            u = [tile(x_ref, e * ROWS + 8 * n, c) for n in range(5)]
            rho, mom, energy = u[0], u[1:4], u[4]
            inv = 1.0 / rho
            vel = [m * inv for m in mom]
            kinetic = 0.5 * (mom[0] * vel[0] + mom[1] * vel[1] + mom[2] * vel[2])
            pressure = (HEAT_RATIO - 1.0) * (energy - kinetic)
            sound = jnp.sqrt(HEAT_RATIO * pressure * inv)
            total = energy + pressure
            for d in range(3):
                f = [mom[d]] + [mom[n] * vel[d] for n in range(3)] + [total * vel[d]]
                f[1 + d] = f[1 + d] + pressure
                for n in range(5):
                    put(flux_ref.at[d], e * ROWS + 8 * n, c, f[n])
                put(speed_ref.at[d], e * 8, c, jnp.abs(vel[d]) + sound)
        return carry

    lax.fori_loop(0, 8, fluxes, 0)

    def volume(r, carry):
        rows = pl.ds(pl.multiple_of(r * 80, 8), 80)
        total = jnp.dot(flux_ref[0, rows, :], mx_ref[...], precision=PRECISE, preferred_element_type=jnp.float32)
        for h in range(2):
            cols = slice(256 * h, 256 * h + 256)
            part = jnp.dot(
                flux_ref[1, rows, cols], my_ref[...], precision=PRECISE, preferred_element_type=jnp.float32
            ) + jnp.dot(flux_ref[2, rows, cols], mz_ref[...], precision=PRECISE, preferred_element_type=jnp.float32)
            out_ref[rows, cols] = total[:, cols] + part
        return carry

    lax.fori_loop(0, 4, volume, 0)

    def subcells(e, carry):
        ex, ey = e // 4, e % 4
        blend = blend_ref[pl.ds(pl.multiple_of(e * 8, 8), 8), :]
        up_y = jnp.minimum(e + 1, 7)
        up_x = jnp.minimum(e + 4, 7)
        has_up_y = jnp.where(ey < 3, 1.0, 0.0)
        has_up_x = jnp.where(ex == 0, 1.0, 0.0)
        low_y = jnp.maximum(e - 1, 0)
        has_low_y, has_low_x = ey > 0, ex == 1
        acc = {}

        def gather(e_row, c, d):
            u = [tile(x_ref, e_row * ROWS + 8 * n, c) for n in range(5)]
            f = [u[1 + d]] + [tile(flux_ref.at[d], e_row * ROWS + 8 * n, c) for n in range(1, 5)]
            return u + f[1:] + [tile(speed_ref.at[d], e_row * 8, c)]

        def interface(own, other, d):
            lu, ru = own[:5], other[:5]
            lf, rf = [lu[1 + d]] + own[5:9], [ru[1 + d]] + other[5:9]
            return upwind(lu, lf, own[9], ru, rf, other[9])

        for c in range(4):
            own = gather(e, c, 2)
            other = [
                jnp.where(k == 7, pltpu.roll(roll(v, 7), 7, 0), roll(v, -1)) for v in own
            ]
            weight = jnp.where(k == 7, jnp.where(sub < 7, 1.0, 0.0), blend)
            for n, g in enumerate(interface(own, other, 2)):
                g = g * weight
                low = jnp.where(k == 0, pltpu.roll(roll(g, -7), 1, 0), roll(g, 1))
                acc[n, c] = (low - g) * scale_z
            own = gather(e, c, 1)
            beyond = gather(up_y, c, 1)
            other = [jnp.where(j == 7, roll(b, 56), roll(v, -8)) for v, b in zip(own, beyond)]
            weight = jnp.where(j == 7, has_up_y, blend)
            for n, g in enumerate(interface(own, other, 1)):
                g = g * weight
                below = jnp.where(has_low_y, tile(gy_ref, low_y * ROWS + 8 * n, c), 0.0)
                low = jnp.where(j == 0, roll(below, -56), roll(g, 8))
                put(gy_ref, e * ROWS + 8 * n, c, g)
                acc[n, c] = acc[n, c] + (low - g) * scale_y
        own = [gather(e, c, 0) for c in range(4)]
        turned = [[roll(v, 64) for v in own[c]] for c in range(4)]
        turned.append([roll(v, 64) for v in gather(up_x, 0, 0)])
        before = [roll(jnp.where(has_low_x, tile(gx_ref, (e % 4) * ROWS + 8 * n, 0), 0.0), 64) for n in range(5)]
        for c in range(4):
            other = [jnp.where(half == 0, a, b) for a, b in zip(turned[c], turned[c + 1])]
            weight = jnp.where(half == 1, has_up_x, blend) if c == 3 else blend
            for n, g in enumerate(interface(own[c], other, 0)):
                g = g * weight
                if c == 3:
                    put(gx_ref, (e % 4) * ROWS + 8 * n, 0, g)
                moved = roll(g, 64)
                low = jnp.where(half == 0, before[n], moved)
                before[n] = moved
                here = acc[n, c] + (low - g) * scale_x[c]
                row = e * ROWS + 8 * n
                put(out_ref, row, c, tile(out_ref, row, c) * (1.0 - blend) + here)
        return carry

    lax.fori_loop(0, 8, subcells, 0)


def outer_kernel(place_ref, pre_ref, own_ref, halo_ref, near_ref, far_ref, out_ref):
    lane = lanes_of((8, 128))
    left_half = lane < 64
    core, odd_x, odd_y = place_ref[0], place_ref[1], place_ref[2]
    out_ref[...] = pre_ref[...]

    def own(tile):
        return own_ref[pl.ds(tile * 8, 8), :]

    def add(row, c, value):
        out_ref[pl.ds(row, 8), c * 128 : (c + 1) * 128] = (
            out_ref[pl.ds(row, 8), c * 128 : (c + 1) * 128] + value
        )

    zero = jnp.zeros((8, 128), jnp.float32)
    for q in range(2):
        mine = [own(5 * q + n) for n in range(5)]
        below = [halo_ref[0, 1 - odd_x, core, pl.ds((5 * q + n) * 8, 8), :] for n in range(5)]
        for n, star in enumerate(rusanov(below, mine, 0)):
            star = EDGE * star
            add((2 * q) * ROWS + 8 * n, 0, jnp.where(left_half, star, zero))
            add((2 * q + 1) * ROWS + 8 * n, 0, jnp.where(left_half, roll(star, 64), zero))
        mine = [own(10 + 5 * q + n) for n in range(5)]
        above = [halo_ref[0, odd_x, core, pl.ds((5 * q + n) * 8, 8), :] for n in range(5)]
        for n, star in enumerate(rusanov(mine, above, 0)):
            star = -EDGE * star
            add((4 + 2 * q) * ROWS + 8 * n, 3, jnp.where(left_half, zero, roll(star, 64)))
            add((4 + 2 * q + 1) * ROWS + 8 * n, 3, jnp.where(left_half, zero, star))
    for face, (ey, j) in enumerate(((0, 0), (3, 7))):
        mine = [own(20 + 5 * face + n) for n in range(5)]
        if face == 0:
            below = [halo_ref[1, 1 - odd_y, core, pl.ds((5 + n) * 8, 8), :] for n in range(5)]
            stars = [EDGE * s for s in rusanov(below, mine, 1)]
        else:
            above = [halo_ref[1, odd_y, core, pl.ds(n * 8, 8), :] for n in range(5)]
            stars = [-EDGE * s for s in rusanov(mine, above, 1)]
        for n, star in enumerate(stars):
            for ex in range(2):
                for c in range(4):
                    start = ex * 64 + 16 * c
                    first = roll(star, j * 8 - start)
                    second = roll(star, 64 + j * 8 - start - 8)
                    value = jnp.where(left_half, first, second)
                    value = jnp.where((lane // 8) % 8 == j, value, zero)
                    add((ex * 4 + ey) * ROWS + 8 * n, c, value)
    first_core = core == 0
    mine = [own(30 + n) for n in range(5)]
    other = []
    for n in range(5):
        near = near_ref[1 - core, pl.ds((30 + n) * 8, 8), :]
        far = far_ref[pl.ds(n * 8, 8), :]
        above = jnp.where(first_core, near, far)
        below = jnp.where(first_core, far, near)
        other.append(roll(jnp.where(left_half, above, below), 64))
    left = [jnp.where(left_half, o, m) for o, m in zip(other, mine)]
    right = [jnp.where(left_half, m, o) for o, m in zip(other, mine)]
    for n, star in enumerate(rusanov(left, right, 2)):
        for face, (ez, k) in enumerate(((0, 0), (7, 7))):
            signed = (EDGE if face == 0 else -EDGE) * star
            for c in range(4):
                value = roll(spread(roll(signed, -(face * 64 + 16 * c)), lane), k)
                value = jnp.where(lane % 8 == k, value, zero)
                cols = slice(c * 128, (c + 1) * 128)
                for e in range(8):
                    row = pl.ds(e * ROWS + n * 8 + ez, 1)
                    out_ref[row, cols] = out_ref[row, cols] + value[e : e + 1, :]


def pairs(size, shift):
    return [[(2 * n + shift) % size, (2 * n + 1 + shift) % size] for n in range(size // 2)]


def crossed(sizes, shift):
    nx, ny, nz = sizes
    moves = []
    for z in range(nz):
        for a, b in pairs(nx, shift) if z % 2 == 0 else pairs(ny, shift):
            for other in range(ny if z % 2 == 0 else nx):
                ends = [((v * ny + other) if z % 2 == 0 else (other * ny + v)) * nz + z for v in (a, b)]
                moves += [(ends[0], ends[1]), (ends[1], ends[0])]
    return sorted(set(moves))


def in_vmem():
    return pl.BlockSpec(memory_space=pltpu.VMEM)


LIMIT = pltpu.CompilerParams(vmem_limit_bytes=32 * 1024 * 1024)


def on_device(conserved, troubled, blend_level):
    sizes = [lax.axis_size(a) for a in AXES]
    ix, iy, iz = [lax.axis_index(a) for a in AXES]
    core, odd_x, odd_y = iz & 1, ix & 1, iy & 1
    state = conserved.transpose(0, 1, 3, 2, 4).reshape(8 * ROWS, 512)

    own = pl.pallas_call(
        faces_kernel,
        out_shape=jax.ShapeDtypeStruct((7 * ROWS, 128), jnp.float32),
        in_specs=[in_vmem()],
        out_specs=in_vmem(),
        compiler_params=LIMIT,
        name="faces",
    )(state)

    both = lax.all_gather(own, "gz", axis_index_groups=pairs(sizes[2], 0))
    x_faces = both[:, : 4 * ROWS].reshape(2, 2, 2 * ROWS, 128)
    y_faces = both[:, 4 * ROWS : 6 * ROWS]
    arrived = []
    for shift in range(2):
        face = odd_x if shift else 1 - odd_x
        x_part = lax.dynamic_index_in_dim(x_faces, face, 1, keepdims=False)
        sent = jnp.where(core == 0, x_part, y_faces)
        arrived.append(lax.ppermute(sent, AXES, crossed(sizes, shift)))
    swap = pairs(sizes[2], 1)
    far = lax.ppermute(own[6 * ROWS :], "gz", [(a, b) for a, b in swap] + [(b, a) for a, b in swap])

    blend = troubled.reshape(64).astype(jnp.float32) * blend_level.reshape(64).astype(jnp.float32) / 5.0
    inner = pl.pallas_call(
        inner_kernel,
        out_shape=jax.ShapeDtypeStruct((8 * ROWS, 512), jnp.float32),
        in_specs=[in_vmem()] * 5,
        out_specs=in_vmem(),
        scratch_shapes=[
            pltpu.VMEM((3, 8 * ROWS, 512), jnp.float32),
            pltpu.VMEM((3, 64, 512), jnp.float32),
            pltpu.VMEM((8 * ROWS, 512), jnp.float32),
            pltpu.VMEM((4 * ROWS, 128), jnp.float32),
        ],
        compiler_params=LIMIT,
        cost_estimate=pl.CostEstimate(flops=4_000_000_000, bytes_accessed=3_000_000, transcendentals=65536),
        name="inner",
    )(state, jnp.broadcast_to(blend[:, None], (64, 128)), *weak_tables())

    halo = lax.all_gather(jnp.stack(arrived), "gz", axis_index_groups=pairs(sizes[2], 0))
    place = jnp.stack([core, odd_x, odd_y]).astype(jnp.int32)
    full = pl.pallas_call(
        outer_kernel,
        out_shape=jax.ShapeDtypeStruct((8 * ROWS, 512), jnp.float32),
        in_specs=[pl.BlockSpec(memory_space=pltpu.SMEM)] + [in_vmem()] * 5,
        out_specs=in_vmem(),
        compiler_params=LIMIT,
        name="outer",
    )(place, inner, own, halo, both, far)
    return full.reshape(2, 4, 5, 8, 512).transpose(0, 1, 3, 2, 4)


def solution(mesh):
    placed = (P("gx", "gy", "gz", None, None), P("gx", "gy", "gz"), P("gx", "gy", "gz"))
    return jax.shard_map(
        on_device,
        mesh=mesh,
        in_specs=placed,
        out_specs=P("gx", "gy", "gz", None, None),
        check_vma=False,
    )
```

time: 92.8 us -> 51.2 us (0.55)
  the two profiles are of different devices: /device:TPU:8 before, /device:TPU:1 now
where the time goes in v1:
time: 51.2 us; the launch traced here: 50.9 us
  starting transfers between devices  20.4 us (40%)
  Pallas kernels  15.1 us (29%)
  blocking collectives  12.8 us (25%)
  local copies, waits for them, and re-layouts  2.24 us (4%)
    ppermute x1, starting transfers between devices, on_device(): lax.ppermute(own[6 * ROWS:], 'gz', [(a, b) for a, b in swap] + [(b, a) fo...  12.2 us
    pallas_call x1, Pallas kernels, on_device(): pl.pallas_call(inner_kernel, out_shape=jax.ShapeDtypeStruct((8 * ROWS, 51...  11.5 us
    all_gather x1, blocking collectives, on_device(): both = lax.all_gather(own, 'gz', axis_index_groups=pairs(sizes[2], 0))  8.76 us
    ppermute x2, starting transfers between devices, on_device(): arrived.append(lax.ppermute(sent, AXES, crossed(sizes, shift)))  8.21 us
    all_gather x1, blocking collectives, on_device(): lax.all_gather(jnp.stack(arrived), 'gz', axis_index_groups=pairs(sizes[2]...  4.09 us
    pallas_call x1, Pallas kernels, on_device(): pl.pallas_call(outer_kernel, out_shape=jax.ShapeDtypeStruct((8 * ROWS, 51...  2.41 us
    unnamed x14, local copies, waits for them, and re-layouts  2.06 us
    pallas_call x1, Pallas kernels, on_device(): pl.pallas_call(faces_kernel, out_shape=jax.ShapeDtypeStruct((7 * ROWS, 12...  1.25 us
  transfers between devices with their start and end apart: 3, of which 0 were waited for; matrix products, arithmetic and copies ran while one was open for 1% of the time, Pallas kernels for 23%

profile of v1, /device:TPU:1, one launch (start us, length us, event | category | flops | bytes accessed | tf_op | source)
XLA Modules:
  0.0 50.9 jit_solution(17959533892776373268)
XLA Ops:
  0.0 0.0 copy-start
  0.0 1.1 %copy-done = f32[2,4,8,5,512]{4,2,3,1,0:T(8,128)S(1)} copy-done((f32[2,4,8,5,512]{4,2,3,1,0:T(8,128)S(1)}, f32[2,4,8,5,512]{4,2,3,1,0:T(8,128)}, u32[]{:S(2)}) %copy-start) | copy-done | bytes 655384
  1.1 0.0 copy-start.2
  1.1 1.2 %faces.1.own_ref = f32[280,128]{1,0:T(8,128)S(1)} custom-call(f32[320,512]{1,0:T(8,128)S(1)} %bitcast.26), custom_call_target="tpu_custom_call" | custom-call | tf_op jit(solution)/shard_map/faces/pallas_call | solution.py:360
  2.3 0.0 copy-start.1
  2.4 12.2 %collective-permute-start.2 = (f32[40,128]{1,0:T(8,128)S(1)}, f32[40,128]{1,0:T(8,128)S(1)}, u32[]{:S(2)}, u32[]{:S(2)}) collective-permute-start(f32[40,128]{1,0:T(8,128)S(1)} %slice.14), channel_id=1, source_target_pairs={{1,2},{3,4},{5,6},{7,0},{2,1},{4,3},{6,5},{0,7},{9,10},{11,12},{13... | collective-permute-start | bytes 61448 | tf_op jit(solution)/shard_map/ppermute | solution.py:379
  14.5 8.8 %all-gather = f32[560,128]{1,0:T(8,128)S(1)} all-gather(f32[280,128]{1,0:T(8,128)S(1)} %faces.1.own_ref), channel_id=2, replica_groups={{0,1},{2,3},{4,5},{6,7},{8,9},{10,11},{12,13},{14,15},{16,17},{18,19},{..., dimensions={0}, use_global_device_ids=true | all-gather | bytes 430080 | tf_op jit(solution)/shard_map/all_gather | solution.py:369
  23.3 0.0 copy-start.3
  23.4 3.3 %collective-permute-start = (f32[2,80,128]{2,1,0:T(8,128)S(1)}, f32[2,80,128]{2,1,0:T(8,128)S(1)}, u32[]{:S(2)}, u32[]{:S(2)}) collective-permute-start(f32[2,80,128]{2,1,0:T(8,128)S(1)} %get-tuple-element.5), channel_id=1, source_target_pairs={{0,64},{1,9},{2,66},{3,11},{4,68},{5,13},{6,70},{7,15},{8,72},{9,1... | collective-permute-start | bytes 245768 | tf_op jit(solution)/shard_map/ppermute | solution.py:377
  26.7 0.0 copy-start.6
  26.7 0.0 copy-start.5
  26.7 4.9 %collective-permute-start.1 = (f32[2,80,128]{2,1,0:T(8,128)S(1)}, f32[2,80,128]{2,1,0:T(8,128)S(1)}, u32[]{:S(2)}, u32[]{:S(2)}) collective-permute-start(f32[2,80,128]{2,1,0:T(8,128)S(1)} %get-tuple-element.6), channel_id=1, source_target_pairs={{0,960},{1,57},{2,962},{3,59},{4,964},{5,61},{6,966},{7,63},{8,968... | collective-permute-start | bytes 245768 | tf_op jit(solution)/shard_map/ppermute | solution.py:377
  31.6 0.0 copy-done.6
  31.6 0.0 copy-done.5
  31.6 0.1 div.10
  31.7 0.1 broadcast_in_dim.2.blend_ref
  31.8 0.0 copy-done.2
  31.8 0.0 copy-done.1
  31.8 0.0 copy-done.3
  31.8 0.0 copy-start.4
  31.8 0.9 %copy-done.4 = f32[256,256]{1,0:T(8,128)S(1)} copy-done((f32[256,256]{1,0:T(8,128)S(1)}, f32[256,256]{1,0:T(8,128)}, u32[]{:S(2)}) %copy-start.4) | copy-done | bytes 262168
  32.8 11.5 %inner.1.pre_ref = f32[320,512]{1,0:T(8,128)S(1)} custom-call(f32[320,512]{1,0:T(8,128)S(1)} %bitcast.27, f32[64,128]{1,0:T(8,128)S(1)} %broadcast_in_dim.2.blend_ref, f32[512,512]{1,0:T(8,128)S(1)} %copy-done.2, f32[256,256]{1,0:T(8,128)S(1)} %copy-done.4, f32[256,256]{1,0:T(8,128)S(1)} %copy-done.3), custom_call_target="tpu_custom_call" | custom-call | flops 4000000000 | bytes 3000000 | tf_op jit(solution)/shard_map/inner/pallas_call | solution.py:382
  44.2 0.1 pad_add_fusion.place_ref
  44.3 0.0 collective-permute-done
  44.3 0.0 collective-permute-done.1
  44.4 4.1 %all-gather.1 = f32[4,2,80,128]{3,2,1,0:T(8,128)S(1)} all-gather(f32[2,2,80,128]{3,2,1,0:T(8,128)S(1)} %pad_maximum_fusion), channel_id=3, replica_groups={{0,1},{2,3},{4,5},{6,7},{8,9},{10,11},{12,13},{14,15},{16,17},{18,19},{..., dimensions={0}, use_global_device_ids=true | all-gather | bytes 491520 | tf_op jit(solution)/shard_map/all_gather | solution.py:398
  48.4 0.0 collective-permute-done.2.far_ref
  48.4 2.4 %outer.1 = f32[320,512]{1,0:T(8,128)} custom-call(s32[3]{0:T(128)S(1)} %pad_add_fusion.place_ref, f32[320,512]{1,0:T(8,128)S(1)} %inner.1.pre_ref, f32[280,128]{1,0:T(8,128)S(1)} %faces.1.own_ref, f32[2,2,2,80,128]{4,3,2,1,0:T(8,128)S(1)} %bitcast.25, f32[2,280,128]{2,1,0:T(8,128)S(1)} %bitcast.24, f32[40,128]{1,0:T(8,128)S(1)} %collective-permute-done.2.far_ref), custom_call_target="tpu_custom_call" | custom-call | tf_op jit(solution)/shard_map/outer/pallas_call | solution.py:400
  (5 shorter events, 0.1 us)
Async XLA Ops:
  0.0 1.1 %copy-start = (f32[2,4,8,5,512]{4,2,3,1,0:T(8,128)S(1)}, f32[2,4,8,5,512]{4,2,3,1,0:T(8,128)}, u32[]{:S(2)}) copy-start(f32[2,4,8,5,512]{4,2,3,1,0:T(8,128)} %param.6) | copy-start | bytes 1966084
  1.1 30.7 %copy-start.2 = (f32[512,512]{1,0:T(8,128)S(1)}, f32[512,512]{1,0:T(8,128)}, u32[]{:S(2)}) copy-start(f32[512,512]{1,0:T(8,128)} %constant.35.clone.mx_ref) | copy-start | bytes 3145732
  2.3 29.5 %copy-start.1 = (f32[2,4,8,5,512]{4,2,3,1,0:T(8,128)S(1)}, f32[2,4,8,5,512]{4,2,3,1,0:T(8,128)}, u32[]{:S(2)}) copy-start(f32[2,4,8,5,512]{4,2,3,1,0:T(8,128)} %param.6) | copy-start | bytes 1966084
  2.4 46.1 %collective-permute-start.2 = (f32[40,128]{1,0:T(8,128)S(1)}, f32[40,128]{1,0:T(8,128)S(1)}, u32[]{:S(2)}, u32[]{:S(2)}) collective-permute-start(f32[40,128]{1,0:T(8,128)S(1)} %slice.14), channel_id=1, source_target_pairs={{1,2},{3,4},{5,6},{7,0},{2,1},{4,3},{6,5},{0,7},{9,10},{11,12},{13... | collective-permute-start | bytes 61448 | tf_op jit(solution)/shard_map/ppermute | solution.py:379
  23.3 8.5 %copy-start.3 = (f32[256,256]{1,0:T(8,128)S(1)}, f32[256,256]{1,0:T(8,128)}, u32[]{:S(2)}) copy-start(f32[256,256]{1,0:T(8,128)} %constant.37.clone.mz_ref) | copy-start | bytes 786436
  23.4 21.0 %collective-permute-start = (f32[2,80,128]{2,1,0:T(8,128)S(1)}, f32[2,80,128]{2,1,0:T(8,128)S(1)}, u32[]{:S(2)}, u32[]{:S(2)}) collective-permute-start(f32[2,80,128]{2,1,0:T(8,128)S(1)} %get-tuple-element.5), channel_id=1, source_target_pairs={{0,64},{1,9},{2,66},{3,11},{4,68},{5,13},{6,70},{7,15},{8,72},{9,1... | collective-permute-start | bytes 245768 | tf_op jit(solution)/shard_map/ppermute | solution.py:377
  26.7 4.9 %copy-start.6 = (s32[2,4,8]{2,1,0:T(4,128)S(1)}, s32[2,4,8]{2,1,0:T(4,128)}, u32[]{:S(2)}) copy-start(s32[2,4,8]{2,1,0:T(4,128)} %param.7) | copy-start | bytes 772
  26.7 4.9 %copy-start.5 = (s32[2,4,8]{2,1,0:T(4,128)S(1)}, s32[2,4,8]{2,1,0:T(4,128)}, u32[]{:S(2)}) copy-start(s32[2,4,8]{2,1,0:T(4,128)} %param.8) | copy-start | bytes 772
  26.7 17.6 %collective-permute-start.1 = (f32[2,80,128]{2,1,0:T(8,128)S(1)}, f32[2,80,128]{2,1,0:T(8,128)S(1)}, u32[]{:S(2)}, u32[]{:S(2)}) collective-permute-start(f32[2,80,128]{2,1,0:T(8,128)S(1)} %get-tuple-element.6), channel_id=1, source_target_pairs={{0,960},{1,57},{2,962},{3,59},{4,964},{5,61},{6,966},{7,63},{8,968... | collective-permute-start | bytes 245768 | tf_op jit(solution)/shard_map/ppermute | solution.py:377
  31.8 1.0 %copy-start.4 = (f32[256,256]{1,0:T(8,128)S(1)}, f32[256,256]{1,0:T(8,128)}, u32[]{:S(2)}) copy-start(f32[256,256]{1,0:T(8,128)} %constant.36.clone.my_ref) | copy-start | bytes 786436

commit v2 on v1

--- a/solution.py
+++ b/solution.py
@@ -11,7 +11,6 @@
 AXES = ("gx", "gy", "gz")
 HEAT_RATIO = 1.4
 GRID_SCALE = 0.05
-PRECISE = lax.Precision.HIGHEST
 LOBATTO_POINTS = [
     -1.0,
     -0.8717401485096066,
@@ -36,7 +35,7 @@
 ROWS = 40
 
 
-def weak_tables():
+def weak_matrix():
     points = np.array(LOBATTO_POINTS)
     weights = np.array(LOBATTO_WEIGHTS)
     bary = np.array([1.0 / np.prod([points[i] - points[j] for j in range(8) if j != i]) for i in range(8)])
@@ -48,12 +47,7 @@
         derivative[i, i] = -np.sum(derivative[i])
     derivative[0, 0] += 1.0 / weights[0]
     derivative[7, 7] -= 1.0 / weights[0]
-    weak = -GRID_SCALE * derivative.T
-    eye = np.eye(8)
-    along_x = np.kron(weak, np.eye(64))
-    along_y = np.kron(np.eye(4), np.kron(weak, eye))
-    along_z = np.kron(np.eye(32), weak)
-    return [jnp.asarray(m, jnp.float32) for m in (along_x, along_y, along_z)]
+    return -GRID_SCALE * derivative
 
 
 def lanes_of(shape):
@@ -143,122 +137,143 @@
         out_ref[pl.ds(6 * ROWS + comp * 8, 8), :] = packed
 
 
-def inner_kernel(x_ref, blend_ref, mx_ref, my_ref, mz_ref, out_ref, flux_ref, speed_ref, gy_ref, gx_ref):
+def inner_kernel(x_ref, blend_ref, out_ref, u_ref, flux_ref, speed_ref, acc_ref):
+    weak, scale = weak_matrix(), [GRID_SCALE / w for w in LOBATTO_WEIGHTS]
     lane = lanes_of((8, 128))
-    sub = lax.broadcasted_iota(jnp.int32, (8, 128), 0)
-    k, j, half = lane % 8, (lane // 8) % 8, lane // 64
-    weights = [float(w) for w in LOBATTO_WEIGHTS]
-
-    def by_index(index, table):
-        value = jnp.full(index.shape, table[0], jnp.float32)
+    k = lax.broadcasted_iota(jnp.int32, (8, 128), 0)
+    upper, ex, ey, ez = lane >= 64, (lane // 32) % 2, (lane // 8) % 4, lane % 8
+    blend = blend_ref[...]
+    smooth, half_blend = 1.0 - blend, 0.5 * blend
+
+    def by_row(values):
+        value = jnp.full((8, 128), float(values[0]), jnp.float32)
         for n in range(1, 8):
-            value = jnp.where(index == n, table[n], value)
+            value = jnp.where(k == n, float(values[n]), value)
         return value
 
-    scale = [GRID_SCALE / w for w in weights]
-    scale_z, scale_y = by_index(k, scale), by_index(j, scale)
-    scale_x = [jnp.where(half == 0, scale[2 * c], scale[2 * c + 1]) for c in range(4)]
-
-    def tile(ref, row, c):
-        return ref[pl.ds(pl.multiple_of(row, 8), 8), c * 128 : (c + 1) * 128]
-
-    def put(ref, row, c, value):
-        ref[pl.ds(pl.multiple_of(row, 8), 8), c * 128 : (c + 1) * 128] = value
-
-    def fluxes(e, carry):
-        for c in range(4):
-            u = [tile(x_ref, e * ROWS + 8 * n, c) for n in range(5)]
-            rho, mom, energy = u[0], u[1:4], u[4]
-            inv = 1.0 / rho
-            vel = [m * inv for m in mom]
-            kinetic = 0.5 * (mom[0] * vel[0] + mom[1] * vel[1] + mom[2] * vel[2])
-            pressure = (HEAT_RATIO - 1.0) * (energy - kinetic)
-            sound = jnp.sqrt(HEAT_RATIO * pressure * inv)
-            total = energy + pressure
-            for d in range(3):
-                f = [mom[d]] + [mom[n] * vel[d] for n in range(3)] + [total * vel[d]]
-                f[1 + d] = f[1 + d] + pressure
-                for n in range(5):
-                    put(flux_ref.at[d], e * ROWS + 8 * n, c, f[n])
-                put(speed_ref.at[d], e * 8, c, jnp.abs(vel[d]) + sound)
+    def by_half(low, high):
+        return jnp.where(upper, float(high), float(low))
+
+    def rows(row):
+        return pl.ds(pl.multiple_of(row, 8), 8)
+
+    for n in range(5):
+        for h in range(2):
+            parts = [
+                x_ref[pl.ds(e * ROWS + 8 * n, 8), 256 * g + 128 * h : 256 * g + 128 * h + 128]
+                for g in range(2)
+                for e in range(8)
+            ]
+            u_ref[n, pl.ds(128 * h, 128), :] = jnp.concatenate(parts, axis=0).T
+
+    weak_z = [by_row([weak[r][(r + s) % 8] for r in range(8)]) for s in range(8)]
+    scale_z = by_row(scale)
+    weight_z = jnp.where(k == 7, 0.0, half_blend)
+
+    def first(t, carry):
+        at = rows(t * 8)
+        u = [u_ref[n, at, :] for n in range(5)]
+        rho, mom, energy = u[0], u[1:4], u[4]
+        inv = 1.0 / rho
+        vel = [m * inv for m in mom]
+        kinetic = 0.5 * (mom[0] * vel[0] + mom[1] * vel[1] + mom[2] * vel[2])
+        pressure = (HEAT_RATIO - 1.0) * (energy - kinetic)
+        sound = jnp.sqrt(HEAT_RATIO * pressure * inv)
+        total = energy + pressure
+        for d in range(3):
+            f = [mom[d]] + [mom[n] * vel[d] for n in range(3)] + [total * vel[d]]
+            f[1 + d] = f[1 + d] + pressure
+            speed = jnp.abs(vel[d]) + sound
+            speed_ref[d, at, :] = speed
+            for n in range(1, 5):
+                flux_ref[d, n - 1, at, :] = f[n]
+        largest = jnp.maximum(speed, pltpu.roll(speed, 7, 0))
+        for n in range(5):
+            turned = [f[n]] + [pltpu.roll(f[n], 8 - s, 0) for s in range(1, 8)]
+            volume = weak_z[0] * turned[0]
+            for s in range(1, 8):
+                volume = volume + weak_z[s] * turned[s]
+            g = weight_z * (f[n] + turned[1] - largest * (pltpu.roll(u[n], 7, 0) - u[n]))
+            acc_ref[n, at, :] = smooth * volume + scale_z * (pltpu.roll(g, 1, 0) - g)
         return carry
 
-    lax.fori_loop(0, 8, fluxes, 0)
-
-    def volume(r, carry):
-        rows = pl.ds(pl.multiple_of(r * 80, 8), 80)
-        total = jnp.dot(flux_ref[0, rows, :], mx_ref[...], precision=PRECISE, preferred_element_type=jnp.float32)
+    lax.fori_loop(0, 32, first, 0, unroll=2)
+
+    def flux(d, n, at):
+        return u_ref[1 + d, at, :] if n == 0 else flux_ref[d, n - 1, at, :]
+
+    def between(i, carry):
+        last, start = pl.ds(i * 64 + 7, 8, stride=8), pl.ds(i * 64, 8, stride=8)
+        weight = jnp.where(ez < 7, 0.5 * EDGE, 0.0)
+        largest = jnp.maximum(speed_ref[2, last, :], roll(speed_ref[2, start, :], -1))
+        for n in range(5):
+            jump = roll(u_ref[n, start, :], -1) - u_ref[n, last, :]
+            star = weight * (flux(2, n, last) + roll(flux(2, n, start), -1) - largest * jump)
+            acc_ref[n, last, :] = acc_ref[n, last, :] - star
+            acc_ref[n, start, :] = acc_ref[n, start, :] + roll(star, 1)
+        return carry
+
+    lax.fori_loop(0, 4, between, 0)
+
+    end_y = jnp.where(ey < 3, 0.5, 0.0)
+
+    def second(i, carry):
+        at = [rows(i * 64 + 8 * j) for j in range(8)]
+        speed = [speed_ref[1, a, :] for a in at]
+        largest = [jnp.maximum(speed[j], speed[j + 1]) for j in range(7)]
+        largest.append(jnp.maximum(speed[7], roll(speed[0], -8)))
+        for n in range(5):
+            u, f = [u_ref[n, a, :] for a in at], [flux(1, n, a) for a in at]
+            g = [half_blend * (f[j] + f[j + 1] - largest[j] * (u[j + 1] - u[j])) for j in range(7)]
+            g.append(end_y * (f[7] + roll(f[0], -8) - largest[7] * (roll(u[0], -8) - u[7])))
+            for j in range(8):
+                volume = float(weak[j][0]) * f[0]
+                for m in range(1, 8):
+                    volume = volume + float(weak[j][m]) * f[m]
+                low = g[j - 1] if j else roll(g[7], 8)
+                acc_ref[n, at[j], :] = acc_ref[n, at[j], :] + (smooth * volume + scale[j] * (low - g[j]))
+        return carry
+
+    lax.fori_loop(0, 4, second, 0)
+
+    weak_x = [[by_half(weak[r][m], weak[4 + r][4 + m]) for m in range(4)] for r in range(4)]
+    cross_x = [[by_half(weak[r][4 + m], weak[4 + r][m]) for m in range(4)] for r in range(4)]
+    scale_x = [by_half(scale[r], scale[4 + r]) for r in range(4)]
+    end_x = jnp.where(upper, jnp.where(ex == 0, 0.5, 0.0), half_blend)
+
+    def following(value, swapped):
+        return jnp.where(upper, roll(value, 32), swapped)
+
+    def third(j, carry):
+        at = [rows(i * 64 + 8 * j) for i in range(4)]
+        speed = [speed_ref[0, a, :] for a in at]
+        largest = [jnp.maximum(speed[i], speed[i + 1]) for i in range(3)]
+        largest.append(jnp.maximum(speed[3], following(speed[0], roll(speed[0], 64))))
+        for n in range(5):
+            u, f = [u_ref[n, a, :] for a in at], [flux(0, n, a) for a in at]
+            swapped = [roll(v, 64) for v in f]
+            g = [half_blend * (f[i] + f[i + 1] - largest[i] * (u[i + 1] - u[i])) for i in range(3)]
+            jump = following(u[0], roll(u[0], 64)) - u[3]
+            g.append(end_x * (f[3] + following(f[0], swapped[0]) - largest[3] * jump))
+            start = jnp.where(upper, roll(g[3], 64), jnp.where(ex == 1, roll(g[3], -32), 0.0))
+            for i in range(4):
+                volume = weak_x[i][0] * f[0] + cross_x[i][0] * swapped[0]
+                for m in range(1, 4):
+                    volume = volume + weak_x[i][m] * f[m] + cross_x[i][m] * swapped[m]
+                low = g[i - 1] if i else start
+                acc_ref[n, at[i], :] = acc_ref[n, at[i], :] + (smooth * volume + scale_x[i] * (low - g[i]))
+        return carry
+
+    lax.fori_loop(0, 8, third, 0)
+
+    for n in range(5):
         for h in range(2):
-            cols = slice(256 * h, 256 * h + 256)
-            part = jnp.dot(
-                flux_ref[1, rows, cols], my_ref[...], precision=PRECISE, preferred_element_type=jnp.float32
-            ) + jnp.dot(flux_ref[2, rows, cols], mz_ref[...], precision=PRECISE, preferred_element_type=jnp.float32)
-            out_ref[rows, cols] = total[:, cols] + part
-        return carry
-
-    lax.fori_loop(0, 4, volume, 0)
-
-    def subcells(e, carry):
-        ex, ey = e // 4, e % 4
-        blend = blend_ref[pl.ds(pl.multiple_of(e * 8, 8), 8), :]
-        up_y = jnp.minimum(e + 1, 7)
-        up_x = jnp.minimum(e + 4, 7)
-        has_up_y = jnp.where(ey < 3, 1.0, 0.0)
-        has_up_x = jnp.where(ex == 0, 1.0, 0.0)
-        low_y = jnp.maximum(e - 1, 0)
-        has_low_y, has_low_x = ey > 0, ex == 1
-        acc = {}
-
-        def gather(e_row, c, d):
-            u = [tile(x_ref, e_row * ROWS + 8 * n, c) for n in range(5)]
-            f = [u[1 + d]] + [tile(flux_ref.at[d], e_row * ROWS + 8 * n, c) for n in range(1, 5)]
-            return u + f[1:] + [tile(speed_ref.at[d], e_row * 8, c)]
-
-        def interface(own, other, d):
-            lu, ru = own[:5], other[:5]
-            lf, rf = [lu[1 + d]] + own[5:9], [ru[1 + d]] + other[5:9]
-            return upwind(lu, lf, own[9], ru, rf, other[9])
-
-        for c in range(4):
-            own = gather(e, c, 2)
-            other = [
-                jnp.where(k == 7, pltpu.roll(roll(v, 7), 7, 0), roll(v, -1)) for v in own
-            ]
-            weight = jnp.where(k == 7, jnp.where(sub < 7, 1.0, 0.0), blend)
-            for n, g in enumerate(interface(own, other, 2)):
-                g = g * weight
-                low = jnp.where(k == 0, pltpu.roll(roll(g, -7), 1, 0), roll(g, 1))
-                acc[n, c] = (low - g) * scale_z
-            own = gather(e, c, 1)
-            beyond = gather(up_y, c, 1)
-            other = [jnp.where(j == 7, roll(b, 56), roll(v, -8)) for v, b in zip(own, beyond)]
-            weight = jnp.where(j == 7, has_up_y, blend)
-            for n, g in enumerate(interface(own, other, 1)):
-                g = g * weight
-                below = jnp.where(has_low_y, tile(gy_ref, low_y * ROWS + 8 * n, c), 0.0)
-                low = jnp.where(j == 0, roll(below, -56), roll(g, 8))
-                put(gy_ref, e * ROWS + 8 * n, c, g)
-                acc[n, c] = acc[n, c] + (low - g) * scale_y
-        own = [gather(e, c, 0) for c in range(4)]
-        turned = [[roll(v, 64) for v in own[c]] for c in range(4)]
-        turned.append([roll(v, 64) for v in gather(up_x, 0, 0)])
-        before = [roll(jnp.where(has_low_x, tile(gx_ref, (e % 4) * ROWS + 8 * n, 0), 0.0), 64) for n in range(5)]
-        for c in range(4):
-            other = [jnp.where(half == 0, a, b) for a, b in zip(turned[c], turned[c + 1])]
-            weight = jnp.where(half == 1, has_up_x, blend) if c == 3 else blend
-            for n, g in enumerate(interface(own[c], other, 0)):
-                g = g * weight
-                if c == 3:
-                    put(gx_ref, (e % 4) * ROWS + 8 * n, 0, g)
-                moved = roll(g, 64)
-                low = jnp.where(half == 0, before[n], moved)
-                before[n] = moved
-                here = acc[n, c] + (low - g) * scale_x[c]
-                row = e * ROWS + 8 * n
-                put(out_ref, row, c, tile(out_ref, row, c) * (1.0 - blend) + here)
-        return carry
-
-    lax.fori_loop(0, 8, subcells, 0)
+            block = acc_ref[n, pl.ds(128 * h, 128), :].T
+            for g in range(2):
+                for e in range(8):
+                    out_ref[pl.ds(e * ROWS + 8 * n, 8), 256 * g + 128 * h : 256 * g + 128 * h + 128] = block[
+                        64 * g + 8 * e : 64 * g + 8 * e + 8, :
+                    ]
 
 
 def outer_kernel(place_ref, pre_ref, own_ref, halo_ref, near_ref, far_ref, out_ref):
@@ -382,18 +397,18 @@
     inner = pl.pallas_call(
         inner_kernel,
         out_shape=jax.ShapeDtypeStruct((8 * ROWS, 512), jnp.float32),
-        in_specs=[in_vmem()] * 5,
+        in_specs=[in_vmem()] * 2,
         out_specs=in_vmem(),
         scratch_shapes=[
-            pltpu.VMEM((3, 8 * ROWS, 512), jnp.float32),
-            pltpu.VMEM((3, 64, 512), jnp.float32),
-            pltpu.VMEM((8 * ROWS, 512), jnp.float32),
-            pltpu.VMEM((4 * ROWS, 128), jnp.float32),
+            pltpu.VMEM((5, 256, 128), jnp.float32),
+            pltpu.VMEM((3, 4, 256, 128), jnp.float32),
+            pltpu.VMEM((3, 256, 128), jnp.float32),
+            pltpu.VMEM((5, 256, 128), jnp.float32),
         ],
         compiler_params=LIMIT,
-        cost_estimate=pl.CostEstimate(flops=4_000_000_000, bytes_accessed=3_000_000, transcendentals=65536),
+        cost_estimate=pl.CostEstimate(flops=20_000_000, bytes_accessed=1_400_000, transcendentals=65536),
         name="inner",
-    )(state, jnp.broadcast_to(blend[:, None], (64, 128)), *weak_tables())
+    )(state, jnp.broadcast_to(jnp.concatenate([blend, blend])[None, :], (8, 128)))
 
     halo = lax.all_gather(jnp.stack(arrived), "gz", axis_index_groups=pairs(sizes[2], 0))
     place = jnp.stack([core, odd_x, odd_y]).astype(jnp.int32)

time: 51.2 us -> 42.8 us (0.84)
  Pallas kernels: 15.1 us -> 7.85 us
  local copies, waits for them, and re-layouts: 2.24 us -> 1.21 us
    pallas_call x1, Pallas kernels: 11.5 us -> 4.19 us  [on_device(): pl.pallas_call(inner_kernel, out_shape=jax.ShapeDtypeStruct((8 * ROWS, 51...]
    unnamed x14 -> x8, local copies, waits for them, and re-layouts: 2.06 us -> 1.11 us
  transfers between devices with their start and end apart: 3 -> 3, of which waited for: 0 -> 0; matrix products, arithmetic and copies ran while one was open for 1% -> 1% of each run, Pallas kernels for 23% -> 10%
where the time goes in v2:
time: 42.8 us; the launch traced here: 42.5 us
  starting transfers between devices  20.2 us (47%)
  blocking collectives  12.9 us (30%)
  Pallas kernels  7.85 us (18%)
  local copies, waits for them, and re-layouts  1.21 us (3%)
    ppermute x1, starting transfers between devices, on_device(): lax.ppermute(own[6 * ROWS:], 'gz', [(a, b) for a, b in swap] + [(b, a) fo...  12.2 us
    all_gather x1, blocking collectives, on_device(): both = lax.all_gather(own, 'gz', axis_index_groups=pairs(sizes[2], 0))  8.76 us
    ppermute x2, starting transfers between devices, on_device(): arrived.append(lax.ppermute(sent, AXES, crossed(sizes, shift)))  8.07 us
    pallas_call x1, Pallas kernels, on_device(): pl.pallas_call(inner_kernel, out_shape=jax.ShapeDtypeStruct((8 * ROWS, 51...  4.19 us
    all_gather x1, blocking collectives, on_device(): lax.all_gather(jnp.stack(arrived), 'gz', axis_index_groups=pairs(sizes[2]...  4.1 us
    pallas_call x1, Pallas kernels, on_device(): pl.pallas_call(outer_kernel, out_shape=jax.ShapeDtypeStruct((8 * ROWS, 51...  2.41 us
    pallas_call x1, Pallas kernels, on_device(): pl.pallas_call(faces_kernel, out_shape=jax.ShapeDtypeStruct((7 * ROWS, 12...  1.25 us
    unnamed x8, local copies, waits for them, and re-layouts  1.11 us
  transfers between devices with their start and end apart: 3, of which 0 were waited for; matrix products, arithmetic and copies ran while one was open for 1% of the time, Pallas kernels for 10%

profile of v2, /device:TPU:1, one launch (start us, length us, event | category | flops | bytes accessed | tf_op | source)
XLA Modules:
  0.0 42.5 jit_solution(11588193062704541200)
XLA Ops:
  0.0 0.0 copy-start
  0.0 1.1 %copy-done = f32[2,4,8,5,512]{4,2,3,1,0:T(8,128)S(1)} copy-done((f32[2,4,8,5,512]{4,2,3,1,0:T(8,128)S(1)}, f32[2,4,8,5,512]{4,2,3,1,0:T(8,128)}, u32[]{:S(2)}) %copy-start) | copy-done | bytes 655384
  1.1 1.2 %faces.1.own_ref = f32[280,128]{1,0:T(8,128)S(1)} custom-call(f32[320,512]{1,0:T(8,128)S(1)} %bitcast.22), custom_call_target="tpu_custom_call" | custom-call | tf_op jit(solution)/shard_map/faces/pallas_call | solution.py:375
  2.3 0.0 copy-start.1
  2.4 12.2 %collective-permute-start.2 = (f32[40,128]{1,0:T(8,128)S(1)}, f32[40,128]{1,0:T(8,128)S(1)}, u32[]{:S(2)}, u32[]{:S(2)}) collective-permute-start(f32[40,128]{1,0:T(8,128)S(1)} %slice.14), channel_id=1, source_target_pairs={{1,2},{3,4},{5,6},{7,0},{2,1},{4,3},{6,5},{0,7},{9,10},{11,12},{13... | collective-permute-start | bytes 61448 | tf_op jit(solution)/shard_map/ppermute | solution.py:394
  14.5 8.8 %all-gather = f32[560,128]{1,0:T(8,128)S(1)} all-gather(f32[280,128]{1,0:T(8,128)S(1)} %faces.1.own_ref), channel_id=2, replica_groups={{0,1},{2,3},{4,5},{6,7},{8,9},{10,11},{12,13},{14,15},{16,17},{18,19},{..., dimensions={0}, use_global_device_ids=true | all-gather | bytes 430080 | tf_op jit(solution)/shard_map/all_gather | solution.py:384
  23.3 3.2 %collective-permute-start = (f32[2,80,128]{2,1,0:T(8,128)S(1)}, f32[2,80,128]{2,1,0:T(8,128)S(1)}, u32[]{:S(2)}, u32[]{:S(2)}) collective-permute-start(f32[2,80,128]{2,1,0:T(8,128)S(1)} %get-tuple-element.5), channel_id=1, source_target_pairs={{0,64},{1,9},{2,66},{3,11},{4,68},{5,13},{6,70},{7,15},{8,72},{9,1... | collective-permute-start | bytes 245768 | tf_op jit(solution)/shard_map/ppermute | solution.py:392
  26.5 0.0 copy-start.3
  26.6 0.0 copy-start.2
  26.6 4.9 %collective-permute-start.1 = (f32[2,80,128]{2,1,0:T(8,128)S(1)}, f32[2,80,128]{2,1,0:T(8,128)S(1)}, u32[]{:S(2)}, u32[]{:S(2)}) collective-permute-start(f32[2,80,128]{2,1,0:T(8,128)S(1)} %get-tuple-element.6), channel_id=1, source_target_pairs={{0,960},{1,57},{2,962},{3,59},{4,964},{5,61},{6,966},{7,63},{8,968... | collective-permute-start | bytes 245768 | tf_op jit(solution)/shard_map/ppermute | solution.py:392
  31.5 0.0 copy-done.3
  31.5 0.0 copy-done.2
  31.5 0.1 div.10
  31.6 0.1 pad_maximum_fusion.1
  31.7 0.0 copy-done.1
  31.7 4.2 %inner.1.pre_ref = f32[320,512]{1,0:T(8,128)S(1)} custom-call(f32[320,512]{1,0:T(8,128)S(1)} %bitcast.23, f32[8,128]{1,0:T(8,128)S(1)} %broadcast_in_dim.2.blend_ref), custom_call_target="tpu_custom_call" | custom-call | flops 20000000 | bytes 1400000 | tf_op jit(solution)/shard_map/inner/pallas_call | solution.py:397
  35.9 0.1 pad_add_fusion.place_ref
  35.9 0.0 collective-permute-done
  35.9 0.0 collective-permute-done.1
  36.0 4.1 %all-gather.1 = f32[4,2,80,128]{3,2,1,0:T(8,128)S(1)} all-gather(f32[2,2,80,128]{3,2,1,0:T(8,128)S(1)} %pad_maximum_fusion), channel_id=3, replica_groups={{0,1},{2,3},{4,5},{6,7},{8,9},{10,11},{12,13},{14,15},{16,17},{18,19},{..., dimensions={0}, use_global_device_ids=true | all-gather | bytes 491520 | tf_op jit(solution)/shard_map/all_gather | solution.py:413
  40.1 0.0 collective-permute-done.2.far_ref
  40.1 2.4 %outer.1 = f32[320,512]{1,0:T(8,128)} custom-call(s32[3]{0:T(128)S(1)} %pad_add_fusion.place_ref, f32[320,512]{1,0:T(8,128)S(1)} %inner.1.pre_ref, f32[280,128]{1,0:T(8,128)S(1)} %faces.1.own_ref, f32[2,2,2,80,128]{4,3,2,1,0:T(8,128)S(1)} %bitcast.27, f32[2,280,128]{2,1,0:T(8,128)S(1)} %bitcast.26, f32[40,128]{1,0:T(8,128)S(1)} %collective-permute-done.2.far_ref), custom_call_target="tpu_custom_call" | custom-call | tf_op jit(solution)/shard_map/outer/pallas_call | solution.py:415
  (6 shorter events, 0.1 us)
Async XLA Ops:
  0.0 1.1 %copy-start = (f32[2,4,8,5,512]{4,2,3,1,0:T(8,128)S(1)}, f32[2,4,8,5,512]{4,2,3,1,0:T(8,128)}, u32[]{:S(2)}) copy-start(f32[2,4,8,5,512]{4,2,3,1,0:T(8,128)} %param.3) | copy-start | bytes 1966084
  2.3 29.3 %copy-start.1 = (f32[2,4,8,5,512]{4,2,3,1,0:T(8,128)S(1)}, f32[2,4,8,5,512]{4,2,3,1,0:T(8,128)}, u32[]{:S(2)}) copy-start(f32[2,4,8,5,512]{4,2,3,1,0:T(8,128)} %param.3) | copy-start | bytes 1966084
  2.4 37.7 %collective-permute-start.2 = (f32[40,128]{1,0:T(8,128)S(1)}, f32[40,128]{1,0:T(8,128)S(1)}, u32[]{:S(2)}, u32[]{:S(2)}) collective-permute-start(f32[40,128]{1,0:T(8,128)S(1)} %slice.14), channel_id=1, source_target_pairs={{1,2},{3,4},{5,6},{7,0},{2,1},{4,3},{6,5},{0,7},{9,10},{11,12},{13... | collective-permute-start | bytes 61448 | tf_op jit(solution)/shard_map/ppermute | solution.py:394
  23.3 12.6 %collective-permute-start = (f32[2,80,128]{2,1,0:T(8,128)S(1)}, f32[2,80,128]{2,1,0:T(8,128)S(1)}, u32[]{:S(2)}, u32[]{:S(2)}) collective-permute-start(f32[2,80,128]{2,1,0:T(8,128)S(1)} %get-tuple-element.5), channel_id=1, source_target_pairs={{0,64},{1,9},{2,66},{3,11},{4,68},{5,13},{6,70},{7,15},{8,72},{9,1... | collective-permute-start | bytes 245768 | tf_op jit(solution)/shard_map/ppermute | solution.py:392
  26.5 4.9 %copy-start.3 = (s32[2,4,8]{2,1,0:T(4,128)S(1)}, s32[2,4,8]{2,1,0:T(4,128)}, u32[]{:S(2)}) copy-start(s32[2,4,8]{2,1,0:T(4,128)} %param.4) | copy-start | bytes 772
  26.6 4.9 %copy-start.2 = (s32[2,4,8]{2,1,0:T(4,128)S(1)}, s32[2,4,8]{2,1,0:T(4,128)}, u32[]{:S(2)}) copy-start(s32[2,4,8]{2,1,0:T(4,128)} %param.5) | copy-start | bytes 772
  26.6 9.4 %collective-permute-start.1 = (f32[2,80,128]{2,1,0:T(8,128)S(1)}, f32[2,80,128]{2,1,0:T(8,128)S(1)}, u32[]{:S(2)}, u32[]{:S(2)}) collective-permute-start(f32[2,80,128]{2,1,0:T(8,128)S(1)} %get-tuple-element.6), channel_id=1, source_target_pairs={{0,960},{1,57},{2,962},{3,59},{4,964},{5,61},{6,966},{7,63},{8,968... | collective-permute-start | bytes 245768 | tf_op jit(solution)/shard_map/ppermute | solution.py:392

commit v3 on v2

--- a/solution.py
+++ b/solution.py
@@ -1,5 +1,3 @@
-import functools
-
 import jax
 import jax.numpy as jnp
 import numpy as np
@@ -80,46 +78,37 @@
     return upwind(left, *euler(left, d), right, *euler(right, d))
 
 
-def squeeze(tile, lane, first):
-    tile = roll(tile, -first)
-    for bit in range(4):
-        step = 1 << bit
-        moved = functools.reduce(
-            jnp.logical_or, [lane == 8 * m - 7 * (m % (2 * step)) for m in range(16) if m & step]
+def faces_kernel(x_hbm, out_ref, x_ref, arrived):
+    parts = ((3, 2), (0, 1), (7, 1), (1, 2), (5, 2))
+    copies = [
+        pltpu.make_async_copy(
+            x_hbm.at[pl.ds(e * ROWS, many * ROWS)], x_ref.at[pl.ds(e * ROWS, many * ROWS)], arrived.at[n]
         )
-        tile = jnp.where(moved, roll(tile, -7 * step), tile)
-    return tile
-
-
-def spread(tile, lane):
-    for bit in reversed(range(4)):
-        step = 1 << bit
-        moved = functools.reduce(
-            jnp.logical_or, [lane == 8 * m - 7 * (m % step) for m in range(16) if m & step]
-        )
-        tile = jnp.where(moved, roll(tile, 7 * step), tile)
-    return tile
-
-
-def faces_kernel(x_ref, out_ref):
-    lane3 = lanes_of((ROWS, 128))
+        for n, (e, many) in enumerate(parts)
+    ]
+    for copy in copies:
+        copy.start()
+    lane = lanes_of((ROWS, 128))
+    for copy in copies[:3]:
+        copy.wait()
+    for face, (ey, j) in enumerate(((0, 0), (3, 7))):
+        packed = None
+        for ex in range(2):
+            for chunk in range(4):
+                goal = 32 * ex + 8 * chunk
+                piece = x_ref[pl.ds((ex * 4 + ey) * ROWS, ROWS), chunk * 128 : (chunk + 1) * 128]
+                piece = roll(piece, goal - 8 * j)
+                packed = piece if packed is None else jnp.where(lane % 64 >= goal, piece, packed)
+        out_ref[pl.ds((4 + face) * ROWS, ROWS), :] = packed
+    for copy in copies[3:]:
+        copy.wait()
     for q in range(2):
         first = x_ref[pl.ds((2 * q) * ROWS, ROWS), 0:128]
         second = x_ref[pl.ds((2 * q + 1) * ROWS, ROWS), 0:128]
-        out_ref[pl.ds(q * ROWS, ROWS), :] = jnp.where(lane3 < 64, first, roll(second, 64))
+        out_ref[pl.ds(q * ROWS, ROWS), :] = jnp.where(lane < 64, first, roll(second, 64))
         first = x_ref[pl.ds((4 + 2 * q) * ROWS, ROWS), 384:512]
         second = x_ref[pl.ds((4 + 2 * q + 1) * ROWS, ROWS), 384:512]
-        out_ref[pl.ds((2 + q) * ROWS, ROWS), :] = jnp.where(lane3 < 64, roll(first, 64), second)
-    for face, (ey, j) in enumerate(((0, 0), (3, 7))):
-        packed = None
-        for ex in range(2):
-            for i in range(8):
-                chunk, half = i // 2, i % 2
-                goal = ex * 64 + i * 8
-                piece = x_ref[pl.ds((ex * 4 + ey) * ROWS, ROWS), chunk * 128 : (chunk + 1) * 128]
-                piece = roll(piece, goal - half * 64 - j * 8)
-                packed = piece if packed is None else jnp.where(lane3 >= goal, piece, packed)
-        out_ref[pl.ds((4 + face) * ROWS, ROWS), :] = packed
+        out_ref[pl.ds((2 + q) * ROWS, ROWS), :] = jnp.where(lane < 64, roll(first, 64), second)
     lane = lanes_of((8, 128))
     sub = lax.broadcasted_iota(jnp.int32, (8, 128), 0)
     for comp in range(5):
@@ -130,14 +119,14 @@
                 for e in range(8):
                     row = x_ref[pl.ds(e * ROWS + comp * 8 + ez, 1), chunk * 128 : (chunk + 1) * 128]
                     row = jnp.broadcast_to(row, (8, 128))
-                    piece = row if piece is None else jnp.where(sub >= e, row, piece)
-                piece = squeeze(piece, lane, k)
-                goal = face * 64 + chunk * 16
-                packed = piece if packed is None else jnp.where(lane >= goal, roll(piece, goal), packed)
+                    piece = row if piece is None else jnp.where(sub == e, row, piece)
+                goal = 4 * face + chunk
+                piece = roll(piece, goal - k)
+                packed = piece if packed is None else jnp.where(lane % 8 >= goal, piece, packed)
         out_ref[pl.ds(6 * ROWS + comp * 8, 8), :] = packed
 
 
-def inner_kernel(x_ref, blend_ref, out_ref, u_ref, flux_ref, speed_ref, acc_ref):
+def inner_kernel(x_ref, blend_ref, out_ref, u_ref, flux_ref, speed_ref, acc_ref, acc_x_ref):
     weak, scale = weak_matrix(), [GRID_SCALE / w for w in LOBATTO_WEIGHTS]
     lane = lanes_of((8, 128))
     k = lax.broadcasted_iota(jnp.int32, (8, 128), 0)
@@ -234,7 +223,6 @@
                 acc_ref[n, at[j], :] = acc_ref[n, at[j], :] + (smooth * volume + scale[j] * (low - g[j]))
         return carry
 
-    lax.fori_loop(0, 4, second, 0)
 
     weak_x = [[by_half(weak[r][m], weak[4 + r][4 + m]) for m in range(4)] for r in range(4)]
     cross_x = [[by_half(weak[r][4 + m], weak[4 + r][m]) for m in range(4)] for r in range(4)]
@@ -261,14 +249,21 @@
                 for m in range(1, 4):
                     volume = volume + weak_x[i][m] * f[m] + cross_x[i][m] * swapped[m]
                 low = g[i - 1] if i else start
-                acc_ref[n, at[i], :] = acc_ref[n, at[i], :] + (smooth * volume + scale_x[i] * (low - g[i]))
+                acc_x_ref[n, at[i], :] = smooth * volume + scale_x[i] * (low - g[i])
         return carry
 
-    lax.fori_loop(0, 8, third, 0)
+    def both(t, carry):
+        second(t, carry)
+        third(2 * t, carry)
+        third(2 * t + 1, carry)
+        return carry
+
+    lax.fori_loop(0, 4, both, 0)
 
     for n in range(5):
         for h in range(2):
-            block = acc_ref[n, pl.ds(128 * h, 128), :].T
+            at = pl.ds(128 * h, 128)
+            block = (acc_ref[n, at, :] + acc_x_ref[n, at, :]).T
             for g in range(2):
                 for e in range(8):
                     out_ref[pl.ds(e * ROWS + 8 * n, 8), 256 * g + 128 * h : 256 * g + 128 * h + 128] = block[
@@ -276,51 +271,16 @@
                     ]
 
 
-def outer_kernel(place_ref, pre_ref, own_ref, halo_ref, near_ref, far_ref, out_ref):
+def outer_kernel(place_ref, pre_ref, own_ref, halo_ref, near_ref, far_ref, out_hbm, out_ref, star_ref, left_sem):
     lane = lanes_of((8, 128))
-    left_half = lane < 64
+    sub = lax.broadcasted_iota(jnp.int32, (8, 128), 0)
+    left_half, low_face = lane < 64, lane % 8 < 4
     core, odd_x, odd_y = place_ref[0], place_ref[1], place_ref[2]
-    out_ref[...] = pre_ref[...]
+    zero = jnp.zeros((8, 128), jnp.float32)
 
     def own(tile):
         return own_ref[pl.ds(tile * 8, 8), :]
 
-    def add(row, c, value):
-        out_ref[pl.ds(row, 8), c * 128 : (c + 1) * 128] = (
-            out_ref[pl.ds(row, 8), c * 128 : (c + 1) * 128] + value
-        )
-
-    zero = jnp.zeros((8, 128), jnp.float32)
-    for q in range(2):
-        mine = [own(5 * q + n) for n in range(5)]
-        below = [halo_ref[0, 1 - odd_x, core, pl.ds((5 * q + n) * 8, 8), :] for n in range(5)]
-        for n, star in enumerate(rusanov(below, mine, 0)):
-            star = EDGE * star
-            add((2 * q) * ROWS + 8 * n, 0, jnp.where(left_half, star, zero))
-            add((2 * q + 1) * ROWS + 8 * n, 0, jnp.where(left_half, roll(star, 64), zero))
-        mine = [own(10 + 5 * q + n) for n in range(5)]
-        above = [halo_ref[0, odd_x, core, pl.ds((5 * q + n) * 8, 8), :] for n in range(5)]
-        for n, star in enumerate(rusanov(mine, above, 0)):
-            star = -EDGE * star
-            add((4 + 2 * q) * ROWS + 8 * n, 3, jnp.where(left_half, zero, roll(star, 64)))
-            add((4 + 2 * q + 1) * ROWS + 8 * n, 3, jnp.where(left_half, zero, star))
-    for face, (ey, j) in enumerate(((0, 0), (3, 7))):
-        mine = [own(20 + 5 * face + n) for n in range(5)]
-        if face == 0:
-            below = [halo_ref[1, 1 - odd_y, core, pl.ds((5 + n) * 8, 8), :] for n in range(5)]
-            stars = [EDGE * s for s in rusanov(below, mine, 1)]
-        else:
-            above = [halo_ref[1, odd_y, core, pl.ds(n * 8, 8), :] for n in range(5)]
-            stars = [-EDGE * s for s in rusanov(mine, above, 1)]
-        for n, star in enumerate(stars):
-            for ex in range(2):
-                for c in range(4):
-                    start = ex * 64 + 16 * c
-                    first = roll(star, j * 8 - start)
-                    second = roll(star, 64 + j * 8 - start - 8)
-                    value = jnp.where(left_half, first, second)
-                    value = jnp.where((lane // 8) % 8 == j, value, zero)
-                    add((ex * 4 + ey) * ROWS + 8 * n, c, value)
     first_core = core == 0
     mine = [own(30 + n) for n in range(5)]
     other = []
@@ -329,19 +289,62 @@
         far = far_ref[pl.ds(n * 8, 8), :]
         above = jnp.where(first_core, near, far)
         below = jnp.where(first_core, far, near)
-        other.append(roll(jnp.where(left_half, above, below), 64))
-    left = [jnp.where(left_half, o, m) for o, m in zip(other, mine)]
-    right = [jnp.where(left_half, m, o) for o, m in zip(other, mine)]
+        other.append(jnp.where(low_face, roll(below, -4), roll(above, 4)))
+    left = [jnp.where(low_face, o, m) for o, m in zip(other, mine)]
+    right = [jnp.where(low_face, m, o) for o, m in zip(other, mine)]
     for n, star in enumerate(rusanov(left, right, 2)):
-        for face, (ez, k) in enumerate(((0, 0), (7, 7))):
-            signed = (EDGE if face == 0 else -EDGE) * star
+        star = EDGE * star
+        for c in range(4):
+            cols = slice(c * 128, (c + 1) * 128)
+            star_ref[pl.ds(8 * n, 8), cols] = jnp.where(lane % 8 == 0, roll(star, -c), zero)
+            star_ref[pl.ds(ROWS + 8 * n, 8), cols] = jnp.where(lane % 8 == 7, -roll(star, 3 - c), zero)
+
+    along_x = {}
+    for q in range(2):
+        mine = [own(5 * q + n) for n in range(5)]
+        below = [halo_ref[0, 1 - odd_x, core, pl.ds((5 * q + n) * 8, 8), :] for n in range(5)]
+        for n, star in enumerate(rusanov(below, mine, 0)):
+            star = EDGE * star
+            along_x[2 * q, n] = jnp.where(left_half, star, zero)
+            along_x[2 * q + 1, n] = jnp.where(left_half, roll(star, 64), zero)
+        mine = [own(10 + 5 * q + n) for n in range(5)]
+        above = [halo_ref[0, odd_x, core, pl.ds((5 * q + n) * 8, 8), :] for n in range(5)]
+        for n, star in enumerate(rusanov(mine, above, 0)):
+            star = -EDGE * star
+            along_x[4 + 2 * q, n] = jnp.where(left_half, zero, roll(star, 64))
+            along_x[5 + 2 * q, n] = jnp.where(left_half, zero, star)
+
+    mine = [own(20 + n) for n in range(5)]
+    below = [halo_ref[1, 1 - odd_y, core, pl.ds((5 + n) * 8, 8), :] for n in range(5)]
+    low_y = [EDGE * s for s in rusanov(below, mine, 1)]
+    mine = [own(25 + n) for n in range(5)]
+    above = [halo_ref[1, odd_y, core, pl.ds(n * 8, 8), :] for n in range(5)]
+    high_y = [-EDGE * s for s in rusanov(mine, above, 1)]
+    row_j = (lane // 8) % 8
+
+    copies = []
+    for e in (1, 2, 5, 6, 0, 3, 4, 7):
+        ex, ey = e // 4, e % 4
+        for n in range(5):
             for c in range(4):
-                value = roll(spread(roll(signed, -(face * 64 + 16 * c)), lane), k)
-                value = jnp.where(lane % 8 == k, value, zero)
                 cols = slice(c * 128, (c + 1) * 128)
-                for e in range(8):
-                    row = pl.ds(e * ROWS + n * 8 + ez, 1)
-                    out_ref[row, cols] = out_ref[row, cols] + value[e : e + 1, :]
+                value = pre_ref[pl.ds(e * ROWS + 8 * n, 8), cols]
+                low = jnp.broadcast_to(star_ref[pl.ds(8 * n + e, 1), cols], (8, 128))
+                high = jnp.broadcast_to(star_ref[pl.ds(ROWS + 8 * n + e, 1), cols], (8, 128))
+                value = value + jnp.where(sub == 0, low, jnp.where(sub == 7, high, zero))
+                if c == (0, 3)[ex]:
+                    value = value + along_x[e, n]
+                start = 32 * ex + 8 * c
+                if ey == 0:
+                    value = value + jnp.where(row_j == 0, roll(low_y[n], -start), zero)
+                if ey == 3:
+                    value = value + jnp.where(row_j == 7, roll(high_y[n], 56 - start), zero)
+                out_ref[pl.ds(e * ROWS + 8 * n, 8), cols] = value
+        at = pl.ds(e * ROWS, ROWS)
+        copies.append(pltpu.make_async_copy(out_ref.at[at], out_hbm.at[at], left_sem.at[e]))
+        copies[-1].start()
+    for copy in copies:
+        copy.wait()
 
 
 def pairs(size, shift):
@@ -363,6 +366,10 @@
     return pl.BlockSpec(memory_space=pltpu.VMEM)
 
 
+def in_hbm():
+    return pl.BlockSpec(memory_space=pl.ANY)
+
+
 LIMIT = pltpu.CompilerParams(vmem_limit_bytes=32 * 1024 * 1024)
 
 
@@ -375,8 +382,9 @@
     own = pl.pallas_call(
         faces_kernel,
         out_shape=jax.ShapeDtypeStruct((7 * ROWS, 128), jnp.float32),
-        in_specs=[in_vmem()],
+        in_specs=[in_hbm()],
         out_specs=in_vmem(),
+        scratch_shapes=[pltpu.VMEM((8 * ROWS, 512), jnp.float32), pltpu.SemaphoreType.DMA((5,))],
         compiler_params=LIMIT,
         name="faces",
     )(state)
@@ -404,6 +412,7 @@
             pltpu.VMEM((3, 4, 256, 128), jnp.float32),
             pltpu.VMEM((3, 256, 128), jnp.float32),
             pltpu.VMEM((5, 256, 128), jnp.float32),
+            pltpu.VMEM((5, 256, 128), jnp.float32),
         ],
         compiler_params=LIMIT,
         cost_estimate=pl.CostEstimate(flops=20_000_000, bytes_accessed=1_400_000, transcendentals=65536),
@@ -416,7 +425,12 @@
         outer_kernel,
         out_shape=jax.ShapeDtypeStruct((8 * ROWS, 512), jnp.float32),
         in_specs=[pl.BlockSpec(memory_space=pltpu.SMEM)] + [in_vmem()] * 5,
-        out_specs=in_vmem(),
+        out_specs=in_hbm(),
+        scratch_shapes=[
+            pltpu.VMEM((8 * ROWS, 512), jnp.float32),
+            pltpu.VMEM((2 * ROWS, 512), jnp.float32),
+            pltpu.SemaphoreType.DMA((8,)),
+        ],
         compiler_params=LIMIT,
         name="outer",
     )(place, inner, own, halo, both, far)

time: 42.8 us -> 41.1 us (0.960)
  Pallas kernels: 7.85 us -> 6.2 us
    pallas_call x1, Pallas kernels: 4.19 us -> 3.32 us  [on_device(): pl.pallas_call(inner_kernel, out_shape=jax.ShapeDtypeStruct((8 * ROWS, 51...]
    pallas_call x1, Pallas kernels: 2.41 us -> 1.75 us  [on_device(): pl.pallas_call(outer_kernel, out_shape=jax.ShapeDtypeStruct((8 * ROWS, 51...]
  transfers between devices with their start and end apart: 3 -> 3, of which waited for: 0 -> 0; matrix products, arithmetic and copies ran while one was open for 1% -> 1% of each run, Pallas kernels for 10% -> 8%
where the time goes in v3:
time: 41.1 us; the launch traced here: 40.8 us
  starting transfers between devices  20.2 us (49%)
  blocking collectives  12.9 us (31%)
  Pallas kernels  6.2 us (15%)
  local copies, waits for them, and re-layouts  1.21 us (3%)
    ppermute x1, starting transfers between devices, on_device(): lax.ppermute(own[6 * ROWS:], 'gz', [(a, b) for a, b in swap] + [(b, a) fo...  12.2 us
    all_gather x1, blocking collectives, on_device(): both = lax.all_gather(own, 'gz', axis_index_groups=pairs(sizes[2], 0))  8.76 us
    ppermute x2, starting transfers between devices, on_device(): arrived.append(lax.ppermute(sent, AXES, crossed(sizes, shift)))  8.07 us
    all_gather x1, blocking collectives, on_device(): lax.all_gather(jnp.stack(arrived), 'gz', axis_index_groups=pairs(sizes[2]...  4.1 us
    pallas_call x1, Pallas kernels, on_device(): pl.pallas_call(inner_kernel, out_shape=jax.ShapeDtypeStruct((8 * ROWS, 51...  3.32 us
    pallas_call x1, Pallas kernels, on_device(): pl.pallas_call(outer_kernel, out_shape=jax.ShapeDtypeStruct((8 * ROWS, 51...  1.75 us
    pallas_call x1, Pallas kernels, on_device(): pl.pallas_call(faces_kernel, out_shape=jax.ShapeDtypeStruct((7 * ROWS, 12...  1.13 us
    unnamed x8, local copies, waits for them, and re-layouts  1.11 us
  transfers between devices with their start and end apart: 3, of which 0 were waited for; matrix products, arithmetic and copies ran while one was open for 1% of the time, Pallas kernels for 8%

profile of v3, /device:TPU:1, one launch (start us, length us, event | category | flops | bytes accessed | tf_op | source)
XLA Modules:
  0.0 40.8 jit_solution(16590039843558595919)
XLA Ops:
  0.0 0.0 copy-start
  0.0 1.1 %copy-done = f32[2,4,8,5,512]{4,2,3,1,0:T(8,128)S(1)} copy-done((f32[2,4,8,5,512]{4,2,3,1,0:T(8,128)S(1)}, f32[2,4,8,5,512]{4,2,3,1,0:T(8,128)}, u32[]{:S(2)}) %copy-start) | copy-done | bytes 655384
  1.1 1.1 %faces.1.own_ref = f32[280,128]{1,0:T(8,128)S(1)} custom-call(f32[320,512]{1,0:T(8,128)S(1)} %bitcast.22), custom_call_target="tpu_custom_call" | custom-call | tf_op jit(solution)/shard_map/faces/pallas_call | solution.py:382
  2.2 0.0 copy-start.1
  2.3 12.2 %collective-permute-start.2 = (f32[40,128]{1,0:T(8,128)S(1)}, f32[40,128]{1,0:T(8,128)S(1)}, u32[]{:S(2)}, u32[]{:S(2)}) collective-permute-start(f32[40,128]{1,0:T(8,128)S(1)} %slice.14), channel_id=1, source_target_pairs={{1,2},{3,4},{5,6},{7,0},{2,1},{4,3},{6,5},{0,7},{9,10},{11,12},{13... | collective-permute-start | bytes 61448 | tf_op jit(solution)/shard_map/ppermute | solution.py:402
  14.4 8.8 %all-gather = f32[560,128]{1,0:T(8,128)S(1)} all-gather(f32[280,128]{1,0:T(8,128)S(1)} %faces.1.own_ref), channel_id=2, replica_groups={{0,1},{2,3},{4,5},{6,7},{8,9},{10,11},{12,13},{14,15},{16,17},{18,19},{..., dimensions={0}, use_global_device_ids=true | all-gather | bytes 430080 | tf_op jit(solution)/shard_map/all_gather | solution.py:392
  23.2 3.2 %collective-permute-start = (f32[2,80,128]{2,1,0:T(8,128)S(1)}, f32[2,80,128]{2,1,0:T(8,128)S(1)}, u32[]{:S(2)}, u32[]{:S(2)}) collective-permute-start(f32[2,80,128]{2,1,0:T(8,128)S(1)} %get-tuple-element.5), channel_id=1, source_target_pairs={{0,64},{1,9},{2,66},{3,11},{4,68},{5,13},{6,70},{7,15},{8,72},{9,1... | collective-permute-start | bytes 245768 | tf_op jit(solution)/shard_map/ppermute | solution.py:400
  26.4 0.0 copy-start.3
  26.5 0.0 copy-start.2
  26.5 4.9 %collective-permute-start.1 = (f32[2,80,128]{2,1,0:T(8,128)S(1)}, f32[2,80,128]{2,1,0:T(8,128)S(1)}, u32[]{:S(2)}, u32[]{:S(2)}) collective-permute-start(f32[2,80,128]{2,1,0:T(8,128)S(1)} %get-tuple-element.6), channel_id=1, source_target_pairs={{0,960},{1,57},{2,962},{3,59},{4,964},{5,61},{6,966},{7,63},{8,968... | collective-permute-start | bytes 245768 | tf_op jit(solution)/shard_map/ppermute | solution.py:400
  31.3 0.0 copy-done.3
  31.4 0.0 copy-done.2
  31.4 0.1 div.10
  31.5 0.1 pad_maximum_fusion.1
  31.5 0.0 copy-done.1
  31.6 3.3 %inner.1.pre_ref = f32[320,512]{1,0:T(8,128)S(1)} custom-call(f32[320,512]{1,0:T(8,128)S(1)} %bitcast.23, f32[8,128]{1,0:T(8,128)S(1)} %broadcast_in_dim.2.blend_ref), custom_call_target="tpu_custom_call" | custom-call | flops 20000000 | bytes 1400000 | tf_op jit(solution)/shard_map/inner/pallas_call | solution.py:405
  34.9 0.1 pad_add_fusion.place_ref
  35.0 0.0 collective-permute-done
  35.0 0.0 collective-permute-done.1
  35.0 4.1 %all-gather.1 = f32[4,2,80,128]{3,2,1,0:T(8,128)S(1)} all-gather(f32[2,2,80,128]{3,2,1,0:T(8,128)S(1)} %pad_maximum_fusion), channel_id=3, replica_groups={{0,1},{2,3},{4,5},{6,7},{8,9},{10,11},{12,13},{14,15},{16,17},{18,19},{..., dimensions={0}, use_global_device_ids=true | all-gather | bytes 491520 | tf_op jit(solution)/shard_map/all_gather | solution.py:422
  39.1 0.0 collective-permute-done.2.far_ref
  39.1 1.7 %outer.1 = f32[320,512]{1,0:T(8,128)} custom-call(s32[3]{0:T(128)S(1)} %pad_add_fusion.place_ref, f32[320,512]{1,0:T(8,128)S(1)} %inner.1.pre_ref, f32[280,128]{1,0:T(8,128)S(1)} %faces.1.own_ref, f32[2,2,2,80,128]{4,3,2,1,0:T(8,128)S(1)} %bitcast.27, f32[2,280,128]{2,1,0:T(8,128)S(1)} %bitcast.26, f32[40,128]{1,0:T(8,128)S(1)} %collective-permute-done.2.far_ref), custom_call_target="tpu_custom_call" | custom-call | tf_op jit(solution)/shard_map/outer/pallas_call | solution.py:424
  (6 shorter events, 0.1 us)
Async XLA Ops:
  0.0 1.1 %copy-start = (f32[2,4,8,5,512]{4,2,3,1,0:T(8,128)S(1)}, f32[2,4,8,5,512]{4,2,3,1,0:T(8,128)}, u32[]{:S(2)}) copy-start(f32[2,4,8,5,512]{4,2,3,1,0:T(8,128)} %param.3) | copy-start | bytes 1966084
  2.2 29.3 %copy-start.1 = (f32[2,4,8,5,512]{4,2,3,1,0:T(8,128)S(1)}, f32[2,4,8,5,512]{4,2,3,1,0:T(8,128)}, u32[]{:S(2)}) copy-start(f32[2,4,8,5,512]{4,2,3,1,0:T(8,128)} %param.3) | copy-start | bytes 1966084
  2.3 36.8 %collective-permute-start.2 = (f32[40,128]{1,0:T(8,128)S(1)}, f32[40,128]{1,0:T(8,128)S(1)}, u32[]{:S(2)}, u32[]{:S(2)}) collective-permute-start(f32[40,128]{1,0:T(8,128)S(1)} %slice.14), channel_id=1, source_target_pairs={{1,2},{3,4},{5,6},{7,0},{2,1},{4,3},{6,5},{0,7},{9,10},{11,12},{13... | collective-permute-start | bytes 61448 | tf_op jit(solution)/shard_map/ppermute | solution.py:402
  23.2 11.7 %collective-permute-start = (f32[2,80,128]{2,1,0:T(8,128)S(1)}, f32[2,80,128]{2,1,0:T(8,128)S(1)}, u32[]{:S(2)}, u32[]{:S(2)}) collective-permute-start(f32[2,80,128]{2,1,0:T(8,128)S(1)} %get-tuple-element.5), channel_id=1, source_target_pairs={{0,64},{1,9},{2,66},{3,11},{4,68},{5,13},{6,70},{7,15},{8,72},{9,1... | collective-permute-start | bytes 245768 | tf_op jit(solution)/shard_map/ppermute | solution.py:400
  26.4 4.9 %copy-start.3 = (s32[2,4,8]{2,1,0:T(4,128)S(1)}, s32[2,4,8]{2,1,0:T(4,128)}, u32[]{:S(2)}) copy-start(s32[2,4,8]{2,1,0:T(4,128)} %param.4) | copy-start | bytes 772
  26.5 4.9 %copy-start.2 = (s32[2,4,8]{2,1,0:T(4,128)S(1)}, s32[2,4,8]{2,1,0:T(4,128)}, u32[]{:S(2)}) copy-start(s32[2,4,8]{2,1,0:T(4,128)} %param.5) | copy-start | bytes 772
  26.5 8.5 %collective-permute-start.1 = (f32[2,80,128]{2,1,0:T(8,128)S(1)}, f32[2,80,128]{2,1,0:T(8,128)S(1)}, u32[]{:S(2)}, u32[]{:S(2)}) collective-permute-start(f32[2,80,128]{2,1,0:T(8,128)S(1)} %get-tuple-element.6), channel_id=1, source_target_pairs={{0,960},{1,57},{2,962},{3,59},{4,964},{5,61},{6,966},{7,63},{8,968... | collective-permute-start | bytes 245768 | tf_op jit(solution)/shard_map/ppermute | solution.py:400

commit v4 on v3

--- a/solution.py
+++ b/solution.py
@@ -302,23 +302,23 @@
     along_x = {}
     for q in range(2):
         mine = [own(5 * q + n) for n in range(5)]
-        below = [halo_ref[0, 1 - odd_x, core, pl.ds((5 * q + n) * 8, 8), :] for n in range(5)]
+        below = [halo_ref[0, odd_x, core, pl.ds((5 * q + n) * 8, 8), :] for n in range(5)]
         for n, star in enumerate(rusanov(below, mine, 0)):
             star = EDGE * star
             along_x[2 * q, n] = jnp.where(left_half, star, zero)
             along_x[2 * q + 1, n] = jnp.where(left_half, roll(star, 64), zero)
         mine = [own(10 + 5 * q + n) for n in range(5)]
-        above = [halo_ref[0, odd_x, core, pl.ds((5 * q + n) * 8, 8), :] for n in range(5)]
+        above = [halo_ref[0, 1 - odd_x, core, pl.ds((5 * q + n) * 8, 8), :] for n in range(5)]
         for n, star in enumerate(rusanov(mine, above, 0)):
             star = -EDGE * star
             along_x[4 + 2 * q, n] = jnp.where(left_half, zero, roll(star, 64))
             along_x[5 + 2 * q, n] = jnp.where(left_half, zero, star)
 
     mine = [own(20 + n) for n in range(5)]
-    below = [halo_ref[1, 1 - odd_y, core, pl.ds((5 + n) * 8, 8), :] for n in range(5)]
+    below = [halo_ref[1, odd_y, core, pl.ds((5 + n) * 8, 8), :] for n in range(5)]
     low_y = [EDGE * s for s in rusanov(below, mine, 1)]
     mine = [own(25 + n) for n in range(5)]
-    above = [halo_ref[1, odd_y, core, pl.ds(n * 8, 8), :] for n in range(5)]
+    above = [halo_ref[1, 1 - odd_y, core, pl.ds(n * 8, 8), :] for n in range(5)]
     high_y = [-EDGE * s for s in rusanov(mine, above, 1)]
     row_j = (lane // 8) % 8
 
@@ -367,7 +367,7 @@
 
 
 def in_hbm():
-    return pl.BlockSpec(memory_space=pl.ANY)
+    return pl.BlockSpec(memory_space=pltpu.HBM)
 
 
 LIMIT = pltpu.CompilerParams(vmem_limit_bytes=32 * 1024 * 1024)
@@ -387,17 +387,17 @@
         scratch_shapes=[pltpu.VMEM((8 * ROWS, 512), jnp.float32), pltpu.SemaphoreType.DMA((5,))],
         compiler_params=LIMIT,
         name="faces",
-    )(state)
+    )(pltpu.with_memory_space_constraint(state, pltpu.HBM))
 
     both = lax.all_gather(own, "gz", axis_index_groups=pairs(sizes[2], 0))
     x_faces = both[:, : 4 * ROWS].reshape(2, 2, 2 * ROWS, 128)
     y_faces = both[:, 4 * ROWS : 6 * ROWS]
-    arrived = []
-    for shift in range(2):
+    arrived = {}
+    for shift in (1, 0):
         face = odd_x if shift else 1 - odd_x
         x_part = lax.dynamic_index_in_dim(x_faces, face, 1, keepdims=False)
         sent = jnp.where(core == 0, x_part, y_faces)
-        arrived.append(lax.ppermute(sent, AXES, crossed(sizes, shift)))
+        arrived[shift] = lax.ppermute(sent, AXES, crossed(sizes, shift))
     swap = pairs(sizes[2], 1)
     far = lax.ppermute(own[6 * ROWS :], "gz", [(a, b) for a, b in swap] + [(b, a) for a, b in swap])
 
@@ -419,7 +419,7 @@
         name="inner",
     )(state, jnp.broadcast_to(jnp.concatenate([blend, blend])[None, :], (8, 128)))
 
-    halo = lax.all_gather(jnp.stack(arrived), "gz", axis_index_groups=pairs(sizes[2], 0))
+    halo = lax.all_gather(jnp.stack([arrived[1], arrived[0]]), "gz", axis_index_groups=pairs(sizes[2], 0))
     place = jnp.stack([core, odd_x, odd_y]).astype(jnp.int32)
     full = pl.pallas_call(
         outer_kernel,

time: 41.1 us -> 40.2 us (0.978)
  local copies, waits for them, and re-layouts: 1.21 us -> 0.12 us
  blocking collectives: 12.9 us -> 13.9 us
  starting transfers between devices: 20.2 us -> 19.2 us
    unnamed x8 -> x6, local copies, waits for them, and re-layouts: 1.11 us -> 0.02 us
    ppermute x2, starting transfers between devices: 8.07 us -> 7.02 us  [on_device(): arrived[shift] = lax.ppermute(sent, AXES, crossed(sizes, shift))]
    all_gather x1, blocking collectives: 4.1 us -> 5.11 us  [on_device(): lax.all_gather(jnp.stack([arrived[1], arrived[0]]), 'gz', axis_index_grou...]
where the time goes in v4:
time: 40.2 us; the launch traced here: 39.9 us
  starting transfers between devices  19.2 us (48%)
  blocking collectives  13.9 us (35%)
  Pallas kernels  6.39 us (16%)
    ppermute x1, starting transfers between devices, on_device(): lax.ppermute(own[6 * ROWS:], 'gz', [(a, b) for a, b in swap] + [(b, a) fo...  12.2 us
    all_gather x1, blocking collectives, on_device(): both = lax.all_gather(own, 'gz', axis_index_groups=pairs(sizes[2], 0))  8.76 us
    ppermute x2, starting transfers between devices, on_device(): arrived[shift] = lax.ppermute(sent, AXES, crossed(sizes, shift))  7.02 us
    all_gather x1, blocking collectives, on_device(): lax.all_gather(jnp.stack([arrived[1], arrived[0]]), 'gz', axis_index_grou...  5.11 us
    pallas_call x1, Pallas kernels, on_device(): pl.pallas_call(inner_kernel, out_shape=jax.ShapeDtypeStruct((8 * ROWS, 51...  3.32 us
    pallas_call x1, Pallas kernels, on_device(): pl.pallas_call(outer_kernel, out_shape=jax.ShapeDtypeStruct((8 * ROWS, 51...  1.75 us
    pallas_call x1, Pallas kernels, on_device(): pl.pallas_call(faces_kernel, out_shape=jax.ShapeDtypeStruct((7 * ROWS, 12...  1.32 us
  transfers between devices with their start and end apart: 3, of which 0 were waited for; matrix products, arithmetic and copies ran while one was open for 1% of the time, Pallas kernels for 8%

profile of v4, /device:TPU:1, one launch (start us, length us, event | category | flops | bytes accessed | tf_op | source)
XLA Modules:
  0.0 39.9 jit_solution(2361256538310303687)
XLA Ops:
  0.0 1.3 %faces.1.own_ref = f32[280,128]{1,0:T(8,128)S(1)} custom-call(f32[320,512]{1,0:T(8,128)} %bitcast.22), custom_call_target="tpu_custom_call" | custom-call | tf_op jit(solution)/shard_map/faces/pallas_call | solution.py:382
  1.3 0.0 copy-start
  1.4 12.2 %collective-permute-start.2 = (f32[40,128]{1,0:T(8,128)S(1)}, f32[40,128]{1,0:T(8,128)S(1)}, u32[]{:S(2)}, u32[]{:S(2)}) collective-permute-start(f32[40,128]{1,0:T(8,128)S(1)} %slice.14), channel_id=1, source_target_pairs={{1,2},{3,4},{5,6},{7,0},{2,1},{4,3},{6,5},{0,7},{9,10},{11,12},{13... | collective-permute-start | bytes 61448 | tf_op jit(solution)/shard_map/ppermute | solution.py:402
  13.5 8.8 %all-gather = f32[560,128]{1,0:T(8,128)S(1)} all-gather(f32[280,128]{1,0:T(8,128)S(1)} %faces.1.own_ref), channel_id=2, replica_groups={{0,1},{2,3},{4,5},{6,7},{8,9},{10,11},{12,13},{14,15},{16,17},{18,19},{..., dimensions={0}, use_global_device_ids=true | all-gather | bytes 430080 | tf_op jit(solution)/shard_map/all_gather | solution.py:392
  22.3 5.1 %collective-permute-start = (f32[2,80,128]{2,1,0:T(8,128)S(1)}, f32[2,80,128]{2,1,0:T(8,128)S(1)}, u32[]{:S(2)}, u32[]{:S(2)}) collective-permute-start(f32[2,80,128]{2,1,0:T(8,128)S(1)} %get-tuple-element.5), channel_id=1, source_target_pairs={{0,960},{1,57},{2,962},{3,59},{4,964},{5,61},{6,966},{7,63},{8,968... | collective-permute-start | bytes 245768 | tf_op jit(solution)/shard_map/ppermute | solution.py:400
  27.4 0.0 copy-start.2
  27.4 0.0 copy-start.1
  27.5 1.9 %collective-permute-start.1 = (f32[2,80,128]{2,1,0:T(8,128)S(1)}, f32[2,80,128]{2,1,0:T(8,128)S(1)}, u32[]{:S(2)}, u32[]{:S(2)}) collective-permute-start(f32[2,80,128]{2,1,0:T(8,128)S(1)} %get-tuple-element.6), channel_id=1, source_target_pairs={{0,64},{1,9},{2,66},{3,11},{4,68},{5,13},{6,70},{7,15},{8,72},{9,1... | collective-permute-start | bytes 245768 | tf_op jit(solution)/shard_map/ppermute | solution.py:400
  29.4 0.0 copy-done.2
  29.4 0.0 copy-done.1
  29.4 0.1 div.10
  29.5 0.1 pad_maximum_fusion.1
  29.6 0.0 copy-done
  29.6 3.3 %inner.1.pre_ref = f32[320,512]{1,0:T(8,128)S(1)} custom-call(f32[320,512]{1,0:T(8,128)S(1)} %bitcast.23, f32[8,128]{1,0:T(8,128)S(1)} %broadcast_in_dim.2.blend_ref), custom_call_target="tpu_custom_call" | custom-call | flops 20000000 | bytes 1400000 | tf_op jit(solution)/shard_map/inner/pallas_call | solution.py:405
  32.9 0.1 pad_add_fusion.place_ref
  33.0 0.0 collective-permute-done
  33.0 0.0 collective-permute-done.1
  33.0 5.1 %all-gather.1 = f32[4,2,80,128]{3,2,1,0:T(8,128)S(1)} all-gather(f32[2,2,80,128]{3,2,1,0:T(8,128)S(1)} %pad_maximum_fusion), channel_id=3, replica_groups={{0,1},{2,3},{4,5},{6,7},{8,9},{10,11},{12,13},{14,15},{16,17},{18,19},{..., dimensions={0}, use_global_device_ids=true | all-gather | bytes 491520 | tf_op jit(solution)/shard_map/all_gather | solution.py:422
  38.1 0.0 collective-permute-done.2.far_ref
  38.2 1.7 %outer.1 = f32[320,512]{1,0:T(8,128)} custom-call(s32[3]{0:T(128)S(1)} %pad_add_fusion.place_ref, f32[320,512]{1,0:T(8,128)S(1)} %inner.1.pre_ref, f32[280,128]{1,0:T(8,128)S(1)} %faces.1.own_ref, f32[2,2,2,80,128]{4,3,2,1,0:T(8,128)S(1)} %bitcast.27, f32[2,280,128]{2,1,0:T(8,128)S(1)} %bitcast.26, f32[40,128]{1,0:T(8,128)S(1)} %collective-permute-done.2.far_ref), custom_call_target="tpu_custom_call" | custom-call | tf_op jit(solution)/shard_map/outer/pallas_call | solution.py:424
  (6 shorter events, 0.1 us)
Async XLA Ops:
  1.3 28.3 %copy-start = (f32[2,4,8,5,512]{4,2,3,1,0:T(8,128)S(1)}, f32[2,4,8,5,512]{4,2,3,1,0:T(8,128)}, u32[]{:S(2)}) copy-start(f32[2,4,8,5,512]{4,2,3,1,0:T(8,128)} %param.3) | copy-start | bytes 1966084
  1.4 36.8 %collective-permute-start.2 = (f32[40,128]{1,0:T(8,128)S(1)}, f32[40,128]{1,0:T(8,128)S(1)}, u32[]{:S(2)}, u32[]{:S(2)}) collective-permute-start(f32[40,128]{1,0:T(8,128)S(1)} %slice.14), channel_id=1, source_target_pairs={{1,2},{3,4},{5,6},{7,0},{2,1},{4,3},{6,5},{0,7},{9,10},{11,12},{13... | collective-permute-start | bytes 61448 | tf_op jit(solution)/shard_map/ppermute | solution.py:402
  22.3 10.7 %collective-permute-start = (f32[2,80,128]{2,1,0:T(8,128)S(1)}, f32[2,80,128]{2,1,0:T(8,128)S(1)}, u32[]{:S(2)}, u32[]{:S(2)}) collective-permute-start(f32[2,80,128]{2,1,0:T(8,128)S(1)} %get-tuple-element.5), channel_id=1, source_target_pairs={{0,960},{1,57},{2,962},{3,59},{4,964},{5,61},{6,966},{7,63},{8,968... | collective-permute-start | bytes 245768 | tf_op jit(solution)/shard_map/ppermute | solution.py:400
  27.4 2.0 %copy-start.2 = (s32[2,4,8]{2,1,0:T(4,128)S(1)}, s32[2,4,8]{2,1,0:T(4,128)}, u32[]{:S(2)}) copy-start(s32[2,4,8]{2,1,0:T(4,128)} %param.4) | copy-start | bytes 772
  27.4 2.0 %copy-start.1 = (s32[2,4,8]{2,1,0:T(4,128)S(1)}, s32[2,4,8]{2,1,0:T(4,128)}, u32[]{:S(2)}) copy-start(s32[2,4,8]{2,1,0:T(4,128)} %param.5) | copy-start | bytes 772
  27.5 5.6 %collective-permute-start.1 = (f32[2,80,128]{2,1,0:T(8,128)S(1)}, f32[2,80,128]{2,1,0:T(8,128)S(1)}, u32[]{:S(2)}, u32[]{:S(2)}) collective-permute-start(f32[2,80,128]{2,1,0:T(8,128)S(1)} %get-tuple-element.6), channel_id=1, source_target_pairs={{0,64},{1,9},{2,66},{3,11},{4,68},{5,13},{6,70},{7,15},{8,72},{9,1... | collective-permute-start | bytes 245768 | tf_op jit(solution)/shard_map/ppermute | solution.py:400

commit v5 on v4

--- a/solution.py
+++ b/solution.py
@@ -1,3 +1,5 @@
+import functools
+
 import jax
 import jax.numpy as jnp
 import numpy as np
@@ -126,12 +128,19 @@
         out_ref[pl.ds(6 * ROWS + comp * 8, 8), :] = packed
 
 
-def inner_kernel(x_ref, blend_ref, out_ref, u_ref, flux_ref, speed_ref, acc_ref, acc_x_ref):
+def inner_kernel(x_ref, troubled_ref, level_ref, out_ref, u_ref, flux_ref, speed_ref, acc_ref, acc_x_ref):
     weak, scale = weak_matrix(), [GRID_SCALE / w for w in LOBATTO_WEIGHTS]
     lane = lanes_of((8, 128))
     k = lax.broadcasted_iota(jnp.int32, (8, 128), 0)
     upper, ex, ey, ez = lane >= 64, (lane // 32) % 2, (lane // 8) % 4, lane % 8
-    blend = blend_ref[...]
+    blend = jnp.zeros((8, 128), jnp.float32)
+    for x in range(2):
+        marks = (troubled_ref[x] * level_ref[x]).astype(jnp.float32)
+        marks = jnp.dot(marks, jnp.where(ez == k, 1.0, 0.0), preferred_element_type=jnp.float32)
+        for y in range(4):
+            row = jnp.broadcast_to(marks[y : y + 1, :], (8, 128))
+            blend = jnp.where((ex == x) & (ey == y), row, blend)
+    blend = blend / 5.0
     smooth, half_blend = 1.0 - blend, 0.5 * blend
 
     def by_row(values):
@@ -186,7 +195,7 @@
             acc_ref[n, at, :] = smooth * volume + scale_z * (pltpu.roll(g, 1, 0) - g)
         return carry
 
-    lax.fori_loop(0, 32, first, 0, unroll=2)
+    lax.fori_loop(0, 32, first, 0, unroll=4)
 
     def flux(d, n, at):
         return u_ref[1 + d, at, :] if n == 0 else flux_ref[d, n - 1, at, :]
@@ -202,7 +211,7 @@
             acc_ref[n, start, :] = acc_ref[n, start, :] + roll(star, 1)
         return carry
 
-    lax.fori_loop(0, 4, between, 0)
+    lax.fori_loop(0, 4, between, 0, unroll=4)
 
     end_y = jnp.where(ey < 3, 0.5, 0.0)
 
@@ -215,10 +224,16 @@
             u, f = [u_ref[n, a, :] for a in at], [flux(1, n, a) for a in at]
             g = [half_blend * (f[j] + f[j + 1] - largest[j] * (u[j + 1] - u[j])) for j in range(7)]
             g.append(end_y * (f[7] + roll(f[0], -8) - largest[7] * (roll(u[0], -8) - u[7])))
+            even, odd = [f[m] + f[7 - m] for m in range(4)], [f[m] - f[7 - m] for m in range(4)]
+            volumes = [None] * 8
+            for j in range(4):
+                from_odd, from_even = (
+                    sum(float(0.5 * (weak[j][m] + sign * weak[j][7 - m])) * part[m] for m in range(4))
+                    for sign, part in ((-1, odd), (1, even))
+                )
+                volumes[j], volumes[7 - j] = from_odd + from_even, from_odd - from_even
             for j in range(8):
-                volume = float(weak[j][0]) * f[0]
-                for m in range(1, 8):
-                    volume = volume + float(weak[j][m]) * f[m]
+                volume = volumes[j]
                 low = g[j - 1] if j else roll(g[7], 8)
                 acc_ref[n, at[j], :] = acc_ref[n, at[j], :] + (smooth * volume + scale[j] * (low - g[j]))
         return carry
@@ -269,6 +284,22 @@
                     out_ref[pl.ds(e * ROWS + 8 * n, 8), 256 * g + 128 * h : 256 * g + 128 * h + 128] = block[
                         64 * g + 8 * e : 64 * g + 8 * e + 8, :
                     ]
+
+
+def early_kernel(early_ref, *refs):
+    @pl.when(early_ref[0] != 0)
+    def _():
+        inner_kernel(*refs)
+
+
+def late_kernel(early_ref, done_ref, *refs):
+    @pl.when(early_ref[0] != 0)
+    def _():
+        refs[3][...] = done_ref[...]
+
+    @pl.when(early_ref[0] == 0)
+    def _():
+        inner_kernel(*refs)
 
 
 def outer_kernel(place_ref, pre_ref, own_ref, halo_ref, near_ref, far_ref, out_hbm, out_ref, star_ref, left_sem):
@@ -389,23 +420,10 @@
         name="faces",
     )(pltpu.with_memory_space_constraint(state, pltpu.HBM))
 
-    both = lax.all_gather(own, "gz", axis_index_groups=pairs(sizes[2], 0))
-    x_faces = both[:, : 4 * ROWS].reshape(2, 2, 2 * ROWS, 128)
-    y_faces = both[:, 4 * ROWS : 6 * ROWS]
-    arrived = {}
-    for shift in (1, 0):
-        face = odd_x if shift else 1 - odd_x
-        x_part = lax.dynamic_index_in_dim(x_faces, face, 1, keepdims=False)
-        sent = jnp.where(core == 0, x_part, y_faces)
-        arrived[shift] = lax.ppermute(sent, AXES, crossed(sizes, shift))
-    swap = pairs(sizes[2], 1)
-    far = lax.ppermute(own[6 * ROWS :], "gz", [(a, b) for a, b in swap] + [(b, a) for a, b in swap])
-
-    blend = troubled.reshape(64).astype(jnp.float32) * blend_level.reshape(64).astype(jnp.float32) / 5.0
-    inner = pl.pallas_call(
-        inner_kernel,
+    early = ((iz < sizes[2] // 2) | (ix < sizes[0] // 4)).astype(jnp.int32).reshape(1)
+    inner_call = functools.partial(
+        pl.pallas_call,
         out_shape=jax.ShapeDtypeStruct((8 * ROWS, 512), jnp.float32),
-        in_specs=[in_vmem()] * 2,
         out_specs=in_vmem(),
         scratch_shapes=[
             pltpu.VMEM((5, 256, 128), jnp.float32),
@@ -416,8 +434,27 @@
         ],
         compiler_params=LIMIT,
         cost_estimate=pl.CostEstimate(flops=20_000_000, bytes_accessed=1_400_000, transcendentals=65536),
-        name="inner",
-    )(state, jnp.broadcast_to(jnp.concatenate([blend, blend])[None, :], (8, 128)))
+    )
+    in_smem = pl.BlockSpec(memory_space=pltpu.SMEM)
+    done = inner_call(early_kernel, in_specs=[in_smem] + [in_vmem()] * 3, name="early")(
+        early, state, troubled, blend_level
+    )
+    own, done = lax.optimization_barrier((own, done))
+    swap = pairs(sizes[2], 1)
+    far = lax.ppermute(own[6 * ROWS :], "gz", [(a, b) for a, b in swap] + [(b, a) for a, b in swap])
+
+    both = lax.all_gather(own, "gz", axis_index_groups=pairs(sizes[2], 0))
+    x_faces = both[:, : 4 * ROWS].reshape(2, 2, 2 * ROWS, 128)
+    y_faces = both[:, 4 * ROWS : 6 * ROWS]
+    arrived = {}
+    for shift in (1, 0):
+        face = odd_x if shift else 1 - odd_x
+        x_part = lax.dynamic_index_in_dim(x_faces, face, 1, keepdims=False)
+        sent = jnp.where(core == 0, x_part, y_faces)
+        arrived[shift] = lax.ppermute(sent, AXES, crossed(sizes, shift))
+    inner = inner_call(late_kernel, in_specs=[in_smem] + [in_vmem()] * 4, name="late")(
+        early, done, state, troubled, blend_level
+    )
 
     halo = lax.all_gather(jnp.stack([arrived[1], arrived[0]]), "gz", axis_index_groups=pairs(sizes[2], 0))
     place = jnp.stack([core, odd_x, odd_y]).astype(jnp.int32)

time: 40.2 us -> 40.1 us (level)
  waiting for transfers between devices: 0.01 us -> 3.4 us
  blocking collectives: 13.9 us -> 11.2 us
  Pallas kernels: 6.39 us -> 5.93 us
    ppermute x2, waiting for transfers between devices: 0.01 us -> 3.4 us  [on_device(): arrived[shift] = lax.ppermute(sent, AXES, crossed(sizes, shift))]
    all_gather x1, blocking collectives: 5.11 us -> 2.47 us  [on_device(): lax.all_gather(jnp.stack([arrived[1], arrived[0]]), 'gz', axis_index_grou...]
    pallas_call x1 -> x2, Pallas kernels: 3.32 us -> 2.79 us  [the longest x1 2.73 us: on_device(): inner_call(early_kernel, in_specs=[in_smem] + [in_vmem()] * 3, name='early')]
  transfers between devices with their start and end apart: 3 -> 3, of which waited for: 0 -> 1; matrix products, arithmetic and copies ran while one was open for 1% -> 0% of each run, Pallas kernels for 8% -> 0%
where the time goes in v5:
time: 40.1 us; the launch traced here: 39.9 us
  starting transfers between devices  19 us (47%)
  blocking collectives  11.2 us (28%)
  Pallas kernels  5.93 us (15%)
  waiting for transfers between devices  3.4 us (8%)
    ppermute x1, starting transfers between devices, on_device(): lax.ppermute(own[6 * ROWS:], 'gz', [(a, b) for a, b in swap] + [(b, a) fo...  12 us
    all_gather x1, blocking collectives, on_device(): both = lax.all_gather(own, 'gz', axis_index_groups=pairs(sizes[2], 0))  8.76 us
    ppermute x2, starting transfers between devices, on_device(): arrived[shift] = lax.ppermute(sent, AXES, crossed(sizes, shift))  7.02 us
    ppermute x2, waiting for transfers between devices, on_device(): arrived[shift] = lax.ppermute(sent, AXES, crossed(sizes, shift))  3.4 us
    pallas_call x1, Pallas kernels, on_device(): inner_call(early_kernel, in_specs=[in_smem] + [in_vmem()] * 3, name='early')  2.73 us
    all_gather x1, blocking collectives, on_device(): lax.all_gather(jnp.stack([arrived[1], arrived[0]]), 'gz', axis_index_grou...  2.47 us
    pallas_call x1, Pallas kernels, on_device(): pl.pallas_call(outer_kernel, out_shape=jax.ShapeDtypeStruct((8 * ROWS, 51...  1.75 us
    pallas_call x1, Pallas kernels, on_device(): pl.pallas_call(faces_kernel, out_shape=jax.ShapeDtypeStruct((7 * ROWS, 12...  1.39 us
  transfers between devices with their start and end apart: 3, of which 1 were waited for; matrix products, arithmetic and copies ran while one was open for 0% of the time, Pallas kernels for 0%

profile of v5, /device:TPU:1, one launch (start us, length us, event | category | flops | bytes accessed | tf_op | source)
XLA Modules:
  0.0 39.9 jit_solution(9933596942196885823)
XLA Ops:
  0.0 0.0 copy-start
  0.0 0.0 copy-start.1
  0.0 0.0 copy-start.2
  0.0 1.4 %faces.1.own_ref = f32[280,128]{1,0:T(8,128)S(1)} custom-call(f32[320,512]{1,0:T(8,128)} %bitcast.23), custom_call_target="tpu_custom_call" | custom-call | tf_op jit(solution)/shard_map/faces/pallas_call | solution.py:413
  1.4 0.0 copy-done
  1.4 0.0 copy-done.1
  1.4 0.0 copy-done.2
  1.4 2.7 %early.1.done_ref = f32[320,512]{1,0:T(8,128)S(1)} custom-call(s32[1]{0:T(128)} %bitcast.3.early_ref, f32[320,512]{1,0:T(8,128)S(1)} %bitcast.24, s32[2,4,8]{2,1,0:T(4,128)S(1)} %copy-done.1, s32[2,4,8]{2,1,0:T(4,128)S(1)} %copy-done.2), custom_call_target="tpu_custom_call" | custom-call | flops 20000000 | bytes 1400000 | tf_op jit(solution)/shard_map/early/pallas_call | solution.py:439
  4.2 12.0 %collective-permute-start.2 = (f32[40,128]{1,0:T(8,128)S(1)}, f32[40,128]{1,0:T(8,128)S(1)}, u32[]{:S(2)}, u32[]{:S(2)}) collective-permute-start(f32[40,128]{1,0:T(8,128)S(1)} %slice.11), channel_id=1, source_target_pairs={{1,2},{3,4},{5,6},{7,0},{2,1},{4,3},{6,5},{0,7},{9,10},{11,12},{13... | collective-permute-start | bytes 61448 | tf_op jit(solution)/shard_map/ppermute | solution.py:444
  16.2 8.8 %all-gather = f32[560,128]{1,0:T(8,128)S(1)} all-gather(f32[280,128]{1,0:T(8,128)S(1)} %faces.1.own_ref), channel_id=2, replica_groups={{0,1},{2,3},{4,5},{6,7},{8,9},{10,11},{12,13},{14,15},{16,17},{18,19},{..., dimensions={0}, use_global_device_ids=true | all-gather | bytes 430080 | tf_op jit(solution)/shard_map/all_gather | solution.py:446
  25.0 5.1 %collective-permute-start = (f32[2,80,128]{2,1,0:T(8,128)S(1)}, f32[2,80,128]{2,1,0:T(8,128)S(1)}, u32[]{:S(2)}, u32[]{:S(2)}) collective-permute-start(f32[2,80,128]{2,1,0:T(8,128)S(1)} %get-tuple-element.9), channel_id=1, source_target_pairs={{0,960},{1,57},{2,962},{3,59},{4,964},{5,61},{6,966},{7,63},{8,968... | collective-permute-start | bytes 245768 | tf_op jit(solution)/shard_map/ppermute | solution.py:454
  30.1 1.9 %collective-permute-start.1 = (f32[2,80,128]{2,1,0:T(8,128)S(1)}, f32[2,80,128]{2,1,0:T(8,128)S(1)}, u32[]{:S(2)}, u32[]{:S(2)}) collective-permute-start(f32[2,80,128]{2,1,0:T(8,128)S(1)} %get-tuple-element.10), channel_id=1, source_target_pairs={{0,64},{1,9},{2,66},{3,11},{4,68},{5,13},{6,70},{7,15},{8,72},{9,1... | collective-permute-start | bytes 245768 | tf_op jit(solution)/shard_map/ppermute | solution.py:454
  32.1 0.1 late.1.pre_ref
  32.1 0.1 pad_add_fusion.place_ref
  32.2 0.0 collective-permute-done
  32.2 3.4 %collective-permute-done.1 = f32[2,80,128]{2,1,0:T(8,128)S(1)} collective-permute-done((f32[2,80,128]{2,1,0:T(8,128)S(1)}, f32[2,80,128]{2,1,0:T(8,128)S(1)}, u32[]{:S(2)}, u32[]{:S(2)}) %collective-permute-start.1) | collective-permute-done | bytes 81952 | tf_op jit(solution)/shard_map/ppermute | solution.py:454
  35.6 2.5 %all-gather.1 = f32[4,2,80,128]{3,2,1,0:T(8,128)S(1)} all-gather(f32[2,2,80,128]{3,2,1,0:T(8,128)S(1)} %pad_maximum_fusion), channel_id=3, replica_groups={{0,1},{2,3},{4,5},{6,7},{8,9},{10,11},{12,13},{14,15},{16,17},{18,19},{..., dimensions={0}, use_global_device_ids=true | all-gather | bytes 491520 | tf_op jit(solution)/shard_map/all_gather | solution.py:459
  38.1 0.0 collective-permute-done.2.far_ref
  38.1 1.7 %outer.1 = f32[320,512]{1,0:T(8,128)} custom-call(s32[3]{0:T(128)S(1)} %pad_add_fusion.place_ref, f32[320,512]{1,0:T(8,128)S(1)} %late.1.pre_ref, f32[280,128]{1,0:T(8,128)S(1)} %faces.1.own_ref, f32[2,2,2,80,128]{4,3,2,1,0:T(8,128)S(1)} %bitcast.29, f32[2,280,128]{2,1,0:T(8,128)S(1)} %bitcast.28, f32[40,128]{1,0:T(8,128)S(1)} %collective-permute-done.2.far_ref), custom_call_target="tpu_custom_call" | custom-call | tf_op jit(solution)/shard_map/outer/pallas_call | solution.py:461
  (4 shorter events, 0.1 us)
Async XLA Ops:
  0.0 1.4 %copy-start = (f32[2,4,8,5,512]{4,2,3,1,0:T(8,128)S(1)}, f32[2,4,8,5,512]{4,2,3,1,0:T(8,128)}, u32[]{:S(2)}) copy-start(f32[2,4,8,5,512]{4,2,3,1,0:T(8,128)} %param.3) | copy-start | bytes 1966084
  0.0 1.4 %copy-start.1 = (s32[2,4,8]{2,1,0:T(4,128)S(1)}, s32[2,4,8]{2,1,0:T(4,128)}, u32[]{:S(2)}) copy-start(s32[2,4,8]{2,1,0:T(4,128)} %refs_1_.3) | copy-start | bytes 772
  0.0 1.4 %copy-start.2 = (s32[2,4,8]{2,1,0:T(4,128)S(1)}, s32[2,4,8]{2,1,0:T(4,128)}, u32[]{:S(2)}) copy-start(s32[2,4,8]{2,1,0:T(4,128)} %refs_2_.3) | copy-start | bytes 772
  4.2 33.9 %collective-permute-start.2 = (f32[40,128]{1,0:T(8,128)S(1)}, f32[40,128]{1,0:T(8,128)S(1)}, u32[]{:S(2)}, u32[]{:S(2)}) collective-permute-start(f32[40,128]{1,0:T(8,128)S(1)} %slice.11), channel_id=1, source_target_pairs={{1,2},{3,4},{5,6},{7,0},{2,1},{4,3},{6,5},{0,7},{9,10},{11,12},{13... | collective-permute-start | bytes 61448 | tf_op jit(solution)/shard_map/ppermute | solution.py:444
  25.0 7.2 %collective-permute-start = (f32[2,80,128]{2,1,0:T(8,128)S(1)}, f32[2,80,128]{2,1,0:T(8,128)S(1)}, u32[]{:S(2)}, u32[]{:S(2)}) collective-permute-start(f32[2,80,128]{2,1,0:T(8,128)S(1)} %get-tuple-element.9), channel_id=1, source_target_pairs={{0,960},{1,57},{2,962},{3,59},{4,964},{5,61},{6,966},{7,63},{8,968... | collective-permute-start | bytes 245768 | tf_op jit(solution)/shard_map/ppermute | solution.py:454
  30.1 5.5 %collective-permute-start.1 = (f32[2,80,128]{2,1,0:T(8,128)S(1)}, f32[2,80,128]{2,1,0:T(8,128)S(1)}, u32[]{:S(2)}, u32[]{:S(2)}) collective-permute-start(f32[2,80,128]{2,1,0:T(8,128)S(1)} %get-tuple-element.10), channel_id=1, source_target_pairs={{0,64},{1,9},{2,66},{3,11},{4,68},{5,13},{6,70},{7,15},{8,72},{9,1... | collective-permute-start | bytes 245768 | tf_op jit(solution)/shard_map/ppermute | solution.py:454

commit v6 on v5

--- a/solution.py
+++ b/solution.py
@@ -420,7 +420,17 @@
         name="faces",
     )(pltpu.with_memory_space_constraint(state, pltpu.HBM))
 
-    early = ((iz < sizes[2] // 2) | (ix < sizes[0] // 4)).astype(jnp.int32).reshape(1)
+    both = lax.all_gather(own, "gz", axis_index_groups=pairs(sizes[2], 0))
+    x_faces = both[:, : 4 * ROWS].reshape(2, 2, 2 * ROWS, 128)
+    y_faces = both[:, 4 * ROWS : 6 * ROWS]
+    sent = []
+    for shift in range(2):
+        face = odd_x if shift else 1 - odd_x
+        x_part = lax.dynamic_index_in_dim(x_faces, face, 1, keepdims=False)
+        sent.append(jnp.where(core == 0, x_part, y_faces))
+    arrived_long = lax.ppermute(sent[1], AXES, crossed(sizes, 1))
+
+    early = (iz < sizes[2] // 2).astype(jnp.int32).reshape(1)
     inner_call = functools.partial(
         pl.pallas_call,
         out_shape=jax.ShapeDtypeStruct((8 * ROWS, 512), jnp.float32),
@@ -439,24 +449,16 @@
     done = inner_call(early_kernel, in_specs=[in_smem] + [in_vmem()] * 3, name="early")(
         early, state, troubled, blend_level
     )
-    own, done = lax.optimization_barrier((own, done))
+    z_faces, short, done = lax.optimization_barrier((own[6 * ROWS :], sent[0], done))
     swap = pairs(sizes[2], 1)
-    far = lax.ppermute(own[6 * ROWS :], "gz", [(a, b) for a, b in swap] + [(b, a) for a, b in swap])
-
-    both = lax.all_gather(own, "gz", axis_index_groups=pairs(sizes[2], 0))
-    x_faces = both[:, : 4 * ROWS].reshape(2, 2, 2 * ROWS, 128)
-    y_faces = both[:, 4 * ROWS : 6 * ROWS]
-    arrived = {}
-    for shift in (1, 0):
-        face = odd_x if shift else 1 - odd_x
-        x_part = lax.dynamic_index_in_dim(x_faces, face, 1, keepdims=False)
-        sent = jnp.where(core == 0, x_part, y_faces)
-        arrived[shift] = lax.ppermute(sent, AXES, crossed(sizes, shift))
+    far = lax.ppermute(z_faces, "gz", [(a, b) for a, b in swap] + [(b, a) for a, b in swap])
+    arrived_short = lax.ppermute(short, AXES, crossed(sizes, 0))
+
     inner = inner_call(late_kernel, in_specs=[in_smem] + [in_vmem()] * 4, name="late")(
         early, done, state, troubled, blend_level
     )
 
-    halo = lax.all_gather(jnp.stack([arrived[1], arrived[0]]), "gz", axis_index_groups=pairs(sizes[2], 0))
+    halo = lax.all_gather(jnp.stack([arrived_long, arrived_short]), "gz", axis_index_groups=pairs(sizes[2], 0))
     place = jnp.stack([core, odd_x, odd_y]).astype(jnp.int32)
     full = pl.pallas_call(
         outer_kernel,

time: 40.1 us -> 38.8 us (0.968)
  starting transfers between devices: 19 us -> 11.5 us
  blocking collectives: 11.2 us -> 18.1 us
  waiting for transfers between devices: 3.4 us -> 2.12 us
  local copies, waits for them, and re-layouts: 0.03 us -> 0.69 us
    ppermute x3, starting transfers between devices: 19 us -> 11.5 us  [the longest x1 6.41 us: on_device(): lax.ppermute(z_faces, 'gz', [(a, b) for a, b in swap] + [(b, a) for a, b...]
    all_gather x1, blocking collectives: 8.76 us -> 15.9 us  [on_device(): both = lax.all_gather(own, 'gz', axis_index_groups=pairs(sizes[2], 0))]
    ppermute x3, waiting for transfers between devices: 3.4 us -> 2.12 us  [the longest x1 2.12 us: on_device(): arrived_short = lax.ppermute(short, AXES, crossed(sizes, 0))]
    unnamed x6, local copies, waits for them, and re-layouts: 0.01 us -> 0.68 us
  transfers between devices with their start and end apart: 3 -> 3, of which waited for: 1 -> 1; matrix products, arithmetic and copies ran while one was open for 0% -> 0% of each run, Pallas kernels for 0% -> 7%
where the time goes in v6:
time: 38.8 us; the launch traced here: 38.6 us
  blocking collectives  18.1 us (47%)
  starting transfers between devices  11.5 us (30%)
  Pallas kernels  5.85 us (15%)
  waiting for transfers between devices  2.12 us (5%)
  local copies, waits for them, and re-layouts  0.69 us (2%)
    all_gather x1, blocking collectives, on_device(): both = lax.all_gather(own, 'gz', axis_index_groups=pairs(sizes[2], 0))  15.9 us
    ppermute x1, starting transfers between devices, on_device(): lax.ppermute(z_faces, 'gz', [(a, b) for a, b in swap] + [(b, a) for a, b...  6.41 us
    ppermute x1, starting transfers between devices, on_device(): arrived_short = lax.ppermute(short, AXES, crossed(sizes, 0))  3.2 us
    pallas_call x1, Pallas kernels, on_device(): inner_call(early_kernel, in_specs=[in_smem] + [in_vmem()] * 3, name='early')  2.73 us
    all_gather x1, blocking collectives, on_device(): lax.all_gather(jnp.stack([arrived_long, arrived_short]), 'gz', axis_index...  2.21 us
    ppermute x1, waiting for transfers between devices, on_device(): arrived_short = lax.ppermute(short, AXES, crossed(sizes, 0))  2.12 us
    ppermute x1, starting transfers between devices, on_device(): arrived_long = lax.ppermute(sent[1], AXES, crossed(sizes, 1))  1.92 us
    pallas_call x1, Pallas kernels, on_device(): pl.pallas_call(outer_kernel, out_shape=jax.ShapeDtypeStruct((8 * ROWS, 51...  1.75 us
  transfers between devices with their start and end apart: 3, of which 1 were waited for; matrix products, arithmetic and copies ran while one was open for 0% of the time, Pallas kernels for 7%

profile of v6, /device:TPU:1, one launch (start us, length us, event | category | flops | bytes accessed | tf_op | source)
XLA Modules:
  0.0 38.6 jit_solution(10269376258084197720)
XLA Ops:
  0.0 1.3 %faces.1.own_ref = f32[280,128]{1,0:T(8,128)S(1)} custom-call(f32[320,512]{1,0:T(8,128)} %bitcast.23), custom_call_target="tpu_custom_call" | custom-call | tf_op jit(solution)/shard_map/faces/pallas_call | solution.py:413
  1.3 0.0 copy-start
  1.3 15.9 %all-gather = f32[560,128]{1,0:T(8,128)S(1)} all-gather(f32[280,128]{1,0:T(8,128)S(1)} %faces.1.own_ref), channel_id=2, replica_groups={{0,1},{2,3},{4,5},{6,7},{8,9},{10,11},{12,13},{14,15},{16,17},{18,19},{..., dimensions={0}, use_global_device_ids=true | all-gather | bytes 430080 | tf_op jit(solution)/shard_map/all_gather | solution.py:423
  17.3 1.9 %collective-permute-start = (f32[2,80,128]{2,1,0:T(8,128)S(1)}, f32[2,80,128]{2,1,0:T(8,128)S(1)}, u32[]{:S(2)}, u32[]{:S(2)}) collective-permute-start(f32[2,80,128]{2,1,0:T(8,128)S(1)} %get-tuple-element.11), channel_id=1, source_target_pairs={{0,960},{1,57},{2,962},{3,59},{4,964},{5,61},{6,966},{7,63},{8,968... | collective-permute-start | bytes 245768 | tf_op jit(solution)/shard_map/ppermute | solution.py:431
  19.3 0.0 copy-start.2
  19.3 0.0 copy-start.1
  19.3 0.0 copy-done
  19.3 0.6 %copy-done.2 = s32[2,4,8]{2,1,0:T(4,128)S(1)} copy-done((s32[2,4,8]{2,1,0:T(4,128)S(1)}, s32[2,4,8]{2,1,0:T(4,128)}, u32[]{:S(2)}) %copy-start.2) | copy-done | bytes 280
  19.9 0.0 copy-done.1
  20.0 2.7 %early.1.done_ref = f32[320,512]{1,0:T(8,128)S(1)} custom-call(s32[1]{0:T(128)} %bitcast.3.early_ref, f32[320,512]{1,0:T(8,128)S(1)} %bitcast.24, s32[2,4,8]{2,1,0:T(4,128)S(1)} %copy-done.1, s32[2,4,8]{2,1,0:T(4,128)S(1)} %copy-done.2), custom_call_target="tpu_custom_call" | custom-call | flops 20000000 | bytes 1400000 | tf_op jit(solution)/shard_map/early/pallas_call | solution.py:449
  22.7 6.4 %collective-permute-start.2 = (f32[40,128]{1,0:T(8,128)S(1)}, f32[40,128]{1,0:T(8,128)S(1)}, u32[]{:S(2)}, u32[]{:S(2)}) collective-permute-start(f32[40,128]{1,0:T(8,128)S(1)} %slice.12), channel_id=1, source_target_pairs={{1,2},{3,4},{5,6},{7,0},{2,1},{4,3},{6,5},{0,7},{9,10},{11,12},{13... | collective-permute-start | bytes 61448 | tf_op jit(solution)/shard_map/ppermute | solution.py:454
  29.1 3.2 %collective-permute-start.1 = (f32[2,80,128]{2,1,0:T(8,128)S(1)}, f32[2,80,128]{2,1,0:T(8,128)S(1)}, u32[]{:S(2)}, u32[]{:S(2)}) collective-permute-start(f32[2,80,128]{2,1,0:T(8,128)S(1)} %get-tuple-element.9), channel_id=1, source_target_pairs={{0,64},{1,9},{2,66},{3,11},{4,68},{5,13},{6,70},{7,15},{8,72},{9,1... | collective-permute-start | bytes 245768 | tf_op jit(solution)/shard_map/ppermute | solution.py:455
  32.3 0.1 late.1.pre_ref
  32.4 0.1 pad_add_fusion.place_ref
  32.5 0.0 collective-permute-done
  32.5 2.1 %collective-permute-done.1 = f32[2,80,128]{2,1,0:T(8,128)S(1)} collective-permute-done((f32[2,80,128]{2,1,0:T(8,128)S(1)}, f32[2,80,128]{2,1,0:T(8,128)S(1)}, u32[]{:S(2)}, u32[]{:S(2)}) %collective-permute-start.1) | collective-permute-done | bytes 81952 | tf_op jit(solution)/shard_map/ppermute | solution.py:455
  34.6 2.2 %all-gather.1 = f32[4,2,80,128]{3,2,1,0:T(8,128)S(1)} all-gather(f32[2,2,80,128]{3,2,1,0:T(8,128)S(1)} %pad_maximum_fusion), channel_id=3, replica_groups={{0,1},{2,3},{4,5},{6,7},{8,9},{10,11},{12,13},{14,15},{16,17},{18,19},{..., dimensions={0}, use_global_device_ids=true | all-gather | bytes 491520 | tf_op jit(solution)/shard_map/all_gather | solution.py:461
  36.8 0.0 collective-permute-done.2.far_ref
  36.8 1.7 %outer.1 = f32[320,512]{1,0:T(8,128)} custom-call(s32[3]{0:T(128)S(1)} %pad_add_fusion.place_ref, f32[320,512]{1,0:T(8,128)S(1)} %late.1.pre_ref, f32[280,128]{1,0:T(8,128)S(1)} %faces.1.own_ref, f32[2,2,2,80,128]{4,3,2,1,0:T(8,128)S(1)} %bitcast.29, f32[2,280,128]{2,1,0:T(8,128)S(1)} %bitcast.28, f32[40,128]{1,0:T(8,128)S(1)} %collective-permute-done.2.far_ref), custom_call_target="tpu_custom_call" | custom-call | tf_op jit(solution)/shard_map/outer/pallas_call | solution.py:463
  (4 shorter events, 0.1 us)
Async XLA Ops:
  1.3 18.0 %copy-start = (f32[2,4,8,5,512]{4,2,3,1,0:T(8,128)S(1)}, f32[2,4,8,5,512]{4,2,3,1,0:T(8,128)}, u32[]{:S(2)}) copy-start(f32[2,4,8,5,512]{4,2,3,1,0:T(8,128)} %param.3) | copy-start | bytes 1966084
  17.3 15.2 %collective-permute-start = (f32[2,80,128]{2,1,0:T(8,128)S(1)}, f32[2,80,128]{2,1,0:T(8,128)S(1)}, u32[]{:S(2)}, u32[]{:S(2)}) collective-permute-start(f32[2,80,128]{2,1,0:T(8,128)S(1)} %get-tuple-element.11), channel_id=1, source_target_pairs={{0,960},{1,57},{2,962},{3,59},{4,964},{5,61},{6,966},{7,63},{8,968... | collective-permute-start | bytes 245768 | tf_op jit(solution)/shard_map/ppermute | solution.py:431
  19.3 0.7 %copy-start.2 = (s32[2,4,8]{2,1,0:T(4,128)S(1)}, s32[2,4,8]{2,1,0:T(4,128)}, u32[]{:S(2)}) copy-start(s32[2,4,8]{2,1,0:T(4,128)} %refs_2_.3) | copy-start | bytes 772
  19.3 0.7 %copy-start.1 = (s32[2,4,8]{2,1,0:T(4,128)S(1)}, s32[2,4,8]{2,1,0:T(4,128)}, u32[]{:S(2)}) copy-start(s32[2,4,8]{2,1,0:T(4,128)} %refs_1_.3) | copy-start | bytes 772
  22.7 14.1 %collective-permute-start.2 = (f32[40,128]{1,0:T(8,128)S(1)}, f32[40,128]{1,0:T(8,128)S(1)}, u32[]{:S(2)}, u32[]{:S(2)}) collective-permute-start(f32[40,128]{1,0:T(8,128)S(1)} %slice.12), channel_id=1, source_target_pairs={{1,2},{3,4},{5,6},{7,0},{2,1},{4,3},{6,5},{0,7},{9,10},{11,12},{13... | collective-permute-start | bytes 61448 | tf_op jit(solution)/shard_map/ppermute | solution.py:454
  29.1 5.5 %collective-permute-start.1 = (f32[2,80,128]{2,1,0:T(8,128)S(1)}, f32[2,80,128]{2,1,0:T(8,128)S(1)}, u32[]{:S(2)}, u32[]{:S(2)}) collective-permute-start(f32[2,80,128]{2,1,0:T(8,128)S(1)} %get-tuple-element.9), channel_id=1, source_target_pairs={{0,64},{1,9},{2,66},{3,11},{4,68},{5,13},{6,70},{7,15},{8,72},{9,1... | collective-permute-start | bytes 245768 | tf_op jit(solution)/shard_map/ppermute | solution.py:455

commit v7 on v6

--- a/solution.py
+++ b/solution.py
@@ -286,13 +286,20 @@
                     ]
 
 
-def early_kernel(early_ref, *refs):
+def early_kernel(early_ref, x_hbm, troubled_hbm, level_hbm, out_ref, x_ref, troubled_ref, level_ref, here, *scratch):
     @pl.when(early_ref[0] != 0)
     def _():
-        inner_kernel(*refs)
-
-
-def late_kernel(early_ref, done_ref, *refs):
+        ends = ((x_hbm, x_ref), (troubled_hbm, troubled_ref), (level_hbm, level_ref))
+        copies = [pltpu.make_async_copy(a, b, here.at[n]) for n, (a, b) in enumerate(ends)]
+        for copy in copies:
+            copy.start()
+        for copy in copies:
+            copy.wait()
+        inner_kernel(x_ref, troubled_ref, level_ref, out_ref, *scratch)
+
+
+def late_kernel(early_ref, done_ref, far_ref, *refs):
+    del far_ref
     @pl.when(early_ref[0] != 0)
     def _():
         refs[3][...] = done_ref[...]
@@ -382,10 +389,10 @@
     return [[(2 * n + shift) % size, (2 * n + 1 + shift) % size] for n in range(size // 2)]
 
 
-def crossed(sizes, shift):
+def crossed(sizes, shift, first, last):
     nx, ny, nz = sizes
     moves = []
-    for z in range(nz):
+    for z in range(first, last):
         for a, b in pairs(nx, shift) if z % 2 == 0 else pairs(ny, shift):
             for other in range(ny if z % 2 == 0 else nx):
                 ends = [((v * ny + other) if z % 2 == 0 else (other * ny + v)) * nz + z for v in (a, b)]
@@ -428,37 +435,43 @@
         face = odd_x if shift else 1 - odd_x
         x_part = lax.dynamic_index_in_dim(x_faces, face, 1, keepdims=False)
         sent.append(jnp.where(core == 0, x_part, y_faces))
-    arrived_long = lax.ppermute(sent[1], AXES, crossed(sizes, 1))
-
-    early = (iz < sizes[2] // 2).astype(jnp.int32).reshape(1)
+    ahead = [lax.ppermute(v, AXES, crossed(sizes, n, 0, 2)) for n, v in enumerate(sent)]
+
+    early = (iz < 2).astype(jnp.int32).reshape(1)
+    work = [
+        pltpu.VMEM((5, 256, 128), jnp.float32),
+        pltpu.VMEM((3, 4, 256, 128), jnp.float32),
+        pltpu.VMEM((3, 256, 128), jnp.float32),
+        pltpu.VMEM((5, 256, 128), jnp.float32),
+        pltpu.VMEM((5, 256, 128), jnp.float32),
+    ]
     inner_call = functools.partial(
         pl.pallas_call,
         out_shape=jax.ShapeDtypeStruct((8 * ROWS, 512), jnp.float32),
         out_specs=in_vmem(),
-        scratch_shapes=[
-            pltpu.VMEM((5, 256, 128), jnp.float32),
-            pltpu.VMEM((3, 4, 256, 128), jnp.float32),
-            pltpu.VMEM((3, 256, 128), jnp.float32),
-            pltpu.VMEM((5, 256, 128), jnp.float32),
-            pltpu.VMEM((5, 256, 128), jnp.float32),
-        ],
         compiler_params=LIMIT,
         cost_estimate=pl.CostEstimate(flops=20_000_000, bytes_accessed=1_400_000, transcendentals=65536),
     )
     in_smem = pl.BlockSpec(memory_space=pltpu.SMEM)
-    done = inner_call(early_kernel, in_specs=[in_smem] + [in_vmem()] * 3, name="early")(
-        early, state, troubled, blend_level
-    )
-    z_faces, short, done = lax.optimization_barrier((own[6 * ROWS :], sent[0], done))
+    mine = [
+        pltpu.VMEM((8 * ROWS, 512), jnp.float32),
+        pltpu.VMEM((2, 4, 8), jnp.int32),
+        pltpu.VMEM((2, 4, 8), jnp.int32),
+        pltpu.SemaphoreType.DMA((3,)),
+    ]
+    done = inner_call(
+        early_kernel, in_specs=[in_smem] + [in_hbm()] * 3, scratch_shapes=mine + work, name="early"
+    )(early, *[pltpu.with_memory_space_constraint(v, pltpu.HBM) for v in (state, troubled, blend_level)])
+    z_faces, sent, done = lax.optimization_barrier((own[6 * ROWS :], sent, done))
     swap = pairs(sizes[2], 1)
     far = lax.ppermute(z_faces, "gz", [(a, b) for a, b in swap] + [(b, a) for a, b in swap])
-    arrived_short = lax.ppermute(short, AXES, crossed(sizes, 0))
-
-    inner = inner_call(late_kernel, in_specs=[in_smem] + [in_vmem()] * 4, name="late")(
-        early, done, state, troubled, blend_level
+    after = [lax.ppermute(v, AXES, crossed(sizes, n, 2, sizes[2])) for n, v in enumerate(sent)]
+
+    inner = inner_call(late_kernel, in_specs=[in_smem] + [in_vmem()] * 5, scratch_shapes=work, name="late")(
+        early, done, far, state, troubled, blend_level
     )
 
-    halo = lax.all_gather(jnp.stack([arrived_long, arrived_short]), "gz", axis_index_groups=pairs(sizes[2], 0))
+    halo = lax.all_gather(jnp.stack([ahead[1] + after[1], ahead[0] + after[0]]), "gz", axis_index_groups=pairs(sizes[2], 0))
     place = jnp.stack([core, odd_x, odd_y]).astype(jnp.int32)
     full = pl.pallas_call(
         outer_kernel,

time: 38.8 us -> 39.4 us (1.015)
  the two profiles are of different devices: /device:TPU:1 before, /device:TPU:273 now
where the time goes in v7:
time: 39.4 us; the launch traced here: 39.1 us
  starting transfers between devices  17.5 us (44%)
  blocking collectives  14.8 us (38%)
  Pallas kernels  5.83 us (15%)
  local copies, waits for them, and re-layouts  0.63 us (2%)
    all_gather x1, blocking collectives, on_device(): lax.all_gather(jnp.stack([ahead[1] + after[1], ahead[0] + after[0]]), 'gz...  12.5 us
    ppermute x1, starting transfers between devices, on_device(): lax.ppermute(z_faces, 'gz', [(a, b) for a, b in swap] + [(b, a) for a, b...  11 us
    ppermute x2, starting transfers between devices, on_device(): lax.ppermute(v, AXES, crossed(sizes, n, 2, sizes[2]))  5.13 us
    pallas_call x1, Pallas kernels, on_device(): inner_call(late_kernel, in_specs=[in_smem] + [in_vmem()] * 5, scratch_sha...  2.73 us
    all_gather x1, blocking collectives, on_device(): both = lax.all_gather(own, 'gz', axis_index_groups=pairs(sizes[2], 0))  2.32 us
    pallas_call x1, Pallas kernels, on_device(): pl.pallas_call(outer_kernel, out_shape=jax.ShapeDtypeStruct((8 * ROWS, 51...  1.75 us
    ppermute x2, starting transfers between devices, on_device(): lax.ppermute(v, AXES, crossed(sizes, n, 0, 2))  1.33 us
    pallas_call x1, Pallas kernels, on_device(): pl.pallas_call(faces_kernel, out_shape=jax.ShapeDtypeStruct((7 * ROWS, 12...  1.32 us
  transfers between devices with their start and end apart: 5, of which 0 were waited for; matrix products, arithmetic and copies ran while one was open for 0% of the time, Pallas kernels for 7%

profile of v7, /device:TPU:273, one launch (start us, length us, event | category | flops | bytes accessed | tf_op | source)
XLA Modules:
  0.0 39.1 jit_solution(15856648594256121767)
XLA Ops:
  0.0 1.3 %faces.1.own_ref = f32[280,128]{1,0:T(8,128)S(1)} custom-call(f32[320,512]{1,0:T(8,128)} %bitcast.25), custom_call_target="tpu_custom_call" | custom-call | tf_op jit(solution)/shard_map/faces/pallas_call | solution.py:420
  1.3 2.3 %all-gather = f32[560,128]{1,0:T(8,128)S(1)} all-gather(f32[280,128]{1,0:T(8,128)S(1)} %faces.1.own_ref), channel_id=2, replica_groups={{0,1},{2,3},{4,5},{6,7},{8,9},{10,11},{12,13},{14,15},{16,17},{18,19},{..., dimensions={0}, use_global_device_ids=true | all-gather | bytes 430080 | tf_op jit(solution)/shard_map/all_gather | solution.py:430
  3.7 0.7 %collective-permute-start.3 = (f32[2,80,128]{2,1,0:T(8,128)S(1)}, f32[2,80,128]{2,1,0:T(8,128)S(1)}, u32[]{:S(2)}, u32[]{:S(2)}) collective-permute-start(f32[2,80,128]{2,1,0:T(8,128)S(1)} %get-tuple-element.12), channel_id=1, source_target_pairs={{0,64},{1,9},{8,72},{9,1},{16,80},{17,25},{24,88},{25,17},{32,96},... | collective-permute-start | bytes 245768 | tf_op jit(solution)/shard_map/ppermute | solution.py:438
  4.4 0.7 %collective-permute-start.1 = (f32[2,80,128]{2,1,0:T(8,128)S(1)}, f32[2,80,128]{2,1,0:T(8,128)S(1)}, u32[]{:S(2)}, u32[]{:S(2)}) collective-permute-start(f32[2,80,128]{2,1,0:T(8,128)S(1)} %get-tuple-element.11), channel_id=1, source_target_pairs={{0,960},{1,57},{8,968},{9,17},{16,976},{17,9},{24,984},{25,33},{32... | collective-permute-start | bytes 245768 | tf_op jit(solution)/shard_map/ppermute | solution.py:438
  5.1 0.0 copy-start
  5.1 11.0 %collective-permute-start = (f32[40,128]{1,0:T(8,128)S(1)}, f32[40,128]{1,0:T(8,128)S(1)}, u32[]{:S(2)}, u32[]{:S(2)}) collective-permute-start(f32[40,128]{1,0:T(8,128)S(1)} %slice.12), channel_id=1, source_target_pairs={{1,2},{3,4},{5,6},{7,0},{2,1},{4,3},{6,5},{0,7},{9,10},{11,12},{13... | collective-permute-start | bytes 61448 | tf_op jit(solution)/shard_map/ppermute | solution.py:467
  16.2 3.2 %collective-permute-start.4 = (f32[2,80,128]{2,1,0:T(8,128)S(1)}, f32[2,80,128]{2,1,0:T(8,128)S(1)}, u32[]{:S(2)}, u32[]{:S(2)}) collective-permute-start(f32[2,80,128]{2,1,0:T(8,128)S(1)} %get-tuple-element.12), channel_id=1, source_target_pairs={{2,66},{3,11},{4,68},{5,13},{6,70},{7,15},{10,74},{11,3},{12,76},{... | collective-permute-start | bytes 245768 | tf_op jit(solution)/shard_map/ppermute | solution.py:468
  19.4 1.9 %collective-permute-start.2 = (f32[2,80,128]{2,1,0:T(8,128)S(1)}, f32[2,80,128]{2,1,0:T(8,128)S(1)}, u32[]{:S(2)}, u32[]{:S(2)}) collective-permute-start(f32[2,80,128]{2,1,0:T(8,128)S(1)} %get-tuple-element.11), channel_id=1, source_target_pairs={{2,962},{3,59},{4,964},{5,61},{6,966},{7,63},{10,970},{11,19},{12,... | collective-permute-start | bytes 245768 | tf_op jit(solution)/shard_map/ppermute | solution.py:468
  21.3 0.0 copy-start.2
  21.3 0.0 copy-start.1
  21.3 0.1 pad_add_fusion.place_ref
  21.4 0.0 collective-permute-done.far_ref
  21.4 0.0 copy-done
  21.4 0.6 %copy-done.2 = s32[2,4,8]{2,1,0:T(4,128)S(1)} copy-done((s32[2,4,8]{2,1,0:T(4,128)S(1)}, s32[2,4,8]{2,1,0:T(4,128)}, u32[]{:S(2)}) %copy-start.2) | copy-done | bytes 280
  22.0 0.0 copy-done.1
  22.0 2.7 %late.1.pre_ref = f32[320,512]{1,0:T(8,128)S(1)} custom-call(s32[1]{0:T(128)} %bitcast.3.early_ref, f32[320,512]{1,0:T(8,128)S(1)} %early.1.done_ref, f32[40,128]{1,0:T(8,128)S(1)} %collective-permute-done.far_ref, f32[320,512]{1,0:T(8,128)S(1)} %bitcast.27, s32[2,4,8]{2,1,0:T(4,128)S(1)} %copy-done.1, s32[2,4,8]{2,1,0:T(4,128)S(1)} %copy-done.2), custom_call_target="tpu_custom_call" | custom-call | flops 20000000 | bytes 1400000 | tf_op jit(solution)/shard_map/late/pallas_call | solution.py:470
  24.7 0.0 collective-permute-done.3
  24.8 0.0 collective-permute-done.4
  24.8 0.0 collective-permute-done.1
  24.8 0.0 collective-permute-done.2
  24.8 12.5 %all-gather.1 = f32[4,2,80,128]{3,2,1,0:T(8,128)S(1)} all-gather(f32[2,2,80,128]{3,2,1,0:T(8,128)S(1)} %pad_maximum_fusion), channel_id=3, replica_groups={{0,1},{2,3},{4,5},{6,7},{8,9},{10,11},{12,13},{14,15},{16,17},{18,19},{..., dimensions={0}, use_global_device_ids=true | all-gather | bytes 491520 | tf_op jit(solution)/shard_map/all_gather | solution.py:474
  37.4 1.7 %outer.1 = f32[320,512]{1,0:T(8,128)} custom-call(s32[3]{0:T(128)S(1)} %pad_add_fusion.place_ref, f32[320,512]{1,0:T(8,128)S(1)} %late.1.pre_ref, f32[280,128]{1,0:T(8,128)S(1)} %faces.1.own_ref, f32[2,2,2,80,128]{4,3,2,1,0:T(8,128)S(1)} %bitcast.31, f32[2,280,128]{2,1,0:T(8,128)S(1)} %bitcast.30, f32[40,128]{1,0:T(8,128)S(1)} %collective-permute-done.far_ref), custom_call_target="tpu_custom_call" | custom-call | tf_op jit(solution)/shard_map/outer/pallas_call | solution.py:476
  (7 shorter events, 0.1 us)
Async XLA Ops:
  3.7 21.0 %collective-permute-start.3 = (f32[2,80,128]{2,1,0:T(8,128)S(1)}, f32[2,80,128]{2,1,0:T(8,128)S(1)}, u32[]{:S(2)}, u32[]{:S(2)}) collective-permute-start(f32[2,80,128]{2,1,0:T(8,128)S(1)} %get-tuple-element.12), channel_id=1, source_target_pairs={{0,64},{1,9},{8,72},{9,1},{16,80},{17,25},{24,88},{25,17},{32,96},... | collective-permute-start | bytes 245768 | tf_op jit(solution)/shard_map/ppermute | solution.py:438
  4.4 20.4 %collective-permute-start.1 = (f32[2,80,128]{2,1,0:T(8,128)S(1)}, f32[2,80,128]{2,1,0:T(8,128)S(1)}, u32[]{:S(2)}, u32[]{:S(2)}) collective-permute-start(f32[2,80,128]{2,1,0:T(8,128)S(1)} %get-tuple-element.11), channel_id=1, source_target_pairs={{0,960},{1,57},{8,968},{9,17},{16,976},{17,9},{24,984},{25,33},{32... | collective-permute-start | bytes 245768 | tf_op jit(solution)/shard_map/ppermute | solution.py:438
  5.1 16.3 %copy-start = (f32[2,4,8,5,512]{4,2,3,1,0:T(8,128)S(1)}, f32[2,4,8,5,512]{4,2,3,1,0:T(8,128)}, u32[]{:S(2)}) copy-start(f32[2,4,8,5,512]{4,2,3,1,0:T(8,128)} %param.3) | copy-start | bytes 1966084
  5.1 16.3 %collective-permute-start = (f32[40,128]{1,0:T(8,128)S(1)}, f32[40,128]{1,0:T(8,128)S(1)}, u32[]{:S(2)}, u32[]{:S(2)}) collective-permute-start(f32[40,128]{1,0:T(8,128)S(1)} %slice.12), channel_id=1, source_target_pairs={{1,2},{3,4},{5,6},{7,0},{2,1},{4,3},{6,5},{0,7},{9,10},{11,12},{13... | collective-permute-start | bytes 61448 | tf_op jit(solution)/shard_map/ppermute | solution.py:467
  16.2 8.6 %collective-permute-start.4 = (f32[2,80,128]{2,1,0:T(8,128)S(1)}, f32[2,80,128]{2,1,0:T(8,128)S(1)}, u32[]{:S(2)}, u32[]{:S(2)}) collective-permute-start(f32[2,80,128]{2,1,0:T(8,128)S(1)} %get-tuple-element.12), channel_id=1, source_target_pairs={{2,66},{3,11},{4,68},{5,13},{6,70},{7,15},{10,74},{11,3},{12,76},{... | collective-permute-start | bytes 245768 | tf_op jit(solution)/shard_map/ppermute | solution.py:468
  19.4 5.4 %collective-permute-start.2 = (f32[2,80,128]{2,1,0:T(8,128)S(1)}, f32[2,80,128]{2,1,0:T(8,128)S(1)}, u32[]{:S(2)}, u32[]{:S(2)}) collective-permute-start(f32[2,80,128]{2,1,0:T(8,128)S(1)} %get-tuple-element.11), channel_id=1, source_target_pairs={{2,962},{3,59},{4,964},{5,61},{6,966},{7,63},{10,970},{11,19},{12,... | collective-permute-start | bytes 245768 | tf_op jit(solution)/shard_map/ppermute | solution.py:468
  21.3 0.7 %copy-start.2 = (s32[2,4,8]{2,1,0:T(4,128)S(1)}, s32[2,4,8]{2,1,0:T(4,128)}, u32[]{:S(2)}) copy-start(s32[2,4,8]{2,1,0:T(4,128)} %refs_2_.1) | copy-start | bytes 772
  21.3 0.7 %copy-start.1 = (s32[2,4,8]{2,1,0:T(4,128)S(1)}, s32[2,4,8]{2,1,0:T(4,128)}, u32[]{:S(2)}) copy-start(s32[2,4,8]{2,1,0:T(4,128)} %refs_1_.1) | copy-start | bytes 772

commit v8 on v6

--- a/solution.py
+++ b/solution.py
@@ -1,5 +1,3 @@
-import functools
-
 import jax
 import jax.numpy as jnp
 import numpy as np
@@ -286,20 +284,14 @@
                     ]
 
 
-def early_kernel(early_ref, *refs):
-    @pl.when(early_ref[0] != 0)
-    def _():
-        inner_kernel(*refs)
-
-
-def late_kernel(early_ref, done_ref, *refs):
-    @pl.when(early_ref[0] != 0)
-    def _():
-        refs[3][...] = done_ref[...]
-
-    @pl.when(early_ref[0] == 0)
-    def _():
-        inner_kernel(*refs)
+def middle_kernel(far_ref, *refs):
+    del far_ref
+    inner_kernel(*refs)
+
+
+def pick_kernel(core_ref, both_ref, ahead_ref, out_ref):
+    del ahead_ref
+    out_ref[...] = both_ref[core_ref[0], pl.ds(6 * ROWS, ROWS), :]
 
 
 def outer_kernel(place_ref, pre_ref, own_ref, halo_ref, near_ref, far_ref, out_hbm, out_ref, star_ref, left_sem):
@@ -382,10 +374,10 @@
     return [[(2 * n + shift) % size, (2 * n + 1 + shift) % size] for n in range(size // 2)]
 
 
-def crossed(sizes, shift):
+def crossed(sizes, shift, first, last):
     nx, ny, nz = sizes
     moves = []
-    for z in range(nz):
+    for z in range(first, last):
         for a, b in pairs(nx, shift) if z % 2 == 0 else pairs(ny, shift):
             for other in range(ny if z % 2 == 0 else nx):
                 ends = [((v * ny + other) if z % 2 == 0 else (other * ny + v)) * nz + z for v in (a, b)]
@@ -428,12 +420,27 @@
         face = odd_x if shift else 1 - odd_x
         x_part = lax.dynamic_index_in_dim(x_faces, face, 1, keepdims=False)
         sent.append(jnp.where(core == 0, x_part, y_faces))
-    arrived_long = lax.ppermute(sent[1], AXES, crossed(sizes, 1))
-
-    early = (iz < sizes[2] // 2).astype(jnp.int32).reshape(1)
-    inner_call = functools.partial(
-        pl.pallas_call,
+    half = sizes[2] // 2
+    ahead = [lax.ppermute(v, AXES, crossed(sizes, n, 0, half)) for n, v in enumerate(sent)]
+
+    in_smem = pl.BlockSpec(memory_space=pltpu.SMEM)
+    z_faces = pl.pallas_call(
+        pick_kernel,
+        out_shape=jax.ShapeDtypeStruct((ROWS, 128), jnp.float32),
+        in_specs=[in_smem] + [in_vmem()] * 2,
+        out_specs=in_vmem(),
+        compiler_params=LIMIT,
+        name="pick",
+    )(core.astype(jnp.int32).reshape(1), both, sent[0])
+    z_faces, sent = lax.optimization_barrier((z_faces, sent))
+    swap = pairs(sizes[2], 1)
+    far = lax.ppermute(z_faces, "gz", [(a, b) for a, b in swap] + [(b, a) for a, b in swap])
+    after = [lax.ppermute(v, AXES, crossed(sizes, n, half, sizes[2])) for n, v in enumerate(sent)]
+
+    inner = pl.pallas_call(
+        middle_kernel,
         out_shape=jax.ShapeDtypeStruct((8 * ROWS, 512), jnp.float32),
+        in_specs=[in_vmem()] * 4,
         out_specs=in_vmem(),
         scratch_shapes=[
             pltpu.VMEM((5, 256, 128), jnp.float32),
@@ -444,21 +451,10 @@
         ],
         compiler_params=LIMIT,
         cost_estimate=pl.CostEstimate(flops=20_000_000, bytes_accessed=1_400_000, transcendentals=65536),
-    )
-    in_smem = pl.BlockSpec(memory_space=pltpu.SMEM)
-    done = inner_call(early_kernel, in_specs=[in_smem] + [in_vmem()] * 3, name="early")(
-        early, state, troubled, blend_level
-    )
-    z_faces, short, done = lax.optimization_barrier((own[6 * ROWS :], sent[0], done))
-    swap = pairs(sizes[2], 1)
-    far = lax.ppermute(z_faces, "gz", [(a, b) for a, b in swap] + [(b, a) for a, b in swap])
-    arrived_short = lax.ppermute(short, AXES, crossed(sizes, 0))
-
-    inner = inner_call(late_kernel, in_specs=[in_smem] + [in_vmem()] * 4, name="late")(
-        early, done, state, troubled, blend_level
-    )
-
-    halo = lax.all_gather(jnp.stack([arrived_long, arrived_short]), "gz", axis_index_groups=pairs(sizes[2], 0))
+        name="inner",
+    )(far, state, troubled, blend_level)
+
+    halo = lax.all_gather(jnp.stack([ahead[1] + after[1], ahead[0] + after[0]]), "gz", axis_index_groups=pairs(sizes[2], 0))
     place = jnp.stack([core, odd_x, odd_y]).astype(jnp.int32)
     full = pl.pallas_call(
         outer_kernel,

time: 38.8 us -> 37.1 us (0.956)
  waiting for transfers between devices: 2.12 us -> 1.15 us
  local copies, waits for them, and re-layouts: 0.69 us -> 0.03 us
    ppermute x2 -> x4, waiting for transfers between devices: 2.12 us -> 0.01 us  [the longest x2 0.01 us: on_device(): lax.ppermute(v, AXES, crossed(sizes, n, half, sizes[2]))]
    ppermute x1, waiting for transfers between devices: 0.01 us -> 1.14 us  [on_device(): lax.ppermute(z_faces, 'gz', [(a, b) for a, b in swap] + [(b, a) for a, b...]
    unnamed x6, local copies, waits for them, and re-layouts: 0.68 us -> 0.02 us
    ppermute x2 -> x4, starting transfers between devices: 5.13 us -> 5.3 us  [the longest x2 3.97 us: on_device(): lax.ppermute(v, AXES, crossed(sizes, n, 0, half))]
  transfers between devices with their start and end apart: 3 -> 5, of which waited for: 1 -> 1; matrix products, arithmetic and copies ran while one was open for 0% -> 0% of each run, Pallas kernels for 7% -> 7%
where the time goes in v8:
time: 37.1 us; the launch traced here: 36.8 us
  blocking collectives  17.8 us (48%)
  starting transfers between devices  11.7 us (32%)
  Pallas kernels  5.81 us (16%)
  waiting for transfers between devices  1.15 us (3%)
    all_gather x1, blocking collectives, on_device(): both = lax.all_gather(own, 'gz', axis_index_groups=pairs(sizes[2], 0))  15.8 us
    ppermute x1, starting transfers between devices, on_device(): lax.ppermute(z_faces, 'gz', [(a, b) for a, b in swap] + [(b, a) for a, b...  6.41 us
    ppermute x2, starting transfers between devices, on_device(): lax.ppermute(v, AXES, crossed(sizes, n, 0, half))  3.97 us
    pallas_call x1, Pallas kernels, on_device(): pl.pallas_call(middle_kernel, out_shape=jax.ShapeDtypeStruct((8 * ROWS, 5...  2.73 us
    all_gather x1, blocking collectives, on_device(): lax.all_gather(jnp.stack([ahead[1] + after[1], ahead[0] + after[0]]), 'gz...  2.04 us
    pallas_call x1, Pallas kernels, on_device(): pl.pallas_call(outer_kernel, out_shape=jax.ShapeDtypeStruct((8 * ROWS, 51...  1.75 us
    ppermute x2, starting transfers between devices, on_device(): lax.ppermute(v, AXES, crossed(sizes, n, half, sizes[2]))  1.33 us
    pallas_call x1, Pallas kernels, on_device(): pl.pallas_call(faces_kernel, out_shape=jax.ShapeDtypeStruct((7 * ROWS, 12...  1.32 us
  transfers between devices with their start and end apart: 5, of which 1 were waited for; matrix products, arithmetic and copies ran while one was open for 0% of the time, Pallas kernels for 7%

profile of v8, /device:TPU:1, one launch (start us, length us, event | category | flops | bytes accessed | tf_op | source)
XLA Modules:
  0.0 36.8 jit_solution(9613465842224277426)
XLA Ops:
  0.0 1.3 %faces.1.own_ref = f32[280,128]{1,0:T(8,128)S(1)} custom-call(f32[320,512]{1,0:T(8,128)} %bitcast.28), custom_call_target="tpu_custom_call" | custom-call | tf_op jit(solution)/shard_map/faces/pallas_call | solution.py:405
  1.3 15.8 %all-gather = f32[560,128]{1,0:T(8,128)S(1)} all-gather(f32[280,128]{1,0:T(8,128)S(1)} %faces.1.own_ref), channel_id=2, replica_groups={{0,1},{2,3},{4,5},{6,7},{8,9},{10,11},{12,13},{14,15},{16,17},{18,19},{..., dimensions={0}, use_global_device_ids=true | all-gather | bytes 430080 | tf_op jit(solution)/shard_map/all_gather | solution.py:415
  17.1 0.0 copy-start
  17.2 2.1 %collective-permute-start.1 = (f32[2,80,128]{2,1,0:T(8,128)S(1)}, f32[2,80,128]{2,1,0:T(8,128)S(1)}, u32[]{:S(2)}, u32[]{:S(2)}) collective-permute-start(f32[2,80,128]{2,1,0:T(8,128)S(1)} %get-tuple-element.9), channel_id=1, source_target_pairs={{0,960},{1,57},{2,962},{3,59},{8,968},{9,17},{10,970},{11,19},{16,... | collective-permute-start | bytes 245768 | tf_op jit(solution)/shard_map/ppermute | solution.py:424
  19.2 1.9 %collective-permute-start.3 = (f32[2,80,128]{2,1,0:T(8,128)S(1)}, f32[2,80,128]{2,1,0:T(8,128)S(1)}, u32[]{:S(2)}, u32[]{:S(2)}) collective-permute-start(f32[2,80,128]{2,1,0:T(8,128)S(1)} %get-tuple-element.10.ahead_ref), channel_id=1, source_target_pairs={{0,64},{1,9},{2,66},{3,11},{8,72},{9,1},{10,74},{11,3},{16,80},{17... | collective-permute-start | bytes 245768 | tf_op jit(solution)/shard_map/ppermute | solution.py:424
  21.2 6.4 %collective-permute-start = (f32[40,128]{1,0:T(8,128)S(1)}, f32[40,128]{1,0:T(8,128)S(1)}, u32[]{:S(2)}, u32[]{:S(2)}) collective-permute-start(f32[40,128]{1,0:T(8,128)S(1)} %pick.1), channel_id=1, source_target_pairs={{1,2},{3,4},{5,6},{7,0},{2,1},{4,3},{6,5},{0,7},{9,10},{11,12},{13... | collective-permute-start | bytes 61448 | tf_op jit(solution)/shard_map/ppermute | solution.py:437
  27.6 0.7 %collective-permute-start.2 = (f32[2,80,128]{2,1,0:T(8,128)S(1)}, f32[2,80,128]{2,1,0:T(8,128)S(1)}, u32[]{:S(2)}, u32[]{:S(2)}) collective-permute-start(f32[2,80,128]{2,1,0:T(8,128)S(1)} %get-tuple-element.9), channel_id=1, source_target_pairs={{4,964},{5,61},{6,966},{7,63},{12,972},{13,21},{14,974},{15,23},{2... | collective-permute-start | bytes 245768 | tf_op jit(solution)/shard_map/ppermute | solution.py:438
  28.3 0.7 %collective-permute-start.4 = (f32[2,80,128]{2,1,0:T(8,128)S(1)}, f32[2,80,128]{2,1,0:T(8,128)S(1)}, u32[]{:S(2)}, u32[]{:S(2)}) collective-permute-start(f32[2,80,128]{2,1,0:T(8,128)S(1)} %get-tuple-element.10.ahead_ref), channel_id=1, source_target_pairs={{4,68},{5,13},{6,70},{7,15},{12,76},{13,5},{14,78},{15,7},{20,84},... | collective-permute-start | bytes 245768 | tf_op jit(solution)/shard_map/ppermute | solution.py:438
  29.0 0.0 copy-start.2
  29.0 0.0 copy-start.1
  29.0 0.1 pad_add_fusion.place_ref
  29.1 1.1 %collective-permute-done.far_ref = f32[40,128]{1,0:T(8,128)S(1)} collective-permute-done((f32[40,128]{1,0:T(8,128)S(1)}, f32[40,128]{1,0:T(8,128)S(1)}, u32[]{:S(2)}, u32[]{:S(2)}) %collective-permute-start) | collective-permute-done | bytes 20512 | tf_op jit(solution)/shard_map/ppermute | solution.py:437
  30.2 0.0 copy-done
  30.2 0.0 copy-done.2
  30.2 0.0 copy-done.1
  30.2 2.7 %inner.1.pre_ref = f32[320,512]{1,0:T(8,128)S(1)} custom-call(f32[40,128]{1,0:T(8,128)S(1)} %collective-permute-done.far_ref, f32[320,512]{1,0:T(8,128)S(1)} %bitcast.29, s32[2,4,8]{2,1,0:T(4,128)S(1)} %copy-done.1, s32[2,4,8]{2,1,0:T(4,128)S(1)} %copy-done.2), custom_call_target="tpu_custom_call" | custom-call | flops 20000000 | bytes 1400000 | tf_op jit(solution)/shard_map/inner/pallas_call | solution.py:440
  32.9 0.0 collective-permute-done.2
  33.0 0.0 collective-permute-done.1
  33.0 0.0 collective-permute-done.4
  33.0 0.0 collective-permute-done.3
  33.0 2.0 %all-gather.1 = f32[4,2,80,128]{3,2,1,0:T(8,128)S(1)} all-gather(f32[2,2,80,128]{3,2,1,0:T(8,128)S(1)} %pad_maximum_fusion), channel_id=3, replica_groups={{0,1},{2,3},{4,5},{6,7},{8,9},{10,11},{12,13},{14,15},{16,17},{18,19},{..., dimensions={0}, use_global_device_ids=true | all-gather | bytes 491520 | tf_op jit(solution)/shard_map/all_gather | solution.py:457
  35.1 1.7 %outer.1 = f32[320,512]{1,0:T(8,128)} custom-call(s32[3]{0:T(128)S(1)} %pad_add_fusion.place_ref, f32[320,512]{1,0:T(8,128)S(1)} %inner.1.pre_ref, f32[280,128]{1,0:T(8,128)S(1)} %faces.1.own_ref, f32[2,2,2,80,128]{4,3,2,1,0:T(8,128)S(1)} %bitcast.30, f32[2,280,128]{2,1,0:T(8,128)S(1)} %bitcast.27, f32[40,128]{1,0:T(8,128)S(1)} %collective-permute-done.far_ref), custom_call_target="tpu_custom_call" | custom-call | tf_op jit(solution)/shard_map/outer/pallas_call | solution.py:459
  (6 shorter events, 0.1 us)
Async XLA Ops:
  17.1 13.1 %copy-start = (f32[2,4,8,5,512]{4,2,3,1,0:T(8,128)S(1)}, f32[2,4,8,5,512]{4,2,3,1,0:T(8,128)}, u32[]{:S(2)}) copy-start(f32[2,4,8,5,512]{4,2,3,1,0:T(8,128)} %param.3) | copy-start | bytes 1966084
  17.2 15.8 %collective-permute-start.1 = (f32[2,80,128]{2,1,0:T(8,128)S(1)}, f32[2,80,128]{2,1,0:T(8,128)S(1)}, u32[]{:S(2)}, u32[]{:S(2)}) collective-permute-start(f32[2,80,128]{2,1,0:T(8,128)S(1)} %get-tuple-element.9), channel_id=1, source_target_pairs={{0,960},{1,57},{2,962},{3,59},{8,968},{9,17},{10,970},{11,19},{16,... | collective-permute-start | bytes 245768 | tf_op jit(solution)/shard_map/ppermute | solution.py:424
  19.2 13.8 %collective-permute-start.3 = (f32[2,80,128]{2,1,0:T(8,128)S(1)}, f32[2,80,128]{2,1,0:T(8,128)S(1)}, u32[]{:S(2)}, u32[]{:S(2)}) collective-permute-start(f32[2,80,128]{2,1,0:T(8,128)S(1)} %get-tuple-element.10.ahead_ref), channel_id=1, source_target_pairs={{0,64},{1,9},{2,66},{3,11},{8,72},{9,1},{10,74},{11,3},{16,80},{17... | collective-permute-start | bytes 245768 | tf_op jit(solution)/shard_map/ppermute | solution.py:424
  21.2 9.0 %collective-permute-start = (f32[40,128]{1,0:T(8,128)S(1)}, f32[40,128]{1,0:T(8,128)S(1)}, u32[]{:S(2)}, u32[]{:S(2)}) collective-permute-start(f32[40,128]{1,0:T(8,128)S(1)} %pick.1), channel_id=1, source_target_pairs={{1,2},{3,4},{5,6},{7,0},{2,1},{4,3},{6,5},{0,7},{9,10},{11,12},{13... | collective-permute-start | bytes 61448 | tf_op jit(solution)/shard_map/ppermute | solution.py:437
  27.6 5.3 %collective-permute-start.2 = (f32[2,80,128]{2,1,0:T(8,128)S(1)}, f32[2,80,128]{2,1,0:T(8,128)S(1)}, u32[]{:S(2)}, u32[]{:S(2)}) collective-permute-start(f32[2,80,128]{2,1,0:T(8,128)S(1)} %get-tuple-element.9), channel_id=1, source_target_pairs={{4,964},{5,61},{6,966},{7,63},{12,972},{13,21},{14,974},{15,23},{2... | collective-permute-start | bytes 245768 | tf_op jit(solution)/shard_map/ppermute | solution.py:438
  28.3 4.7 %collective-permute-start.4 = (f32[2,80,128]{2,1,0:T(8,128)S(1)}, f32[2,80,128]{2,1,0:T(8,128)S(1)}, u32[]{:S(2)}, u32[]{:S(2)}) collective-permute-start(f32[2,80,128]{2,1,0:T(8,128)S(1)} %get-tuple-element.10.ahead_ref), channel_id=1, source_target_pairs={{4,68},{5,13},{6,70},{7,15},{12,76},{13,5},{14,78},{15,7},{20,84},... | collective-permute-start | bytes 245768 | tf_op jit(solution)/shard_map/ppermute | solution.py:438
  29.0 1.2 %copy-start.2 = (s32[2,4,8]{2,1,0:T(4,128)S(1)}, s32[2,4,8]{2,1,0:T(4,128)}, u32[]{:S(2)}) copy-start(s32[2,4,8]{2,1,0:T(4,128)} %refs_2_.1) | copy-start | bytes 772
  29.0 1.2 %copy-start.1 = (s32[2,4,8]{2,1,0:T(4,128)S(1)}, s32[2,4,8]{2,1,0:T(4,128)}, u32[]{:S(2)}) copy-start(s32[2,4,8]{2,1,0:T(4,128)} %refs_1_.1) | copy-start | bytes 772

commit v9 on v8

--- a/solution.py
+++ b/solution.py
@@ -284,11 +284,6 @@
                     ]
 
 
-def middle_kernel(far_ref, *refs):
-    del far_ref
-    inner_kernel(*refs)
-
-
 def pick_kernel(core_ref, both_ref, ahead_ref, out_ref):
     del ahead_ref
     out_ref[...] = both_ref[core_ref[0], pl.ds(6 * ROWS, ROWS), :]
@@ -438,9 +433,9 @@
     after = [lax.ppermute(v, AXES, crossed(sizes, n, half, sizes[2])) for n, v in enumerate(sent)]
 
     inner = pl.pallas_call(
-        middle_kernel,
+        inner_kernel,
         out_shape=jax.ShapeDtypeStruct((8 * ROWS, 512), jnp.float32),
-        in_specs=[in_vmem()] * 4,
+        in_specs=[in_vmem()] * 3,
         out_specs=in_vmem(),
         scratch_shapes=[
             pltpu.VMEM((5, 256, 128), jnp.float32),
@@ -452,9 +447,11 @@
         compiler_params=LIMIT,
         cost_estimate=pl.CostEstimate(flops=20_000_000, bytes_accessed=1_400_000, transcendentals=65536),
         name="inner",
-    )(far, state, troubled, blend_level)
-
-    halo = lax.all_gather(jnp.stack([ahead[1] + after[1], ahead[0] + after[0]]), "gz", axis_index_groups=pairs(sizes[2], 0))
+    )(state, troubled, blend_level)
+
+    gathered = jnp.stack([ahead[1] + after[1], ahead[0] + after[0]])
+    gathered, far = lax.optimization_barrier((gathered, far))
+    halo = lax.all_gather(gathered, "gz", axis_index_groups=pairs(sizes[2], 0))
     place = jnp.stack([core, odd_x, odd_y]).astype(jnp.int32)
     full = pl.pallas_call(
         outer_kernel,

time: 37.1 us -> 36 us (0.970)
  waiting for transfers between devices: 1.15 us -> 0.01 us
    ppermute x1, waiting for transfers between devices: 1.14 us -> 0.01 us  [on_device(): lax.ppermute(z_faces, 'gz', [(a, b) for a, b in swap] + [(b, a) for a, b...]
  transfers between devices with their start and end apart: 5 -> 5, of which waited for: 1 -> 0; matrix products, arithmetic and copies ran while one was open for 0% -> 0% of each run, Pallas kernels for 7% -> 8%
where the time goes in v9:
time: 36 us; the launch traced here: 35.7 us
  blocking collectives  17.8 us (49%)
  starting transfers between devices  11.7 us (32%)
  Pallas kernels  5.81 us (16%)
    all_gather x1, blocking collectives, on_device(): both = lax.all_gather(own, 'gz', axis_index_groups=pairs(sizes[2], 0))  15.8 us
    ppermute x1, starting transfers between devices, on_device(): lax.ppermute(z_faces, 'gz', [(a, b) for a, b in swap] + [(b, a) for a, b...  6.41 us
    ppermute x2, starting transfers between devices, on_device(): lax.ppermute(v, AXES, crossed(sizes, n, 0, half))  3.97 us
    pallas_call x1, Pallas kernels, on_device(): pl.pallas_call(inner_kernel, out_shape=jax.ShapeDtypeStruct((8 * ROWS, 51...  2.73 us
    all_gather x1, blocking collectives, on_device(): halo = lax.all_gather(gathered, 'gz', axis_index_groups=pairs(sizes[2], 0))  2.04 us
    pallas_call x1, Pallas kernels, on_device(): pl.pallas_call(outer_kernel, out_shape=jax.ShapeDtypeStruct((8 * ROWS, 51...  1.75 us
    ppermute x2, starting transfers between devices, on_device(): lax.ppermute(v, AXES, crossed(sizes, n, half, sizes[2]))  1.33 us
    pallas_call x1, Pallas kernels, on_device(): pl.pallas_call(faces_kernel, out_shape=jax.ShapeDtypeStruct((7 * ROWS, 12...  1.32 us
  transfers between devices with their start and end apart: 5, of which 0 were waited for; matrix products, arithmetic and copies ran while one was open for 0% of the time, Pallas kernels for 8%

profile of v9, /device:TPU:1, one launch (start us, length us, event | category | flops | bytes accessed | tf_op | source)
XLA Modules:
  0.0 35.7 jit_solution(5573134418995091030)
XLA Ops:
  0.0 1.3 %faces.1.own_ref = f32[280,128]{1,0:T(8,128)S(1)} custom-call(f32[320,512]{1,0:T(8,128)} %bitcast.28), custom_call_target="tpu_custom_call" | custom-call | tf_op jit(solution)/shard_map/faces/pallas_call | solution.py:400
  1.3 15.8 %all-gather = f32[560,128]{1,0:T(8,128)S(1)} all-gather(f32[280,128]{1,0:T(8,128)S(1)} %faces.1.own_ref), channel_id=2, replica_groups={{0,1},{2,3},{4,5},{6,7},{8,9},{10,11},{12,13},{14,15},{16,17},{18,19},{..., dimensions={0}, use_global_device_ids=true | all-gather | bytes 430080 | tf_op jit(solution)/shard_map/all_gather | solution.py:410
  17.1 0.0 copy-start
  17.2 2.1 %collective-permute-start = (f32[2,80,128]{2,1,0:T(8,128)S(1)}, f32[2,80,128]{2,1,0:T(8,128)S(1)}, u32[]{:S(2)}, u32[]{:S(2)}) collective-permute-start(f32[2,80,128]{2,1,0:T(8,128)S(1)} %get-tuple-element.10), channel_id=1, source_target_pairs={{0,960},{1,57},{2,962},{3,59},{8,968},{9,17},{10,970},{11,19},{16,... | collective-permute-start | bytes 245768 | tf_op jit(solution)/shard_map/ppermute | solution.py:419
  19.2 1.9 %collective-permute-start.2 = (f32[2,80,128]{2,1,0:T(8,128)S(1)}, f32[2,80,128]{2,1,0:T(8,128)S(1)}, u32[]{:S(2)}, u32[]{:S(2)}) collective-permute-start(f32[2,80,128]{2,1,0:T(8,128)S(1)} %get-tuple-element.11.ahead_ref), channel_id=1, source_target_pairs={{0,64},{1,9},{2,66},{3,11},{8,72},{9,1},{10,74},{11,3},{16,80},{17... | collective-permute-start | bytes 245768 | tf_op jit(solution)/shard_map/ppermute | solution.py:419
  21.2 0.0 copy-start.2
  21.2 0.0 copy-start.1
  21.2 6.4 %collective-permute-start.4 = (f32[40,128]{1,0:T(8,128)S(1)}, f32[40,128]{1,0:T(8,128)S(1)}, u32[]{:S(2)}, u32[]{:S(2)}) collective-permute-start(f32[40,128]{1,0:T(8,128)S(1)} %pick.1), channel_id=1, source_target_pairs={{1,2},{3,4},{5,6},{7,0},{2,1},{4,3},{6,5},{0,7},{9,10},{11,12},{13... | collective-permute-start | bytes 61448 | tf_op jit(solution)/shard_map/ppermute | solution.py:432
  27.6 0.7 %collective-permute-start.1 = (f32[2,80,128]{2,1,0:T(8,128)S(1)}, f32[2,80,128]{2,1,0:T(8,128)S(1)}, u32[]{:S(2)}, u32[]{:S(2)}) collective-permute-start(f32[2,80,128]{2,1,0:T(8,128)S(1)} %get-tuple-element.10), channel_id=1, source_target_pairs={{4,964},{5,61},{6,966},{7,63},{12,972},{13,21},{14,974},{15,23},{2... | collective-permute-start | bytes 245768 | tf_op jit(solution)/shard_map/ppermute | solution.py:433
  28.3 0.7 %collective-permute-start.3 = (f32[2,80,128]{2,1,0:T(8,128)S(1)}, f32[2,80,128]{2,1,0:T(8,128)S(1)}, u32[]{:S(2)}, u32[]{:S(2)}) collective-permute-start(f32[2,80,128]{2,1,0:T(8,128)S(1)} %get-tuple-element.11.ahead_ref), channel_id=1, source_target_pairs={{4,68},{5,13},{6,70},{7,15},{12,76},{13,5},{14,78},{15,7},{20,84},... | collective-permute-start | bytes 245768 | tf_op jit(solution)/shard_map/ppermute | solution.py:433
  29.0 0.0 copy-done
  29.0 0.0 copy-done.2
  29.0 0.0 copy-done.1
  29.0 2.7 %inner.1.pre_ref = f32[320,512]{1,0:T(8,128)S(1)} custom-call(f32[320,512]{1,0:T(8,128)S(1)} %bitcast.29, s32[2,4,8]{2,1,0:T(4,128)S(1)} %copy-done.1, s32[2,4,8]{2,1,0:T(4,128)S(1)} %copy-done.2), custom_call_target="tpu_custom_call" | custom-call | flops 20000000 | bytes 1400000 | tf_op jit(solution)/shard_map/inner/pallas_call | solution.py:435
  31.7 0.1 pad_add_fusion.place_ref
  31.8 0.0 collective-permute-done.1
  31.8 0.0 collective-permute-done
  31.9 0.0 collective-permute-done.3
  31.9 0.0 collective-permute-done.2
  31.9 0.0 collective-permute-done.4.far_ref
  31.9 2.0 %all-gather.1 = f32[4,2,80,128]{3,2,1,0:T(8,128)S(1)} all-gather(f32[2,2,80,128]{3,2,1,0:T(8,128)S(1)} %pad_maximum_fusion), channel_id=3, replica_groups={{0,1},{2,3},{4,5},{6,7},{8,9},{10,11},{12,13},{14,15},{16,17},{18,19},{..., dimensions={0}, use_global_device_ids=true | all-gather | bytes 491520 | tf_op jit(solution)/shard_map/all_gather | solution.py:454
  34.0 1.7 %outer.1 = f32[320,512]{1,0:T(8,128)} custom-call(s32[3]{0:T(128)S(1)} %pad_add_fusion.place_ref, f32[320,512]{1,0:T(8,128)S(1)} %inner.1.pre_ref, f32[280,128]{1,0:T(8,128)S(1)} %faces.1.own_ref, f32[2,2,2,80,128]{4,3,2,1,0:T(8,128)S(1)} %bitcast.30, f32[2,280,128]{2,1,0:T(8,128)S(1)} %bitcast.27, f32[40,128]{1,0:T(8,128)S(1)} %collective-permute-done.4.far_ref), custom_call_target="tpu_custom_call" | custom-call | tf_op jit(solution)/shard_map/outer/pallas_call | solution.py:456
  (6 shorter events, 0.1 us)
Async XLA Ops:
  17.1 11.8 %copy-start = (f32[2,4,8,5,512]{4,2,3,1,0:T(8,128)S(1)}, f32[2,4,8,5,512]{4,2,3,1,0:T(8,128)}, u32[]{:S(2)}) copy-start(f32[2,4,8,5,512]{4,2,3,1,0:T(8,128)} %param.3) | copy-start | bytes 1966084
  17.2 14.6 %collective-permute-start = (f32[2,80,128]{2,1,0:T(8,128)S(1)}, f32[2,80,128]{2,1,0:T(8,128)S(1)}, u32[]{:S(2)}, u32[]{:S(2)}) collective-permute-start(f32[2,80,128]{2,1,0:T(8,128)S(1)} %get-tuple-element.10), channel_id=1, source_target_pairs={{0,960},{1,57},{2,962},{3,59},{8,968},{9,17},{10,970},{11,19},{16,... | collective-permute-start | bytes 245768 | tf_op jit(solution)/shard_map/ppermute | solution.py:419
  19.2 12.6 %collective-permute-start.2 = (f32[2,80,128]{2,1,0:T(8,128)S(1)}, f32[2,80,128]{2,1,0:T(8,128)S(1)}, u32[]{:S(2)}, u32[]{:S(2)}) collective-permute-start(f32[2,80,128]{2,1,0:T(8,128)S(1)} %get-tuple-element.11.ahead_ref), channel_id=1, source_target_pairs={{0,64},{1,9},{2,66},{3,11},{8,72},{9,1},{10,74},{11,3},{16,80},{17... | collective-permute-start | bytes 245768 | tf_op jit(solution)/shard_map/ppermute | solution.py:419
  21.2 7.8 %copy-start.2 = (s32[2,4,8]{2,1,0:T(4,128)S(1)}, s32[2,4,8]{2,1,0:T(4,128)}, u32[]{:S(2)}) copy-start(s32[2,4,8]{2,1,0:T(4,128)} %level_ref.1) | copy-start | bytes 772
  21.2 7.8 %copy-start.1 = (s32[2,4,8]{2,1,0:T(4,128)S(1)}, s32[2,4,8]{2,1,0:T(4,128)}, u32[]{:S(2)}) copy-start(s32[2,4,8]{2,1,0:T(4,128)} %troubled_ref.1) | copy-start | bytes 772
  21.2 10.7 %collective-permute-start.4 = (f32[40,128]{1,0:T(8,128)S(1)}, f32[40,128]{1,0:T(8,128)S(1)}, u32[]{:S(2)}, u32[]{:S(2)}) collective-permute-start(f32[40,128]{1,0:T(8,128)S(1)} %pick.1), channel_id=1, source_target_pairs={{1,2},{3,4},{5,6},{7,0},{2,1},{4,3},{6,5},{0,7},{9,10},{11,12},{13... | collective-permute-start | bytes 61448 | tf_op jit(solution)/shard_map/ppermute | solution.py:432
  27.6 4.2 %collective-permute-start.1 = (f32[2,80,128]{2,1,0:T(8,128)S(1)}, f32[2,80,128]{2,1,0:T(8,128)S(1)}, u32[]{:S(2)}, u32[]{:S(2)}) collective-permute-start(f32[2,80,128]{2,1,0:T(8,128)S(1)} %get-tuple-element.10), channel_id=1, source_target_pairs={{4,964},{5,61},{6,966},{7,63},{12,972},{13,21},{14,974},{15,23},{2... | collective-permute-start | bytes 245768 | tf_op jit(solution)/shard_map/ppermute | solution.py:433
  28.3 3.6 %collective-permute-start.3 = (f32[2,80,128]{2,1,0:T(8,128)S(1)}, f32[2,80,128]{2,1,0:T(8,128)S(1)}, u32[]{:S(2)}, u32[]{:S(2)}) collective-permute-start(f32[2,80,128]{2,1,0:T(8,128)S(1)} %get-tuple-element.11.ahead_ref), channel_id=1, source_target_pairs={{4,68},{5,13},{6,70},{7,15},{12,76},{13,5},{14,78},{15,7},{20,84},... | collective-permute-start | bytes 245768 | tf_op jit(solution)/shard_map/ppermute | solution.py:433
